TPU v7x, 256 devices: a whole 4x4x8 slice. The times are simulated.
256 devices in a mesh: img: 64 (over y, z_lo, x), shell: 4 (over z_hi, core).
Axes of the slice: x: 4, y: 4, z: 8 (z_hi: 2, z_lo: 4; z = z_hi * 4 + z_lo), core: 2. Of those that a mesh axis runs over, the one named last changes fastest.
Arguments:
- images: float32 [1024, 40, 384], P('img', 'shell'), may hold values from -70 to 70
- references: bfloat16 [192, 40, 384], P('img', 'shell'), may hold values from -0.2 to 0.2
- class_offset: int32 [192], replicated, may hold values from 0 to 191
- ctf_group: int32 [1024], P('img'), may hold values from 0 to 15
- ctf: float32 [16, 40], P(None, 'shell'), may hold values from -1 to 1
- noise_power: float32 [40], P('shell'), may hold values from 0.3 to 3
- prior_precision: float32 [40], P('shell'), may hold values from 1 to 10
Outputs:
- new_references: bfloat16 [192, 40, 384], P('img', 'shell')
- log_evidence: float32 [1024], P('img')
All inputs are finite; a program needn't handle non-finite values.
Results may differ from a plain program's by a relative error of at most 0.011.
Values may be sent and summed in bfloat16 or wider, within the bound.
No kernel may reach another device: no remote copies, remote signals or barrier semaphores. Data moves between devices by JAX's collectives and lax.ppermute only.
A program may use at most 128 MiB of HBM per device.

v0:
```python
import jax
import jax.numpy as jnp
from jax import lax
from jax.sharding import PartitionSpec as P

ROT = 48


def align_rows(polar, starts):
    angle_count = polar.shape[2]
    doubled = jnp.concatenate((polar, polar), axis=2)

    def one_row(row, start):
        return lax.dynamic_slice_in_dim(row, start, angle_count, 1)

    return jax.vmap(one_row)(doubled, starts)


def turned_images(doubled_images, first_rotation, group_size, angle_step, angle_count):
    views = []
    for inner in range(group_size):
        start = (angle_step * (first_rotation + inner) % angle_count).astype(jnp.int32)
        views.append(lax.dynamic_slice_in_dim(doubled_images, start, angle_count, 2))
    image_count = doubled_images.shape[0]
    return jnp.stack(views, axis=0).reshape(group_size * image_count, -1)


def local(images, references, class_offset, ctf_group, ctf, noise_power, prior_precision):
    image_count, cycles_dev, row_width = images.shape
    angle_count = row_width // 2
    rotations = ROT
    angle_step = angle_count // rotations
    coeff_count = cycles_dev * row_width
    group_count = ctf.shape[0]
    class_count = class_offset.shape[0]
    group_size = 4
    onehot = (ctf_group[:, None] == jnp.arange(group_count)[None, :]).astype(jnp.float32)
    weight = 1.0 / noise_power
    ctf_weighted = ctf * weight[None, :]
    ctf_squared = ctf * ctf * weight[None, :]
    image_filter = jnp.dot(onehot, ctf_weighted, precision=lax.Precision.HIGHEST)
    filtered = (
        (images * image_filter[:, :, None]).astype(jnp.bfloat16).reshape(image_count, coeff_count)
    )
    half_norm = 0.5 * ctf_squared
    polar_images = filtered.reshape(image_count, 2 * cycles_dev, angle_count)
    doubled_images = jnp.concatenate((polar_images, polar_images), axis=2)
    ref_block = lax.all_gather(references, "img", axis=0, tiled=True)
    count = ref_block.shape[0]
    polar = ref_block.reshape(count, 2 * cycles_dev, angle_count)
    aligned = align_rows(polar, (angle_count - class_offset) % angle_count).reshape(
        count, coeff_count
    )
    power = jnp.sum(ref_block.astype(jnp.float32) ** 2, axis=2)
    aligned_refs = aligned
    norm_group = jnp.dot(half_norm, power.T, precision=lax.Precision.HIGHEST)
    norm_image = jnp.dot(onehot, norm_group, precision=lax.Precision.HIGHEST)

    def add_scores(turn_index, running):
        first_rotation = turn_index * group_size
        rotated_images = turned_images(
            doubled_images, first_rotation, group_size, angle_step, angle_count
        )
        cross_terms = lax.dot_general(
            rotated_images,
            aligned_refs,
            (((1,), (1,)), ((), ())),
            preferred_element_type=jnp.float32,
        )
        block = jnp.transpose(cross_terms.reshape(group_size, image_count, class_count), (1, 2, 0))
        return lax.dynamic_update_slice_in_dim(running, block, first_rotation, 2)

    cross_all = lax.fori_loop(
        0,
        rotations // group_size,
        add_scores,
        jnp.zeros((image_count, class_count, rotations), jnp.float32),
    )
    partial_scores = (cross_all - norm_image[:, :, None]).reshape(
        image_count, class_count * rotations
    )
    scores = lax.psum(partial_scores, "shell")
    largest = jnp.max(scores, axis=1, keepdims=True)
    totals = jnp.sum(jnp.exp(scores - largest), axis=1)
    log_evidence = largest[:, 0] + jnp.log(totals)
    probs = jnp.exp(scores - log_evidence[:, None]).astype(jnp.bfloat16)
    prob_cube = probs.reshape(image_count, class_count, rotations)

    def add_rotations(turn_index, running):
        first_rotation = turn_index * group_size
        prob_block = lax.dynamic_slice_in_dim(prob_cube, first_rotation, group_size, 2)
        rotated_images = turned_images(
            doubled_images, first_rotation, group_size, angle_step, angle_count
        )
        weights_block = jnp.transpose(prob_block, (1, 2, 0)).reshape(
            class_count, group_size * image_count
        )
        return running + jnp.dot(weights_block, rotated_images, preferred_element_type=jnp.float32)

    numerators = lax.fori_loop(
        0,
        rotations // group_size,
        add_rotations,
        jnp.zeros((class_count, coeff_count), jnp.float32),
    )
    class_mass = jnp.sum(prob_cube.astype(jnp.float32), axis=2)
    image_squared = jnp.dot(onehot, ctf_squared, precision=lax.Precision.HIGHEST)
    denominators = lax.dot_general(
        class_mass, image_squared, (((0,), (0,)), ((), ())), precision=lax.Precision.HIGHEST
    )
    own_sums, own_weights = (
        lax.psum_scatter(numerators, "img", scatter_dimension=0, tiled=True),
        lax.psum_scatter(denominators, "img", scatter_dimension=0, tiled=True),
    )
    own_count = own_sums.shape[0]
    first_class = lax.axis_index("img") * own_count
    own_offsets = lax.dynamic_slice_in_dim(class_offset, first_class, own_count)
    aligned = align_rows(
        own_sums.reshape(own_count, 2 * cycles_dev, angle_count), own_offsets % angle_count
    )
    averaged = (
        aligned.reshape(own_count, cycles_dev, row_width)
        / (own_weights + prior_precision[None, :])[:, :, None]
    )
    return (averaged.astype(jnp.bfloat16), log_evidence)


def solution(mesh):
    placed = (
        P("img", "shell", None),
        P("img", "shell", None),
        P(),
        P("img"),
        P(None, "shell"),
        P("shell"),
        P("shell"),
    )
    return jax.shard_map(
        local,
        mesh=mesh,
        in_specs=placed,
        out_specs=(P("img", "shell", None), P("img")),
        check_vma=False,
    )
```

profile of v0, /device:TPU:4, one launch (start us, length us, event | category | flops | bytes accessed | tf_op | source)
XLA Modules:
  0.0 1374.4 jit_solution(4085440548430132747)
XLA Ops:
  12.4 350.0 %all-gather.2.cloned.1.call-done = bf16[192,10,384]{2,1,0:T(8,128)(2,1)} async-done(((bf16[3,10,384]{2,1,0:T(8,128)(2,1)}), bf16[192,10,384]{2,1,0:T(8,128)(2,1)}) %all-gather.2.cloned.1.call-update) | async-done | bytes 1474576 | tf_op jit(solution)/shard_map/all_gather | solution.py:48
  362.4 3.1 copy.57
  365.5 6.7 copy.58
  372.3 16.4 %pad_maximum_fusion.1 = bf16[192,20,384]{1,0,2:T(8,128)(2,1)} fusion(bf16[192,20,192]{1,0,2:T(8,128)(2,1)} %copy.58), kind=kLoop, calls=%fused_computation.25 | loop fusion | flops 1474560 | bytes 4423680 | tf_op jit(solution)/shard_map/concatenate | solution.py:11
  388.7 44.3 %gather_fusion = bf16[192,20,192]{1,0,2:T(8,128)(2,1)} fusion(bf16[192,20,384]{1,0,2:T(8,128)(2,1)} %pad_maximum_fusion.1, s32[192]{0:T(256)S(1)} %bitcast.53), kind=kCustom, calls=%fused_computation | custom fusion | bytes 2951424 | tf_op jit(solution)/shard_map/vmap()/gather | solution.py:14
  433.0 8.2 copy.60
  444.4 52.1 %while.31 = (s32[]{:T(128)}, f32[16,192,48]{1,0,2:T(8,128)}, bf16[16,20,384]{2,1,0:T(8,128)(2,1)S(1)}, bf16[192,3840]{1,0:T(8,128)(2,1)}, s32[]{:T(128)}, /*inde...) while((s32[]{:T(128)}, f32[16,192,48]{1,0,2:T(8,128)}, ...), condition=%wide.region_1.2_spmd, body=%wide.region_0.1_spmd.sunk | while | flops 95109168 | bytes 3998339 | solution.py:73
  446.1 2.7 fusion.51
  450.4 2.7 fusion.51
  454.8 2.7 fusion.51
  459.1 2.7 fusion.51
  463.4 2.7 fusion.51
  467.8 2.7 fusion.51
  472.1 2.7 fusion.51
  476.5 2.7 fusion.51
  480.8 2.7 fusion.51
  485.2 2.7 fusion.51
  489.5 2.7 fusion.51
  493.9 2.7 fusion.51
  500.3 57.7 %all-reduce.7.cloned.1.call-done = f32[16,9216]{1,0:T(8,128)} async-done(((f32[16,9216]{1,0:T(8,128)}), f32[16,9216]{1,0:T(8,128)}) %all-reduce.7.cloned.1.call-update) | async-done | bytes 589840 | tf_op jit(solution)/shard_map/psum | solution.py:82
  563.6 2.5 copy.65
  566.0 82.3 %while.32 = (s32[]{:T(128)}, f32[192,3840]{1,0:T(8,128)S(1)}, bf16[16,192,48]{1,0,2:T(8,128)(2,1)}, bf16[16,20,384]{2,1,0:T(8,128)(2,1)S(1)}, s32[]{:T(128)}, /*...) while((s32[]{:T(128)}, f32[192,3840]{1,0:T(8,128)S(1)}, ...), condition=%wide.region_7.8_spmd.clone, body=%wide.region_6.7_spmd.clone.sunk | while | flops 96583728 | bytes 9413261 | solution.py:100
  653.4 360.5 %all-reduce.3 = f32[192,10]{1,0:T(8,128)S(1)} all-reduce(f32[192,10]{1,0:T(8,128)S(1)} %fusion.37), channel_id=3, replica_groups=mesh['img'=64,'shell'=4] {'img'}, use_global_device_ids=true, to_apply=%region_10.11.clone | all-reduce | flops 1920 | bytes 15360
  1014.0 349.9 %all-reduce.9.cloned.1.call-done = f32[192,3840]{1,0:T(8,128)} async-done(((f32[192,3840]{1,0:T(8,128)}), f32[192,3840]{1,0:T(8,128)}) %all-reduce.9.cloned.1.call-update) | async-done | bytes 2949136
  (184 shorter events, 126.6 us)
Async XLA Ops:
  7.2 355.2 %all-gather.2.cloned.1.call-start = ((), (), s32[]{:S(2)}) async-start(), calls=%async_computation | async-start | bytes 2396160 | tf_op jit(solution)/shard_map/all_gather | solution.py:48
  8.6 549.4 %all-reduce.7.cloned.1.call-start = ((), (), s32[]{:S(2)}) async-start(), calls=%async_computation.1 | async-start | bytes 1179648 | tf_op jit(solution)/shard_map/psum | solution.py:82
  444.4 52.1 %copy-start.1 = (bf16[192,10,384]{2,1,0:T(8,128)(2,1)S(1)}, bf16[192,10,384]{2,1,0:T(8,128)(2,1)}, u32[]{:S(2)}) copy-start(bf16[192,10,384]{2,1,0:T(8,128)(2,1)} %all-gather.2.cloned.1.call-done) | copy-start | bytes 4423684
  444.4 52.6 %copy-start.3 = (f32[16,10]{1,0:T(8,128)S(1)}, f32[16,10]{1,0:T(8,128)}, u32[]{:S(2)}) copy-start(f32[16,10]{1,0:T(8,128)} %param.15) | copy-start | bytes 1924
  444.4 52.8 %copy-start.7 = (s32[16]{0:T(128)S(1)}, s32[16]{0:T(128)}, u32[]{:S(2)}) copy-start(s32[16]{0:T(128)} %param.14) | copy-start | bytes 196
  496.5 1.1 copy-start.2
  500.3 863.6 %all-reduce.9.cloned.1.call-start = ((), (), s32[]{:S(2)}) async-start(), calls=%async_computation.2 | async-start | bytes 5898240
  560.6 5.4 copy-start.5
  648.3 1.6 copy-start
  648.3 1.7 copy-start.9
  648.4 2.9 copy-start.4
  648.4 3.0 copy-start.8
  648.4 365.6 %copy-start.6 = (f32[10]{0:T(128)S(1)}, f32[10]{0:T(128)}, u32[]{:S(2)}) copy-start(f32[10]{0:T(128)} %param.17) | copy-start | bytes 124
Sparse Core Ops, SparseCore 0:
  9.8 352.5 all-gather.1
  500.4 57.5 all-reduce.6
  650.1 713.7 all-reduce.8
where the time goes:
time: 1380 us; the launch traced here: 1370 us
  waiting for transfers between devices  758 us (55%)
  blocking collectives  361 us (26%)
  local copies, waits for them, and re-layouts  142 us (10%)
  matrix products  59.3 us (4%)
  other arithmetic  38.1 us (3%)
  between operations  14.6 us (1%)
    unnamed x1, blocking collectives  361 us
    all_gather x1, waiting for transfers between devices, local(): ref_block = lax.all_gather(references, 'img', axis=0, tiled=True)  350 us
    unnamed x4, waiting for transfers between devices  350 us
    psum x1, waiting for transfers between devices, local(): scores = lax.psum(partial_scores, 'shell')  57.7 us
    gather x4, local copies, waits for them, and re-layouts, one_row(): return lax.dynamic_slice_in_dim(row, start, angle_count, 1)  54.2 us
    dot_general x12, matrix products, add_scores(): lax.dot_general(rotated_images, aligned_refs, (((1,), (1,)), ((), ())), p...  32.1 us
    reshape x12, local copies, waits for them, and re-layouts, turned_images(): return jnp.stack(views, axis=0).reshape(group_size * image_count, -1)  29.1 us
  transfers between devices with their start and end apart: 3, of which 3 were waited for; matrix products, arithmetic and copies ran while one was open for 0% of the time, Pallas kernels for 0%

commit v1 on v0

v1 whole, which is shorter than its diff:
```python
import functools

import jax
import jax.numpy as jnp
from jax import lax
from jax.experimental import pallas as pl
from jax.experimental.pallas import tpu as pltpu
from jax.sharding import PartitionSpec as P

ANG = 192
ROT = 48
STEP = ANG // ROT
CYC = 10
ROW = 2 * ANG
TURN = 32
TURNS = ANG // TURN
FINE = TURN // STEP
BLOCK = 2 * CYC * TURN
COEF = TURNS * BLOCK
WIDE = COEF + 128
OWN_IMAGES = 16
OWN_CLASSES = 3
IMG_PEERS = 4
CLS_PEERS = 16
CLS = OWN_CLASSES * CLS_PEERS
ROWS = TURNS * CLS
HALF = FINE * OWN_IMAGES * 2
F32 = jnp.float32
BF16 = jnp.bfloat16
VMEM_LIMIT = 48 * 1024 * 1024


def lanes_of(shape):
    return lax.broadcasted_iota(jnp.int32, shape, len(shape) - 1)


def three_parts(x):
    hi = x.astype(BF16).astype(F32)
    rest = x - hi
    mid = rest.astype(BF16).astype(F32)
    return hi, mid, rest - mid


def pick4(lane, parts):
    return jnp.where(
        lane < 64,
        jnp.where(lane < 32, parts[0], parts[1]),
        jnp.where(lane < 96, parts[2], parts[3]),
    )


def turned_tile(rows_of, w, j, lane):
    parts = []
    for t in range(4):
        p, q = 2 * j + t // 2, t % 2
        start = q * ANG + TURN * w
        vreg, off = start // 128, start % 128
        piece = rows_of[p][:, vreg * 128 : vreg * 128 + 128]
        shift = (32 * t - off) % 128
        parts.append(pltpu.roll(piece, shift, 1) if shift else piece)
    return pick4(lane, parts)


def doubled_roll(x, shift):
    lane = lanes_of(x.shape)
    other = pltpu.roll(x, ANG, 1)
    first = lane < ANG
    a0 = pltpu.roll(jnp.where(first, x, other), shift, 1)
    a1 = pltpu.roll(jnp.where(first, other, x), shift, 1)
    return jnp.where(first, a0, a1)


def prologue_kernel(
    first_ref, offset_ref, group_ref, images_ref, refs_ref, ctf_ref, noise_ref,
    image_msg, class_msg,
    table_f, table_s, filt, square, padded, aligned,
):
    weight = 1.0 / noise_ref[...]
    ctf = ctf_ref[...]
    table_f[...] = jnp.zeros_like(table_f)
    table_s[...] = jnp.zeros_like(table_s)
    table_f[:, :CYC] = ctf * weight
    table_s[:, :CYC] = ctf * ctf * weight
    for i in range(OWN_IMAGES):
        g = group_ref[i]
        filt[i : i + 1, :] = table_f[pl.ds(g, 1), :]
        square[i : i + 1, :] = table_s[pl.ds(g, 1), :]

    lane16 = lanes_of((OWN_IMAGES, 128))
    factors = filt[...]
    rows = []
    for p in range(CYC):
        x = images_ref[:, p, :] * factors[:, p : p + 1]
        rows.append(x.astype(BF16).astype(F32))
    for w in range(TURNS):
        for j in range(5):
            at = w * BLOCK + j * 128
            image_msg[:, at : at + 128] = turned_tile(rows, w, j, lane16).astype(BF16)
    hi, mid, lo = three_parts(square[...])
    extra = hi
    for k, part in enumerate((mid, hi, lo, mid, hi)):
        extra = extra + pltpu.roll(part, 10 * (k + 1), 1)
    image_msg[:, COEF:] = extra.astype(BF16)

    padded[...] = jnp.zeros_like(padded)
    aligned[...] = jnp.zeros_like(aligned)
    for c in range(OWN_CLASSES):
        padded[:CYC, :] = refs_ref[c].astype(F32)
        aligned[c] = doubled_roll(padded[...], offset_ref[first_ref[0] + c])
    lane8 = lanes_of((8, 128))
    rows = [aligned[:, p, :] for p in range(CYC)]
    power = jnp.zeros((8, 128), F32)
    for p in range(CYC):
        power = jnp.where(lane8 == p, jnp.sum(rows[p] * rows[p], axis=1, keepdims=True), power)
    row48 = lax.broadcasted_iota(jnp.int32, (CLS, 128), 0) % OWN_CLASSES

    def spread(tile):
        return jnp.where(
            row48 == 0, tile[0:1], jnp.where(row48 == 1, tile[1:2], tile[2:3])
        ).astype(BF16)

    for w in range(TURNS):
        for j in range(5):
            at = w * BLOCK + j * 128
            class_msg[:, at : at + 128] = spread(turned_tile(rows, w, j, lane8))
    hi, mid, lo = three_parts(-0.5 * power)
    extra = hi
    for k, part in enumerate((hi, mid, hi, mid, lo)):
        extra = extra + pltpu.roll(part, 10 * (k + 1), 1)
    class_msg[:, COEF:] = spread(extra)


def slot_base(place_ref, k):
    owner = place_ref[0] ^ k
    half = (owner >> 1) ^ place_ref[1]
    return half * HALF + (owner & 1) * OWN_IMAGES


def fill_block(image_refs, bases, w, fine_ref):
    lane = lanes_of((OWN_IMAGES, 128))
    inner = lane % TURN
    after = jnp.where(w == TURNS - 1, 0, w + 1)
    for j in range(5):
        here = pl.ds(pl.multiple_of(w * BLOCK + j * 128, 128), 128)
        there = pl.ds(pl.multiple_of(after * BLOCK + j * 128, 128), 128)
        for k in range(IMG_PEERS):
            cur = image_refs[k][:, here]
            fine_ref[pl.ds(pl.multiple_of(bases[k], 16), 16), j * 128 : j * 128 + 128] = cur
            cur = cur.astype(F32)
            nxt = image_refs[k][:, there].astype(F32)
            for rho in range(1, FINE):
                s = STEP * rho
                val = jnp.where(
                    inner < TURN - s, pltpu.roll(cur, 128 - s, 1), pltpu.roll(nxt, TURN - s, 1)
                )
                fine_ref[
                    pl.ds(pl.multiple_of(bases[k] + 32 * rho, 16), 16), j * 128 : j * 128 + 128
                ] = val.astype(BF16)


def fill_extra(image_refs, bases, fine_ref):
    for k in range(IMG_PEERS):
        extra = image_refs[k][:, COEF:]
        for rho in range(FINE):
            fine_ref[pl.ds(pl.multiple_of(bases[k] + 32 * rho, 16), 16), :128] = extra


NT = (((1,), (1,)), ((), ()))


def scores_kernel(place_ref, f0, f1, f2, f3, class_ref, keep_ref, send_ref, fine, stack, total):
    image_refs = (f0, f1, f2, f3)
    bases = [slot_base(place_ref, k) for k in range(IMG_PEERS)]
    fill_extra(image_refs, bases, fine)
    for g in range(TURNS):
        stack[g * CLS : (g + 1) * CLS, :128] = class_ref[:, COEF:]
    total[...] = lax.dot_general(
        stack[:, :128], fine[:, :128], NT, preferred_element_type=F32
    )

    def step(w, carry):
        fill_block(image_refs, bases, w, fine)
        for g in range(TURNS):
            back = jnp.where(w >= g, w - g, w - g + TURNS)
            stack[g * CLS : (g + 1) * CLS, :] = class_ref[
                :, pl.ds(pl.multiple_of(back * BLOCK, 128), BLOCK)
            ]
        total[...] += lax.dot_general(stack[...], fine[...], NT, preferred_element_type=F32)
        return carry

    lax.fori_loop(0, TURNS, step, 0)
    keep_ref[...] = total[:, :HALF]
    send_ref[...] = total[:, HALF:]


def over_rotations(op, x):
    for s in (32, 64, 128):
        x = op(x, pltpu.roll(x, s, 1))
    return x


def stats_kernel(mine_ref, other_ref, scores_ref, stats_ref):
    scores = mine_ref[...] + other_ref[...]
    scores_ref[...] = scores
    big = jnp.max(scores, axis=0, keepdims=True)
    big = over_rotations(jnp.maximum, jnp.broadcast_to(big, (8, HALF)))
    part = jnp.sum(jnp.exp(scores - big[:1]), axis=0, keepdims=True)
    part = over_rotations(jnp.add, jnp.broadcast_to(part, (8, HALF)))
    row = lax.broadcasted_iota(jnp.int32, (8, HALF), 0)
    stats_ref[...] = jnp.where(row < 4, big, part)


def probs_kernel(scores_ref, s0, s1, s2, s3, probs_ref, evidence_ref):
    stats = [s[...] for s in (s0, s1, s2, s3)]
    bigs = [s[0:1] for s in stats]
    parts = [s[4:5] for s in stats]
    largest = jnp.maximum(jnp.maximum(bigs[0], bigs[1]), jnp.maximum(bigs[2], bigs[3]))
    total = sum(p * jnp.exp(b - largest) for b, p in zip(bigs, parts))
    evidence = largest + jnp.log(total)
    probs_ref[...] = jnp.exp(scores_ref[...] - evidence).astype(BF16)
    evidence_ref[...] = jnp.broadcast_to(evidence, (8, HALF))


def sums_kernel(place_ref, f0, f1, f2, f3, keep_ref, other_ref, out_ref, fine, probs, sums):
    image_refs = (f0, f1, f2, f3)
    bases = [slot_base(place_ref, k) for k in range(IMG_PEERS)]
    probs[:, :HALF] = keep_ref[...]
    probs[:, HALF:] = other_ref[...]
    sums[...] = jnp.zeros_like(sums)
    fill_extra(image_refs, bases, fine)
    extra = jnp.dot(probs[...], fine[:, :128], preferred_element_type=F32)
    mass = extra[:CLS]
    for g in range(1, TURNS):
        mass = mass + extra[g * CLS : (g + 1) * CLS]
    mass = mass + pltpu.roll(mass, 118, 1) + pltpu.roll(mass, 98, 1)
    mass = jnp.where(lanes_of((CLS, 128)) < CYC, mass, 0.0)
    hi, mid, lo = three_parts(mass)
    out_ref[:, COEF:] = (hi + pltpu.roll(mid, 10, 1) + pltpu.roll(lo, 20, 1)).astype(BF16)

    def step(w, carry):
        fill_block(image_refs, bases, w, fine)
        turned = jnp.dot(probs[...], fine[...], preferred_element_type=F32)
        for g in range(TURNS):
            back = jnp.where(w >= g, w - g, w - g + TURNS)
            sums[:, pl.ds(pl.multiple_of(back * BLOCK, 128), BLOCK)] += turned[
                g * CLS : (g + 1) * CLS, :
            ]
        return carry

    lax.fori_loop(0, TURNS, step, 0)
    out_ref[:, :COEF] = sums[...].astype(BF16)


def final_kernel(first_ref, offset_ref, msg_ref, prior_ref, out_ref, aligned):
    r = lax.broadcasted_iota(jnp.int32, (16, CLS), 0)
    k = lax.broadcasted_iota(jnp.int32, (16, CLS), 1)
    chosen = jnp.where(k % OWN_CLASSES == r, 1.0, 0.0).astype(BF16)
    total = jnp.dot(chosen, msg_ref[...], preferred_element_type=F32)[:8]
    lane = lanes_of((8, 128))
    extra = total[:, COEF:]
    den = extra + pltpu.roll(extra, 118, 1) + pltpu.roll(extra, 108, 1)
    tiles = {}
    for j in range(5):
        below = []
        for p in (2 * j, 2 * j + 1):
            below.append(den[:, p : p + 1] + prior_ref[0:1, p : p + 1])
        below = jnp.where(lane < 64, below[0], below[1])
        for w in range(TURNS):
            at = w * BLOCK + j * 128
            tiles[w, j] = total[:, at : at + 128] / below
    for p in range(CYC):
        for v in range(3):
            parts = []
            for u in range(4):
                start = 128 * v + 32 * u
                q, w = start // ANG, (start % ANG) // TURN
                t = 2 * (p % 2) + q
                shift = (32 * u - 32 * t) % 128
                piece = tiles[w, p // 2]
                parts.append(pltpu.roll(piece, shift, 1) if shift else piece)
            aligned[:, p, v * 128 : v * 128 + 128] = pick4(lane, parts)
    for c in range(OWN_CLASSES):
        off = offset_ref[first_ref[0] + c]
        back = jnp.where(off == 0, 0, ROW - off)
        out_ref[c] = doubled_roll(aligned[c], back)[:CYC].astype(BF16)


def call(kernel, outs, scratch, specs):
    return pl.pallas_call(
        kernel,
        out_shape=outs,
        in_specs=[pl.BlockSpec(memory_space=s) for s in specs],
        out_specs=jax.tree.map(lambda _: pl.BlockSpec(memory_space=pltpu.VMEM), outs),
        scratch_shapes=scratch,
        compiler_params=pltpu.CompilerParams(vmem_limit_bytes=VMEM_LIMIT),
    )


S, V = pltpu.SMEM, pltpu.VMEM


def shaped(shape, dtype):
    return jax.ShapeDtypeStruct(shape, dtype)


def local(images, references, class_offset, ctf_group, ctf, noise_power, prior_precision):
    img = lax.axis_index("img")
    core = lax.axis_index("shell") % 2
    level = (img // 4) % 4
    first = (img * OWN_CLASSES).astype(jnp.int32).reshape(1)
    place = jnp.stack([level, core]).astype(jnp.int32)

    def along_z(x, k):
        return lax.ppermute(x, "img", [(i, i ^ (4 * k)) for i in range(64)])

    def along_shell(x, k):
        return lax.ppermute(x, "shell", [(i, i ^ k) for i in range(4)])

    groups = [[16 * y + 4 * z + x for y in range(4) for x in range(4)] for z in range(4)]

    def over_classes(x):
        return lax.all_to_all(x, "img", 0, 0, axis_index_groups=groups, tiled=True)

    image_msg, class_msg = call(
        prologue_kernel,
        [shaped((OWN_IMAGES, WIDE), BF16), shaped((CLS, WIDE), BF16)],
        [
            V((16, 128), F32), V((16, 128), F32), V((16, 128), F32), V((16, 128), F32),
            V((16, ROW), F32), V((8, 16, ROW), F32),
        ],
        [S, S, S, V, V, V, V],
    )(first, class_offset, ctf_group, images, references, ctf, noise_power.reshape(1, CYC))
    held = [image_msg] + [along_z(image_msg, k) for k in (1, 2, 3)]
    class_all = over_classes(class_msg)

    keep, send = call(
        scores_kernel,
        [shaped((ROWS, HALF), F32)] * 2,
        [V((2 * HALF, BLOCK), BF16), V((ROWS, BLOCK), BF16), V((ROWS, 2 * HALF), F32)],
        [S, V, V, V, V, V],
    )(place, *held, class_all)
    pair = keep + along_shell(send, 1)
    other = along_shell(pair, 2)
    scores, stats = call(
        stats_kernel, [shaped((ROWS, HALF), F32), shaped((8, HALF), F32)], [], [V, V]
    )(pair, other)
    all_stats = [stats] + [along_z(stats, k) for k in (1, 2, 3)]
    probs, evidence = call(
        probs_kernel, [shaped((ROWS, HALF), BF16), shaped((8, HALF), F32)], [], [V] * 5
    )(scores, *all_stats)
    probs_other = along_shell(probs, 1)
    evidence_other = along_shell(evidence, 1)
    sums = call(
        sums_kernel,
        shaped((CLS, WIDE), BF16),
        [V((2 * HALF, BLOCK), BF16), V((ROWS, 2 * HALF), BF16), V((CLS, COEF), F32)],
        [S] + [V] * 6,
    )(place, *held, probs, probs_other)
    own = over_classes(sums)
    new_references = call(
        final_kernel,
        shaped((OWN_CLASSES, CYC, ROW), BF16),
        [V((8, 16, ROW), F32)],
        [S, S, V, V],
    )(first, class_offset, own, prior_precision.reshape(1, CYC))
    mine = jnp.where(core == level // 2, evidence[0], evidence_other[0])
    log_evidence = lax.dynamic_slice_in_dim(mine, (level % 2) * OWN_IMAGES, OWN_IMAGES)
    return new_references, log_evidence


def solution(mesh):
    placed = (
        P("img", "shell", None),
        P("img", "shell", None),
        P(),
        P("img"),
        P(None, "shell"),
        P("shell"),
        P("shell"),
    )
    return jax.shard_map(
        local,
        mesh=mesh,
        in_specs=placed,
        out_specs=(P("img", "shell", None), P("img")),
        check_vma=False,
    )
```

time: 1380 us -> 90.9 us (0.07)
  the two profiles are of different devices: /device:TPU:4 before, /device:TPU:1 now
where the time goes in v1:
time: 90.9 us; the launch traced here: 90.5 us
  waiting for transfers between devices  34.7 us (38%)
  starting transfers between devices  33.8 us (37%)
  Pallas kernels  14.2 us (16%)
  local copies, waits for them, and re-layouts  6.32 us (7%)
    ppermute x4, waiting for transfers between devices, along_shell(): return lax.ppermute(x, 'shell', [(i, i ^ k) for i in range(4)])  15.9 us
    all_to_all x2, starting transfers between devices, over_classes(): return lax.all_to_all(x, 'img', 0, 0, axis_index_groups=groups, tiled=True)  14.2 us
    all_to_all x2, waiting for transfers between devices, over_classes(): return lax.all_to_all(x, 'img', 0, 0, axis_index_groups=groups, tiled=True)  14 us
    ppermute x4, starting transfers between devices, along_shell(): return lax.ppermute(x, 'shell', [(i, i ^ k) for i in range(4)])  11.2 us
    ppermute x6, starting transfers between devices, along_z(): return lax.ppermute(x, 'img', [(i, i ^ 4 * k) for i in range(64)])  8.38 us
    pallas_call x1, Pallas kernels, local(): call(scores_kernel, [shaped((ROWS, HALF), F32)] * 2, [V((2 * HALF, BLOCK)...  5.76 us
    pallas_call x1, Pallas kernels, local(): call(sums_kernel, shaped((CLS, WIDE), BF16), [V((2 * HALF, BLOCK), BF16),...  5.67 us
    ppermute x6, waiting for transfers between devices, along_z(): return lax.ppermute(x, 'img', [(i, i ^ 4 * k) for i in range(64)])  4.78 us
  transfers between devices with their start and end apart: 12, of which 9 were waited for; matrix products, arithmetic and copies ran while one was open for 1% of the time, Pallas kernels for 0%

profile of v1, /device:TPU:1, one launch (start us, length us, event | category | flops | bytes accessed | tf_op | source)
XLA Modules:
  0.0 90.5 jit_solution(5765347929342623947)
XLA Ops:
  0.6 0.8 copy.13.refs_ref
  1.4 1.1 %copy.12.images_ref = f32[16,10,384]{2,1,0:T(8,128)S(1)} copy(f32[16,10,384]{2,0,1:T(8,128)} %param.7) | data formatting | bytes 491520 | tf_op args[0]
  3.1 1.1 %shard_map.86 = (bf16[16,3968]{1,0:T(8,128)(2,1)S(1)}, bf16[48,3968]{1,0:T(8,128)(2,1)S(1)}) custom-call(s32[1]{0:T(128)} %bitcast.first_ref, s32[192]{0:T(256)S(1)} %copy-done.1, s32[16]{0:T(128)S(1)} %copy-done.3, f32[16,10,384]{2,1,0:T(8,128)S(1)} %copy.12.images_ref, bf16[3,10,384]{2,1,0:T(8,128)(2,1)S(1)} %copy.13.refs_ref, f32[16,10]{1,0:T(8,128)S(1)} %copy-done, ...), custom_call_target="tpu_custom_call" | custom-call | tf_op jit(solution)/shard_map/pallas_call | solution.py:324
  4.3 1.0 %all_to_all.14 = bf16[16,3,3968]{2,1,0:T(4,128)(2,1)} reshape(bf16[48,3968]{1,0:T(8,128)(2,1)S(1)} %get-tuple-element.11) | data formatting | bytes 761856 | tf_op jit(solution)/shard_map/all_to_all | solution.py:322
  5.3 7.6 %all-to-all-start = ((bf16[16,3,3968]{2,1,0:T(4,128)(2,1)}), bf16[16,3,3968]{2,1,0:T(4,128)(2,1)S(1)}, u32[]{:S(2)}, u32[]{:S(2)}) async-start(bf16[16,3,3968]{2,1,0:T(4,128)(2,1)} %all_to_all.14), calls=%async_computation | async-start | bytes 1015808 | tf_op jit(solution)/shard_map/all_to_all | solution.py:322
  12.9 4.4 %collective-permute-start.2 = (bf16[16,3968]{1,0:T(8,128)(2,1)S(1)}, bf16[16,3968]{1,0:T(8,128)(2,1)S(1)}, u32[]{:S(2)}, u32[]{:S(2)}) collective-permute-start(bf16[16,3968]{1,0:T(8,128)(2,1)S(1)} %get-tuple-element.10.f0), channel_id=1, source_target_pairs={{0,48},{4,52},{8,56},{12,60},{16,32},{20,36},{24,40},{28,44},{32,1... | collective-permute-start | bytes 380936 | tf_op jit(solution)/shard_map/ppermute | solution.py:314
  17.7 5.6 %all-to-all-done = bf16[16,3,3968]{2,1,0:T(4,128)(2,1)S(1)} async-done(((bf16[16,3,3968]{2,1,0:T(4,128)(2,1)}), bf16[16,3,3968]{2,1,0:T(4,128)(2,1)S(1)}, u32[]{:S(2)}, u32[]{:S(2)}) %all-to-all-start) | async-done | bytes 380960 | tf_op jit(solution)/shard_map/all_to_all | solution.py:322
  23.6 3.1 %collective-permute-done.1.f2 = bf16[16,3968]{1,0:T(8,128)(2,1)S(1)} collective-permute-done((bf16[16,3968]{1,0:T(8,128)(2,1)S(1)}, bf16[16,3968]{1,0:T(8,128)(2,1)S(1)}, u32[]{:S(2)}, u32[]{:S(2)}) %collective-permute-start.1) | collective-permute-done | bytes 127008 | tf_op jit(solution)/shard_map/ppermute | solution.py:314
  26.8 5.8 %shard_map.87 = (f32[288,256]{1,0:T(8,128)S(1)}, f32[288,256]{1,0:T(8,128)S(1)}) custom-call(s32[2]{0:T(128)S(1)} %pad_add_fusion.place_ref, bf16[16,3968]{1,0:T(8,128)(2,1)S(1)} %get-tuple-element.10.f0, bf16[16,3968]{1,0:T(8,128)(2,1)S(1)} %collective-permute-done.f1, bf16[16,3968]{1,0:T(8,128)(2,1)S(1)} %collective-permute-done.1.f2, ...), custom_call_target="tpu_custom_call" | custom-call | tf_op jit(solution)/shard_map/pallas_call | solution.py:336
  32.6 1.8 %collective-permute-start.3 = (f32[288,256]{1,0:T(8,128)S(1)}, f32[288,256]{1,0:T(8,128)S(1)}, u32[]{:S(2)}, u32[]{:S(2)}) collective-permute-start(f32[288,256]{1,0:T(8,128)S(1)} %get-tuple-element.13), channel_id=1, source_target_pairs={{0,1},{1,0},{2,3},{3,2},{4,5},{5,4},{6,7},{7,6},{8,9},{9,8},{10,11... | collective-permute-start | bytes 884744 | tf_op jit(solution)/shard_map/ppermute | solution.py:317
  34.3 1.2 %collective-permute-done.3 = f32[288,256]{1,0:T(8,128)S(1)} collective-permute-done((f32[288,256]{1,0:T(8,128)S(1)}, f32[288,256]{1,0:T(8,128)S(1)}, u32[]{:S(2)}, u32[]{:S(2)}) %collective-permute-start.3) | collective-permute-done | bytes 294944 | tf_op jit(solution)/shard_map/ppermute | solution.py:317
  35.6 5.9 %collective-permute-start.4 = (f32[288,256]{1,0:T(8,128)S(1)}, f32[288,256]{1,0:T(8,128)S(1)}, u32[]{:S(2)}, u32[]{:S(2)}) collective-permute-start(f32[288,256]{1,0:T(8,128)S(1)} %add.20.mine_ref), channel_id=1, source_target_pairs={{0,2},{1,3},{2,0},{3,1},{4,6},{5,7},{6,4},{7,5},{8,10},{9,11},{10,... | collective-permute-start | bytes 884744 | tf_op jit(solution)/shard_map/ppermute | solution.py:317
  41.5 12.9 %collective-permute-done.4.other_ref = f32[288,256]{1,0:T(8,128)S(1)} collective-permute-done((f32[288,256]{1,0:T(8,128)S(1)}, f32[288,256]{1,0:T(8,128)S(1)}, u32[]{:S(2)}, u32[]{:S(2)}) %collective-permute-start.4) | collective-permute-done | bytes 294944 | tf_op jit(solution)/shard_map/ppermute | solution.py:317
  54.8 1.8 %collective-permute-start.7 = (f32[8,256]{1,0:T(8,128)S(1)}, f32[8,256]{1,0:T(8,128)S(1)}, u32[]{:S(2)}, u32[]{:S(2)}) collective-permute-start(f32[8,256]{1,0:T(8,128)S(1)} %get-tuple-element.15.s0), channel_id=1, source_target_pairs={{0,48},{4,52},{8,56},{12,60},{16,32},{20,36},{24,40},{28,44},{32,1... | collective-permute-start | bytes 24584 | tf_op jit(solution)/shard_map/ppermute | solution.py:314
  56.6 1.8 %collective-permute-start.5 = (f32[8,256]{1,0:T(8,128)S(1)}, f32[8,256]{1,0:T(8,128)S(1)}, u32[]{:S(2)}, u32[]{:S(2)}) collective-permute-start(f32[8,256]{1,0:T(8,128)S(1)} %get-tuple-element.15.s0), channel_id=1, source_target_pairs={{0,16},{4,20},{8,24},{12,28},{16,0},{20,4},{24,8},{28,12},{32,48},... | collective-permute-start | bytes 24584 | tf_op jit(solution)/shard_map/ppermute | solution.py:314
  59.1 0.9 collective-permute-done.6.s2
  60.1 2.8 %collective-permute-start.8 = (bf16[288,256]{1,0:T(8,128)(2,1)S(1)}, bf16[288,256]{1,0:T(8,128)(2,1)S(1)}, u32[]{:S(2)}, u32[]{:S(2)}) collective-permute-start(bf16[288,256]{1,0:T(8,128)(2,1)S(1)} %get-tuple-element.16.keep_ref), channel_id=1, source_target_pairs={{0,1},{1,0},{2,3},{3,2},{4,5},{5,4},{6,7},{7,6},{8,9},{9,8},{10,11... | collective-permute-start | bytes 442376 | tf_op jit(solution)/shard_map/ppermute | solution.py:317
  62.8 1.0 %collective-permute-done.8.other_ref = bf16[288,256]{1,0:T(8,128)(2,1)S(1)} collective-permute-done((bf16[288,256]{1,0:T(8,128)(2,1)S(1)}, bf16[288,256]{1,0:T(8,128)(2,1)S(1)}, u32[]{:S(2)}, u32[]{:S(2)}) %collective-permute-start.8) | collective-permute-done | bytes 147488 | tf_op jit(solution)/shard_map/ppermute | solution.py:317
  63.8 5.7 %shard_map.90 = bf16[48,3968]{1,0:T(8,128)(2,1)S(1)} custom-call(s32[2]{0:T(128)S(1)} %pad_add_fusion.place_ref, bf16[16,3968]{1,0:T(8,128)(2,1)S(1)} %get-tuple-element.10.f0, bf16[16,3968]{1,0:T(8,128)(2,1)S(1)} %collective-permute-done.f1, bf16[16,3968]{1,0:T(8,128)(2,1)S(1)} %collective-permute-done.1.f2, ...), custom_call_target="tpu_custom_call" | custom-call | tf_op jit(solution)/shard_map/pallas_call | solution.py:353
  69.5 1.0 %all_to_all.17 = bf16[16,3,3968]{2,1,0:T(4,128)(2,1)} reshape(bf16[48,3968]{1,0:T(8,128)(2,1)S(1)} %shard_map.90) | data formatting | bytes 761856 | tf_op jit(solution)/shard_map/all_to_all | solution.py:322
  70.5 6.7 %all-to-all-start.1 = ((bf16[16,3,3968]{2,1,0:T(4,128)(2,1)}), bf16[16,3,3968]{2,1,0:T(4,128)(2,1)S(1)}, u32[]{:S(2)}, u32[]{:S(2)}) async-start(bf16[16,3,3968]{2,1,0:T(4,128)(2,1)} %all_to_all.17), calls=%async_computation.1 | async-start | bytes 1015808 | tf_op jit(solution)/shard_map/all_to_all | solution.py:322
  77.9 0.8 collective-permute-done.9
  79.3 8.4 %all-to-all-done.1 = bf16[16,3,3968]{2,1,0:T(4,128)(2,1)S(1)} async-done(((bf16[16,3,3968]{2,1,0:T(4,128)(2,1)}), bf16[16,3,3968]{2,1,0:T(4,128)(2,1)S(1)}, u32[]{:S(2)}, u32[]{:S(2)}) %all-to-all-start.1) | async-done | bytes 380960 | tf_op jit(solution)/shard_map/all_to_all | solution.py:322
  88.7 1.2 %shard_map.91 = bf16[3,10,384]{2,1,0:T(8,128)(2,1)S(1)} custom-call(s32[1]{0:T(128)} %bitcast.first_ref, s32[192]{0:T(256)S(1)} %copy-done.1, bf16[48,3968]{1,0:T(8,128)(2,1)S(1)} %all_to_all.19.msg_ref, f32[1,10]{1,0:T(1,128)S(1)} %bitcast.7), custom_call_target="tpu_custom_call" | custom-call | tf_op jit(solution)/shard_map/pallas_call | solution.py:360
  (28 shorter events, 5.6 us)
Async XLA Ops:
  1.4 1.1 %copy-start = (f32[16,10]{1,0:T(8,128)S(1)}, f32[16,10]{1,0:T(8,128)}, u32[]{:S(2)}) copy-start(f32[16,10]{1,0:T(8,128)} %ctf_ref.1) | copy-start | bytes 1924
  1.4 1.1 %copy-start.4 = (f32[10]{0:T(128)S(1)}, f32[10]{0:T(128)}, u32[]{:S(2)}) copy-start(f32[10]{0:T(128)} %param.12) | copy-start | bytes 124
  2.5 0.7 copy-start.1
  2.5 0.7 copy-start.3
  5.3 18.0 %all-to-all-start = ((bf16[16,3,3968]{2,1,0:T(4,128)(2,1)}), bf16[16,3,3968]{2,1,0:T(4,128)(2,1)S(1)}, u32[]{:S(2)}, u32[]{:S(2)}) async-start(bf16[16,3,3968]{2,1,0:T(4,128)(2,1)} %all_to_all.14), calls=%async_computation | async-start | bytes 1015808 | tf_op jit(solution)/shard_map/all_to_all | solution.py:322
  12.9 10.8 %collective-permute-start.2 = (bf16[16,3968]{1,0:T(8,128)(2,1)S(1)}, bf16[16,3968]{1,0:T(8,128)(2,1)S(1)}, u32[]{:S(2)}, u32[]{:S(2)}) collective-permute-start(bf16[16,3968]{1,0:T(8,128)(2,1)S(1)} %get-tuple-element.10.f0), channel_id=1, source_target_pairs={{0,48},{4,52},{8,56},{12,60},{16,32},{20,36},{24,40},{28,44},{32,1... | collective-permute-start | bytes 380936 | tf_op jit(solution)/shard_map/ppermute | solution.py:314
  17.3 9.5 %collective-permute-start.1 = (bf16[16,3968]{1,0:T(8,128)(2,1)S(1)}, bf16[16,3968]{1,0:T(8,128)(2,1)S(1)}, u32[]{:S(2)}, u32[]{:S(2)}) collective-permute-start(bf16[16,3968]{1,0:T(8,128)(2,1)S(1)} %get-tuple-element.10.f0), channel_id=1, source_target_pairs={{0,32},{4,36},{8,40},{12,44},{16,48},{20,52},{24,56},{28,60},{32,0... | collective-permute-start | bytes 380936 | tf_op jit(solution)/shard_map/ppermute | solution.py:314
  17.3 9.5 %collective-permute-start = (bf16[16,3968]{1,0:T(8,128)(2,1)S(1)}, bf16[16,3968]{1,0:T(8,128)(2,1)S(1)}, u32[]{:S(2)}, u32[]{:S(2)}) collective-permute-start(bf16[16,3968]{1,0:T(8,128)(2,1)S(1)} %get-tuple-element.10.f0), channel_id=1, source_target_pairs={{0,16},{4,20},{8,24},{12,28},{16,0},{20,4},{24,8},{28,12},{32,48},... | collective-permute-start | bytes 380936 | tf_op jit(solution)/shard_map/ppermute | solution.py:314
  32.6 3.0 %collective-permute-start.3 = (f32[288,256]{1,0:T(8,128)S(1)}, f32[288,256]{1,0:T(8,128)S(1)}, u32[]{:S(2)}, u32[]{:S(2)}) collective-permute-start(f32[288,256]{1,0:T(8,128)S(1)} %get-tuple-element.13), channel_id=1, source_target_pairs={{0,1},{1,0},{2,3},{3,2},{4,5},{5,4},{6,7},{7,6},{8,9},{9,8},{10,11... | collective-permute-start | bytes 884744 | tf_op jit(solution)/shard_map/ppermute | solution.py:317
  35.6 18.8 %collective-permute-start.4 = (f32[288,256]{1,0:T(8,128)S(1)}, f32[288,256]{1,0:T(8,128)S(1)}, u32[]{:S(2)}, u32[]{:S(2)}) collective-permute-start(f32[288,256]{1,0:T(8,128)S(1)} %add.20.mine_ref), channel_id=1, source_target_pairs={{0,2},{1,3},{2,0},{3,1},{4,6},{5,7},{6,4},{7,5},{8,10},{9,11},{10,... | collective-permute-start | bytes 884744 | tf_op jit(solution)/shard_map/ppermute | solution.py:317
  54.8 4.3 %collective-permute-start.7 = (f32[8,256]{1,0:T(8,128)S(1)}, f32[8,256]{1,0:T(8,128)S(1)}, u32[]{:S(2)}, u32[]{:S(2)}) collective-permute-start(f32[8,256]{1,0:T(8,128)S(1)} %get-tuple-element.15.s0), channel_id=1, source_target_pairs={{0,48},{4,52},{8,56},{12,60},{16,32},{20,36},{24,40},{28,44},{32,1... | collective-permute-start | bytes 24584 | tf_op jit(solution)/shard_map/ppermute | solution.py:314
  56.6 3.4 %collective-permute-start.6 = (f32[8,256]{1,0:T(8,128)S(1)}, f32[8,256]{1,0:T(8,128)S(1)}, u32[]{:S(2)}, u32[]{:S(2)}) collective-permute-start(f32[8,256]{1,0:T(8,128)S(1)} %get-tuple-element.15.s0), channel_id=1, source_target_pairs={{0,32},{4,36},{8,40},{12,44},{16,48},{20,52},{24,56},{28,60},{32,0... | collective-permute-start | bytes 24584 | tf_op jit(solution)/shard_map/ppermute | solution.py:314
  56.6 3.4 %collective-permute-start.5 = (f32[8,256]{1,0:T(8,128)S(1)}, f32[8,256]{1,0:T(8,128)S(1)}, u32[]{:S(2)}, u32[]{:S(2)}) collective-permute-start(f32[8,256]{1,0:T(8,128)S(1)} %get-tuple-element.15.s0), channel_id=1, source_target_pairs={{0,16},{4,20},{8,24},{12,28},{16,0},{20,4},{24,8},{28,12},{32,48},... | collective-permute-start | bytes 24584 | tf_op jit(solution)/shard_map/ppermute | solution.py:314
  60.1 3.8 %collective-permute-start.8 = (bf16[288,256]{1,0:T(8,128)(2,1)S(1)}, bf16[288,256]{1,0:T(8,128)(2,1)S(1)}, u32[]{:S(2)}, u32[]{:S(2)}) collective-permute-start(bf16[288,256]{1,0:T(8,128)(2,1)S(1)} %get-tuple-element.16.keep_ref), channel_id=1, source_target_pairs={{0,1},{1,0},{2,3},{3,2},{4,5},{5,4},{6,7},{7,6},{8,9},{9,8},{10,11... | collective-permute-start | bytes 442376 | tf_op jit(solution)/shard_map/ppermute | solution.py:317
  70.5 17.2 %all-to-all-start.1 = ((bf16[16,3,3968]{2,1,0:T(4,128)(2,1)}), bf16[16,3,3968]{2,1,0:T(4,128)(2,1)S(1)}, u32[]{:S(2)}, u32[]{:S(2)}) async-start(bf16[16,3,3968]{2,1,0:T(4,128)(2,1)} %all_to_all.17), calls=%async_computation.1 | async-start | bytes 1015808 | tf_op jit(solution)/shard_map/all_to_all | solution.py:322
  77.1 1.6 %collective-permute-start.9 = (f32[8,256]{1,0:T(8,128)S(1)}, f32[8,256]{1,0:T(8,128)S(1)}, u32[]{:S(2)}, u32[]{:S(2)}) collective-permute-start(f32[8,256]{1,0:T(8,128)S(1)} %get-tuple-element.17), channel_id=1, source_target_pairs={{0,1},{1,0},{2,3},{3,2},{4,5},{5,4},{6,7},{7,6},{8,9},{9,8},{10,11... | collective-permute-start | bytes 24584 | tf_op jit(solution)/shard_map/ppermute | solution.py:317
  88.0 0.7 copy-start.2

commit v2 on v1

v2 whole, which is shorter than its diff:
```python
import functools

import jax
import jax.numpy as jnp
from jax import lax
from jax.experimental import pallas as pl
from jax.experimental.pallas import tpu as pltpu
from jax.sharding import PartitionSpec as P

ANG = 192
ROT = 48
STEP = ANG // ROT
CYC = 10
ROW = 2 * ANG
TURN = 32
TURNS = ANG // TURN
FINE = TURN // STEP
BLOCK = 2 * CYC * TURN
COEF = TURNS * BLOCK
WIDE = COEF + 128
OWN_IMAGES = 16
OWN_CLASSES = 3
IMG_PEERS = 4
CLS_PEERS = 16
CLS = OWN_CLASSES * CLS_PEERS
ROWS = TURNS * CLS
HALF = FINE * OWN_IMAGES * 2
F32 = jnp.float32
BF16 = jnp.bfloat16
VMEM_LIMIT = 24 * 1024 * 1024
VMEM_MOST = 60 * 1024 * 1024


def lanes_of(shape):
    return lax.broadcasted_iota(jnp.int32, shape, len(shape) - 1)


def three_parts(x):
    hi = x.astype(BF16).astype(F32)
    rest = x - hi
    mid = rest.astype(BF16).astype(F32)
    return hi, mid, rest - mid


def pick4(lane, parts):
    return jnp.where(
        lane < 64,
        jnp.where(lane < 32, parts[0], parts[1]),
        jnp.where(lane < 96, parts[2], parts[3]),
    )


def turned_tile(rows_of, w, j, lane):
    parts = []
    for t in range(4):
        p, q = 2 * j + t // 2, t % 2
        start = q * ANG + TURN * w
        vreg, off = start // 128, start % 128
        piece = rows_of[p][:, vreg * 128 : vreg * 128 + 128]
        shift = (32 * t - off) % 128
        parts.append(pltpu.roll(piece, shift, 1) if shift else piece)
    return pick4(lane, parts)


def interleaving(back=False):
    a = lax.broadcasted_iota(jnp.int32, (128, 128), 0)
    b = lax.broadcasted_iota(jnp.int32, (128, 128), 1)
    if back:
        a, b = b, a
    return jnp.where(b == (a % TURN) * 4 + a // TURN, 1.0, 0.0).astype(BF16)


def doubled_roll(x, shift):
    lane = lanes_of(x.shape)
    other = pltpu.roll(x, ANG, 1)
    first = lane < ANG
    a0 = pltpu.roll(jnp.where(first, x, other), shift, 1)
    a1 = pltpu.roll(jnp.where(first, other, x), shift, 1)
    return jnp.where(first, a0, a1)


def turn_classes(stacked, shifts):
    row = lax.broadcasted_iota(jnp.int32, stacked.shape, 0) % 8
    turned = doubled_roll(stacked, shifts[0])
    for c in range(1, OWN_CLASSES):
        turned = jnp.where(row == c, doubled_roll(stacked, shifts[c]), turned)
    return turned


def prologue_kernel(
    first_ref, offset_ref, group_ref, images_ref, refs_ref, ctf_ref, noise_ref,
    image_msg, class_msg,
    table_f, table_s, filt, square, stacked, own,
):
    stacked[...] = jnp.zeros_like(stacked)
    for p in range(CYC):
        stacked[p * 8 : p * 8 + OWN_CLASSES, :] = refs_ref[p].astype(F32)
    turned = turn_classes(
        stacked[...], [offset_ref[first_ref[0] + c] for c in range(OWN_CLASSES)]
    )
    rows = [turned[p * 8 : p * 8 + 8] for p in range(CYC)]
    lane8 = lanes_of((8, 128))
    power = jnp.zeros((8, 128), F32)
    for p in range(CYC):
        power = jnp.where(lane8 == p, jnp.sum(rows[p] * rows[p], axis=1, keepdims=True), power)
    mixing = interleaving()
    for w in range(TURNS):
        tiles = [turned_tile(rows, w, j, lane8) for j in range(5)]
        tiles = jnp.concatenate(tiles, axis=0).astype(BF16)
        tiles = jnp.dot(tiles, mixing, preferred_element_type=F32)
        for j in range(5):
            at = w * BLOCK + j * 128
            own[:, at : at + 128] = tiles[j * 8 : j * 8 + 8]
    hi, mid, lo = three_parts(-0.5 * power)
    extra = hi
    for k, part in enumerate((hi, mid, hi, mid, lo)):
        extra = extra + pltpu.roll(part, 10 * (k + 1), 1)
    own[:, COEF:] = extra
    held = own[:OWN_CLASSES, :].astype(BF16)
    for d in range(CLS_PEERS):
        class_msg[d] = held

    weight = 1.0 / noise_ref[...]
    ctf = ctf_ref[...]
    table_f[...] = jnp.zeros_like(table_f)
    table_s[...] = jnp.zeros_like(table_s)
    table_f[:, :CYC] = ctf * weight
    table_s[:, :CYC] = ctf * ctf * weight
    for i in range(OWN_IMAGES):
        g = group_ref[i]
        filt[i : i + 1, :] = table_f[pl.ds(g, 1), :]
        square[i : i + 1, :] = table_s[pl.ds(g, 1), :]
    lane16 = lanes_of((OWN_IMAGES, 128))
    factors = filt[...]
    rows = []
    for p in range(CYC):
        x = images_ref[p] * factors[:, p : p + 1]
        rows.append(x.astype(BF16).astype(F32))
    for w in range(TURNS):
        tiles = [turned_tile(rows, w, j, lane16) for j in range(5)]
        tiles = jnp.concatenate(tiles, axis=0).astype(BF16)
        tiles = jnp.dot(tiles, mixing, preferred_element_type=F32).astype(BF16)
        for j in range(5):
            at = w * BLOCK + j * 128
            image_msg[:, at : at + 128] = tiles[j * 16 : j * 16 + 16]
    hi, mid, lo = three_parts(square[...])
    extra = hi
    for k, part in enumerate((mid, hi, lo, mid, hi)):
        extra = extra + pltpu.roll(part, 10 * (k + 1), 1)
    image_msg[:, COEF:] = extra.astype(BF16)


QUARTER = HALF // 2


def turned_on(cur, nxt, steps):
    s = 4 * STEP * steps
    lane = lanes_of(cur.shape)
    return pltpu.roll(jnp.where(lane >= s, cur, nxt), 128 - s, 1)


def early_kernel(place_ref, f0, f1, f2, f3, early_ref):
    image_refs = (f0, f1, f2, f3)
    bases = []
    for k in range(IMG_PEERS):
        owner = place_ref[0] ^ k
        half = (owner >> 1) ^ place_ref[1]
        bases.append(half * QUARTER + (owner & 1) * OWN_IMAGES)
    for k in range(IMG_PEERS):
        extra = image_refs[k][:, COEF:]
        for rho in range(FINE // 2):
            early_ref[pl.ds(pl.multiple_of(bases[k] + 32 * rho, 16), 16), COEF:] = extra

    def step(w, carry):
        after = jnp.where(w == TURNS - 1, 0, w + 1)
        for j in range(5):
            here = pl.ds(pl.multiple_of(w * BLOCK + j * 128, 128), 128)
            there = pl.ds(pl.multiple_of(after * BLOCK + j * 128, 128), 128)
            for k in range(IMG_PEERS):
                cur = image_refs[k][:, here]
                nxt = image_refs[k][:, there]
                for rho in range(FINE // 2):
                    val = turned_on(cur, nxt, rho) if rho else cur
                    early_ref[pl.ds(pl.multiple_of(bases[k] + 32 * rho, 16), 16), here] = val
        return carry

    lax.fori_loop(0, TURNS, step, 0)


def make_late(early_ref, late_ref):
    late_ref[:, COEF:] = early_ref[:, COEF:]

    def step(w, carry):
        after = jnp.where(w == TURNS - 1, 0, w + 1)
        for j in range(5):
            here = pl.ds(pl.multiple_of(w * BLOCK + j * 128, 128), 128)
            there = pl.ds(pl.multiple_of(after * BLOCK + j * 128, 128), 128)
            late_ref[:, here] = turned_on(early_ref[:, here], early_ref[:, there], FINE // 2)
        return carry

    lax.fori_loop(0, TURNS, step, 0)


NT = (((1,), (1,)), ((), ()))


def scores_kernel(early_ref, class_ref, keep_ref, send_ref, stack, late):
    for g in range(TURNS):
        rows = slice(g * CLS, (g + 1) * CLS)
        cut = COEF - g * BLOCK
        stack[rows, g * BLOCK : COEF] = class_ref[:, :cut]
        if g:
            stack[rows, : g * BLOCK] = class_ref[:, cut:COEF]
        stack[rows, COEF:] = class_ref[:, COEF:]
    part = lax.dot_general(stack[...], early_ref[...], NT, preferred_element_type=F32)
    keep_ref[:, :QUARTER] = part[:, :QUARTER]
    send_ref[:, :QUARTER] = part[:, QUARTER:]
    make_late(early_ref, late)
    part = lax.dot_general(stack[...], late[...], NT, preferred_element_type=F32)
    keep_ref[:, QUARTER:] = part[:, :QUARTER]
    send_ref[:, QUARTER:] = part[:, QUARTER:]


def over_rotations(op, x):
    for s in (32, 64, 128):
        x = op(x, pltpu.roll(x, s, 1))
    return x


def stats_kernel(mine_ref, other_ref, scores_ref, stats_ref):
    scores = mine_ref[...] + other_ref[...]
    scores_ref[...] = scores
    big = jnp.max(scores, axis=0, keepdims=True)
    big = over_rotations(jnp.maximum, jnp.broadcast_to(big, (8, HALF)))
    part = jnp.sum(jnp.exp(scores - big[:1]), axis=0, keepdims=True)
    part = over_rotations(jnp.add, jnp.broadcast_to(part, (8, HALF)))
    row = lax.broadcasted_iota(jnp.int32, (8, HALF), 0)
    stats_ref[...] = jnp.where(row < 4, big, part)


def probs_kernel(scores_ref, s0, s1, s2, s3, probs_ref, evidence_ref):
    stats = [s[...] for s in (s0, s1, s2, s3)]
    bigs = [s[0:1] for s in stats]
    parts = [s[4:5] for s in stats]
    largest = jnp.maximum(jnp.maximum(bigs[0], bigs[1]), jnp.maximum(bigs[2], bigs[3]))
    total = sum(p * jnp.exp(b - largest) for b, p in zip(bigs, parts))
    evidence = largest + jnp.log(total)
    probs_ref[...] = jnp.exp(scores_ref[...] - evidence).astype(BF16)
    evidence_ref[...] = jnp.broadcast_to(evidence, (8, HALF))


def sums_kernel(early_ref, late_ref, keep_ref, other_ref, out_ref, probs, sums):
    probs[:, :QUARTER] = keep_ref[:, :QUARTER]
    probs[:, QUARTER:HALF] = other_ref[:, :QUARTER]
    probs[:, HALF : HALF + QUARTER] = keep_ref[:, QUARTER:]
    probs[:, HALF + QUARTER :] = other_ref[:, QUARTER:]
    for w in range(0, TURNS, 2):
        span = slice(w * BLOCK, (w + 2) * BLOCK + (128 if w == TURNS - 2 else 0))
        turned = jnp.dot(
            probs[:, :HALF], early_ref[:, span], preferred_element_type=F32
        ) + jnp.dot(probs[:, HALF:], late_ref[:, span], preferred_element_type=F32)
        for b in (w, w + 1):
            for g in range(TURNS):
                back = (b - g) % TURNS
                at = slice(back * BLOCK, (back + 1) * BLOCK)
                term = turned[g * CLS : (g + 1) * CLS, (b - w) * BLOCK : (b - w + 1) * BLOCK]
                if b == 0:
                    sums[:, at] = term
                else:
                    sums[:, at] += term
        if w == TURNS - 2:
            mass = turned[:CLS, 2 * BLOCK :]
            for g in range(1, TURNS):
                mass = mass + turned[g * CLS : (g + 1) * CLS, 2 * BLOCK :]
    mass = mass + pltpu.roll(mass, 118, 1) + pltpu.roll(mass, 98, 1)
    mass = jnp.where(lanes_of((CLS, 128)) < CYC, mass, 0.0)
    hi, mid, lo = three_parts(mass)
    sums[:, COEF:] = hi + pltpu.roll(mid, 10, 1) + pltpu.roll(lo, 20, 1)
    for d in range(CLS_PEERS):
        out_ref[d] = sums[d * OWN_CLASSES : (d + 1) * OWN_CLASSES, :].astype(BF16)


def final_kernel(first_ref, offset_ref, msg_ref, prior_ref, out_ref):
    r = lax.broadcasted_iota(jnp.int32, (16, CLS), 0)
    k = lax.broadcasted_iota(jnp.int32, (16, CLS), 1)
    chosen = jnp.where(k % OWN_CLASSES == r, 1.0, 0.0).astype(BF16)
    total = jnp.dot(chosen, msg_ref[...], preferred_element_type=F32)[:8]
    lane = lanes_of((8, 128))
    extra = total[:, COEF:]
    den = extra + pltpu.roll(extra, 118, 1) + pltpu.roll(extra, 108, 1)
    tiles = {}
    for j in range(5):
        below = []
        for p in (2 * j, 2 * j + 1):
            below.append(den[:, p : p + 1] + prior_ref[0:1, p : p + 1])
        below = jnp.where(lane % 4 < 2, below[0], below[1])
        for w in range(TURNS):
            at = w * BLOCK + j * 128
            tiles[w, j] = total[:, at : at + 128] / below
    keys = list(tiles)
    flat = jnp.concatenate([tiles[k] for k in keys], axis=0).astype(BF16)
    flat = jnp.dot(flat, interleaving(back=True), preferred_element_type=F32)
    tiles = {k: flat[8 * n : 8 * n + 8] for n, k in enumerate(keys)}
    rows = []
    for p in range(CYC):
        vregs = []
        for v in range(3):
            parts = []
            for u in range(4):
                start = 128 * v + 32 * u
                q, w = start // ANG, (start % ANG) // TURN
                t = 2 * (p % 2) + q
                shift = (32 * u - 32 * t) % 128
                piece = tiles[w, p // 2]
                parts.append(pltpu.roll(piece, shift, 1) if shift else piece)
            vregs.append(pick4(lane, parts))
        rows.append(jnp.concatenate(vregs, axis=1))
    shifts = []
    for c in range(OWN_CLASSES):
        off = offset_ref[first_ref[0] + c]
        shifts.append(jnp.where(off == 0, 0, ROW - off))
    turned = turn_classes(jnp.concatenate(rows, axis=0), shifts)
    for p in range(CYC):
        out_ref[p] = turned[p * 8 : p * 8 + OWN_CLASSES].astype(BF16)


def call(kernel, outs, scratch, specs, limit=VMEM_LIMIT, cost=None):
    return pl.pallas_call(
        kernel,
        out_shape=outs,
        in_specs=[pl.BlockSpec(memory_space=s) for s in specs],
        out_specs=jax.tree.map(lambda _: pl.BlockSpec(memory_space=pltpu.VMEM), outs),
        scratch_shapes=scratch,
        compiler_params=pltpu.CompilerParams(vmem_limit_bytes=limit),
        cost_estimate=cost,
    )


S, V = pltpu.SMEM, pltpu.VMEM


def shaped(shape, dtype):
    return jax.ShapeDtypeStruct(shape, dtype)


def local(images, references, class_offset, ctf_group, ctf, noise_power, prior_precision):
    img = lax.axis_index("img")
    core = lax.axis_index("shell") % 2
    level = (img // 4) % 4
    first = (img * OWN_CLASSES).astype(jnp.int32).reshape(1)
    place = jnp.stack([level, core]).astype(jnp.int32)

    def along_peers(x, k):
        return lax.ppermute(x, "img", [(i, i ^ (4 * k)) for i in range(64)])

    def along_shell(x, k):
        return lax.ppermute(x, "shell", [(i, i ^ k) for i in range(4)])

    groups = [[16 * y + 4 * z + x for y in range(4) for x in range(4)] for z in range(4)]

    def over_classes(x):
        return lax.all_to_all(x, "img", 0, 0, axis_index_groups=groups, tiled=True)

    image_msg, class_msg = call(
        prologue_kernel,
        [shaped((OWN_IMAGES, WIDE), BF16), shaped((CLS_PEERS, OWN_CLASSES, WIDE), BF16)],
        [V((16, 128), F32)] * 4 + [V((CYC * 8, ROW), F32), V((8, WIDE), F32)],
        [S, S, S, V, V, V, V],
        VMEM_MOST,
    )(
        first, class_offset, ctf_group, jnp.transpose(images, (1, 0, 2)),
        jnp.transpose(references, (1, 0, 2)), ctf, noise_power.reshape(1, CYC),
    )
    held = [image_msg] + [along_peers(image_msg, k) for k in (1, 2, 3)]
    class_all = over_classes(class_msg).reshape(CLS, WIDE)
    early = call(
        early_kernel,
        shaped((HALF, WIDE), BF16),
        [],
        [S] + [V] * 4,
        cost=pl.CostEstimate(flops=10**13, transcendentals=0, bytes_accessed=10**10),
    )(place, *held)
    keep, send = call(
        scores_kernel,
        [shaped((ROWS, HALF), F32)] * 2,
        [V((ROWS, WIDE), BF16), V((HALF, WIDE), BF16)],
        [V, V],
    )(early, class_all)
    pair = keep + along_shell(send, 1)
    other = along_shell(pair, 2)
    early, pair = lax.optimization_barrier((early, pair))
    late = call(make_late, shaped((HALF, WIDE), BF16), [], [V])(early)
    late, other = lax.optimization_barrier((late, other))
    scores, stats = call(
        stats_kernel, [shaped((ROWS, HALF), F32), shaped((8, HALF), F32)], [], [V, V]
    )(pair, other)
    all_stats = [stats] + [along_peers(stats, k) for k in (1, 2, 3)]
    probs, evidence = call(
        probs_kernel, [shaped((ROWS, HALF), BF16), shaped((8, HALF), F32)], [], [V] * 5
    )(scores, *all_stats)
    probs_other = along_shell(probs, 1)
    evidence_other = along_shell(evidence, 1)
    sums = call(
        sums_kernel,
        shaped((CLS_PEERS, OWN_CLASSES, WIDE), BF16),
        [V((ROWS, 2 * HALF), BF16), V((CLS, WIDE), F32)],
        [V] * 4,
    )(early, late, probs, probs_other)
    own = over_classes(sums).reshape(CLS, WIDE)
    new_references = call(
        final_kernel,
        shaped((CYC, OWN_CLASSES, ROW), BF16),
        [],
        [S, S, V, V],
    )(first, class_offset, own, prior_precision.reshape(1, CYC))
    mine = jnp.where(core == level // 2, evidence[0], evidence_other[0])
    log_evidence = lax.dynamic_slice_in_dim(mine, (level % 2) * OWN_IMAGES, OWN_IMAGES)
    return jnp.transpose(new_references, (1, 0, 2)), log_evidence


def solution(mesh):
    placed = (
        P("img", "shell", None),
        P("img", "shell", None),
        P(),
        P("img"),
        P(None, "shell"),
        P("shell"),
        P("shell"),
    )
    return jax.shard_map(
        local,
        mesh=mesh,
        in_specs=placed,
        out_specs=(P("img", "shell", None), P("img")),
        check_vma=False,
    )
```

time: 90.9 us -> 82.6 us (0.909)
  waiting for transfers between devices: 34.7 us -> 30.3 us
  local copies, waits for them, and re-layouts: 6.32 us -> 2.6 us
    ppermute x4, waiting for transfers between devices: 15.9 us -> 10.9 us  [along_shell(): return lax.ppermute(x, 'shell', [(i, i ^ k) for i in range(4)])]
    all_to_all x2, starting transfers between devices: 14.2 us -> 10.4 us  [over_classes(): return lax.all_to_all(x, 'img', 0, 0, axis_index_groups=groups, tiled=True)]
    ppermute x6, starting transfers between devices: 8.38 us -> 12 us  [along_peers(): return lax.ppermute(x, 'img', [(i, i ^ 4 * k) for i in range(64)])]
    unnamed x13 -> x6, local copies, waits for them, and re-layouts: 3.74 us -> 0.92 us
    all_to_all x4 -> x0, local copies, waits for them, and re-layouts: 2.57 us -> none  [over_classes(): return lax.all_to_all(x, 'img', 0, 0, axis_index_groups=groups, tiled=True)]
    reshape x0 -> x2, local copies, waits for them, and re-layouts: none -> 1.68 us  [the longest x1 1.36 us: local(): class_all = over_classes(class_msg).reshape(CLS, WIDE)]
    ppermute x6, waiting for transfers between devices: 4.78 us -> 5.89 us  [along_peers(): return lax.ppermute(x, 'img', [(i, i ^ 4 * k) for i in range(64)])]
    pallas_call x4 -> x6, Pallas kernels: 13.8 us -> 13.4 us  [the longest x1 3.78 us: local(): call(scores_kernel, [shaped((ROWS, HALF), F32)] * 2, [V((ROWS, WIDE), BF1...]
  transfers between devices with their start and end apart: 12 -> 12, of which waited for: 9 -> 9; matrix products, arithmetic and copies ran while one was open for 1% -> 1% of each run, Pallas kernels for 0% -> 3%
where the time goes in v2:
time: 82.6 us; the launch traced here: 82.2 us
  starting transfers between devices  34 us (41%)
  waiting for transfers between devices  30.3 us (37%)
  Pallas kernels  13.9 us (17%)
  local copies, waits for them, and re-layouts  2.6 us (3%)
    all_to_all x2, waiting for transfers between devices, over_classes(): return lax.all_to_all(x, 'img', 0, 0, axis_index_groups=groups, tiled=True)  13.5 us
    ppermute x6, starting transfers between devices, along_peers(): return lax.ppermute(x, 'img', [(i, i ^ 4 * k) for i in range(64)])  12 us
    ppermute x4, starting transfers between devices, along_shell(): return lax.ppermute(x, 'shell', [(i, i ^ k) for i in range(4)])  11.6 us
    ppermute x4, waiting for transfers between devices, along_shell(): return lax.ppermute(x, 'shell', [(i, i ^ k) for i in range(4)])  10.9 us
    all_to_all x2, starting transfers between devices, over_classes(): return lax.all_to_all(x, 'img', 0, 0, axis_index_groups=groups, tiled=True)  10.4 us
    ppermute x6, waiting for transfers between devices, along_peers(): return lax.ppermute(x, 'img', [(i, i ^ 4 * k) for i in range(64)])  5.89 us
    pallas_call x1, Pallas kernels, local(): call(scores_kernel, [shaped((ROWS, HALF), F32)] * 2, [V((ROWS, WIDE), BF1...  3.78 us
    pallas_call x1, Pallas kernels, local(): call(prologue_kernel, [shaped((OWN_IMAGES, WIDE), BF16), shaped((CLS_PEER...  2.53 us
  transfers between devices with their start and end apart: 12, of which 9 were waited for; matrix products, arithmetic and copies ran while one was open for 1% of the time, Pallas kernels for 3%

profile of v2, /device:TPU:1, one launch (start us, length us, event | category | flops | bytes accessed | tf_op | source)
XLA Modules:
  0.0 82.2 jit_solution(8055561912888687533)
XLA Ops:
  0.6 2.5 %shard_map.86 = (bf16[16,3968]{1,0:T(8,128)(2,1)}, bf16[16,3,3968]{2,1,0:T(4,128)(2,1)}) custom-call(s32[1]{0:T(128)} %bitcast.first_ref, s32[192]{0:T(256)} %offset_ref.3, s32[16]{0:T(128)} %group_ref.1, f32[10,16,384]{2,1,0:T(8,128)} %bitcast.11, bf16[10,3,384]{2,1,0:T(4,128)(2,1)} %bitcast.12, f32[16,10]{1,0:T(8,128)} %ctf_ref.1, f32[1,10]{1,0:T(1,128)} %bitcast.14), custom_call_target="tpu_custom_call" | custom-call | tf_op jit(solution)/shard_map/pallas_call | solution.py:364
  3.2 5.2 %collective-permute-start.2 = (bf16[16,3968]{1,0:T(8,128)(2,1)}, bf16[16,3968]{1,0:T(8,128)(2,1)S(1)}, u32[]{:S(2)}, u32[]{:S(2)}) collective-permute-start(bf16[16,3968]{1,0:T(8,128)(2,1)} %get-tuple-element.14.f0), channel_id=1, source_target_pairs={{0,48},{4,52},{8,56},{12,60},{16,32},{20,36},{24,40},{28,44},{32,1... | collective-permute-start | bytes 380936 | tf_op jit(solution)/shard_map/ppermute | solution.py:354
  8.6 6.8 %all-to-all-start = ((bf16[16,3,3968]{2,1,0:T(4,128)(2,1)}), bf16[16,3,3968]{2,1,0:T(4,128)(2,1)}, u32[]{:S(2)}, u32[]{:S(2)}) async-start(bf16[16,3,3968]{2,1,0:T(4,128)(2,1)} %get-tuple-element.15), calls=%async_computation | async-start | bytes 1015808 | tf_op jit(solution)/shard_map/all_to_all | solution.py:362
  15.6 2.8 %collective-permute-done.1.f2 = bf16[16,3968]{1,0:T(8,128)(2,1)S(1)} collective-permute-done((bf16[16,3968]{1,0:T(8,128)(2,1)}, bf16[16,3968]{1,0:T(8,128)(2,1)S(1)}, u32[]{:S(2)}, u32[]{:S(2)}) %collective-permute-start.1) | collective-permute-done | bytes 127008 | tf_op jit(solution)/shard_map/ppermute | solution.py:354
  18.4 0.9 %copy-done.2 = bf16[16,3968]{1,0:T(8,128)(2,1)S(1)} copy-done((bf16[16,3968]{1,0:T(8,128)(2,1)S(1)}, bf16[16,3968]{1,0:T(8,128)(2,1)}, u32[]{:S(2)}) %copy-start.2) | copy-done | bytes 127000
  19.3 1.7 %shard_map.87.early_ref = bf16[256,3968]{1,0:T(8,128)(2,1)S(1)} custom-call(s32[2]{0:T(128)S(1)} %pad_add_fusion.place_ref, bf16[16,3968]{1,0:T(8,128)(2,1)S(1)} %copy-done.2, bf16[16,3968]{1,0:T(8,128)(2,1)S(1)} %collective-permute-done.f1, bf16[16,3968]{1,0:T(8,128)(2,1)S(1)} %collective-permute-done.1.f2, bf16[16,3968]{1,0:T(8,128)(2,1)S(1)} %collective-permute-done.2.f3), custom_call_target="tpu_custom_call" | custom-call | flops 9999999827968 | bytes 10000000000 | tf_op jit(solution)/shard_map/pallas_call | solution.py:376
  20.9 4.5 %all-to-all-done = bf16[16,3,3968]{2,1,0:T(4,128)(2,1)} async-done(((bf16[16,3,3968]{2,1,0:T(4,128)(2,1)}), bf16[16,3,3968]{2,1,0:T(4,128)(2,1)}, u32[]{:S(2)}, u32[]{:S(2)}) %all-to-all-start) | async-done | bytes 380960 | tf_op jit(solution)/shard_map/all_to_all | solution.py:362
  25.5 1.4 %reshape.24.class_ref = bf16[48,3968]{1,0:T(8,128)(2,1)S(1)} reshape(bf16[16,3,3968]{2,1,0:T(4,128)(2,1)} %all-to-all-done) | data formatting | bytes 761856 | tf_op jit(solution)/shard_map/reshape | solution.py:375
  26.9 3.8 %shard_map.88 = (f32[288,256]{1,0:T(8,128)S(1)}, f32[288,256]{1,0:T(8,128)S(1)}) custom-call(bf16[256,3968]{1,0:T(8,128)(2,1)S(1)} %shard_map.87.early_ref, bf16[48,3968]{1,0:T(8,128)(2,1)S(1)} %reshape.24.class_ref), custom_call_target="tpu_custom_call" | custom-call | tf_op jit(solution)/shard_map/pallas_call | solution.py:383
  30.6 2.4 %collective-permute-start.3 = (f32[288,256]{1,0:T(8,128)S(1)}, f32[288,256]{1,0:T(8,128)S(1)}, u32[]{:S(2)}, u32[]{:S(2)}) collective-permute-start(f32[288,256]{1,0:T(8,128)S(1)} %get-tuple-element.17), channel_id=1, source_target_pairs={{0,1},{1,0},{2,3},{3,2},{4,5},{5,4},{6,7},{7,6},{8,9},{9,8},{10,11... | collective-permute-start | bytes 884744 | tf_op jit(solution)/shard_map/ppermute | solution.py:357
  33.0 1.2 %collective-permute-done.3 = f32[288,256]{1,0:T(8,128)S(1)} collective-permute-done((f32[288,256]{1,0:T(8,128)S(1)}, f32[288,256]{1,0:T(8,128)S(1)}, u32[]{:S(2)}, u32[]{:S(2)}) %collective-permute-start.3) | collective-permute-done | bytes 294944 | tf_op jit(solution)/shard_map/ppermute | solution.py:357
  34.3 6.0 %collective-permute-start.4 = (f32[288,256]{1,0:T(8,128)S(1)}, f32[288,256]{1,0:T(8,128)S(1)}, u32[]{:S(2)}, u32[]{:S(2)}) collective-permute-start(f32[288,256]{1,0:T(8,128)S(1)} %add.20.mine_ref), channel_id=1, source_target_pairs={{0,2},{1,3},{2,0},{3,1},{4,6},{5,7},{6,4},{7,5},{8,10},{9,11},{10,... | collective-permute-start | bytes 884744 | tf_op jit(solution)/shard_map/ppermute | solution.py:357
  40.2 1.0 %shard_map.89.late_ref = bf16[256,3968]{1,0:T(8,128)(2,1)S(1)} custom-call(bf16[256,3968]{1,0:T(8,128)(2,1)S(1)} %shard_map.87.early_ref), custom_call_target="tpu_custom_call" | custom-call | tf_op jit(solution)/shard_map/pallas_call | solution.py:392
  41.2 7.9 %collective-permute-done.4.other_ref = f32[288,256]{1,0:T(8,128)S(1)} collective-permute-done((f32[288,256]{1,0:T(8,128)S(1)}, f32[288,256]{1,0:T(8,128)S(1)}, u32[]{:S(2)}, u32[]{:S(2)}) %collective-permute-start.4) | collective-permute-done | bytes 294944 | tf_op jit(solution)/shard_map/ppermute | solution.py:357
  49.5 6.2 %collective-permute-start.7 = (f32[8,256]{1,0:T(8,128)S(1)}, f32[8,256]{1,0:T(8,128)S(1)}, u32[]{:S(2)}, u32[]{:S(2)}) collective-permute-start(f32[8,256]{1,0:T(8,128)S(1)} %get-tuple-element.23.s0), channel_id=1, source_target_pairs={{0,48},{4,52},{8,56},{12,60},{16,32},{20,36},{24,40},{28,44},{32,1... | collective-permute-start | bytes 24584 | tf_op jit(solution)/shard_map/ppermute | solution.py:354
  56.1 0.7 collective-permute-done.7.s3
  56.8 2.4 %collective-permute-done.6.s2 = f32[8,256]{1,0:T(8,128)S(1)} collective-permute-done((f32[8,256]{1,0:T(8,128)S(1)}, f32[8,256]{1,0:T(8,128)S(1)}, u32[]{:S(2)}, u32[]{:S(2)}) %collective-permute-start.6) | collective-permute-done | bytes 8224 | tf_op jit(solution)/shard_map/ppermute | solution.py:354
  59.2 2.8 %collective-permute-start.8 = (bf16[288,256]{1,0:T(8,128)(2,1)S(1)}, bf16[288,256]{1,0:T(8,128)(2,1)S(1)}, u32[]{:S(2)}, u32[]{:S(2)}) collective-permute-start(bf16[288,256]{1,0:T(8,128)(2,1)S(1)} %get-tuple-element.24.keep_ref), channel_id=1, source_target_pairs={{0,1},{1,0},{2,3},{3,2},{4,5},{5,4},{6,7},{7,6},{8,9},{9,8},{10,11... | collective-permute-start | bytes 442376 | tf_op jit(solution)/shard_map/ppermute | solution.py:357
  62.0 1.0 %collective-permute-done.8.other_ref = bf16[288,256]{1,0:T(8,128)(2,1)S(1)} collective-permute-done((bf16[288,256]{1,0:T(8,128)(2,1)S(1)}, bf16[288,256]{1,0:T(8,128)(2,1)S(1)}, u32[]{:S(2)}, u32[]{:S(2)}) %collective-permute-start.8) | collective-permute-done | bytes 147488 | tf_op jit(solution)/shard_map/ppermute | solution.py:357
  63.0 2.5 %shard_map.92 = bf16[16,3,3968]{2,1,0:T(4,128)(2,1)} custom-call(bf16[256,3968]{1,0:T(8,128)(2,1)S(1)} %shard_map.87.early_ref, bf16[256,3968]{1,0:T(8,128)(2,1)S(1)} %shard_map.89.late_ref, bf16[288,256]{1,0:T(8,128)(2,1)S(1)} %get-tuple-element.24.keep_ref, bf16[288,256]{1,0:T(8,128)(2,1)S(1)} %collective-permute-done.8.other_ref), custom_call_target="tpu_custom_call" | custom-call | tf_op jit(solution)/shard_map/pallas_call | solution.py:403
  65.5 3.6 %all-to-all-start.1 = ((bf16[16,3,3968]{2,1,0:T(4,128)(2,1)}), bf16[16,3,3968]{2,1,0:T(4,128)(2,1)S(1)}, u32[]{:S(2)}, u32[]{:S(2)}) async-start(bf16[16,3,3968]{2,1,0:T(4,128)(2,1)} %shard_map.92), calls=%async_computation.1 | async-start | bytes 1015808 | tf_op jit(solution)/shard_map/all_to_all | solution.py:362
  69.5 0.8 %collective-permute-done.9 = f32[8,256]{1,0:T(8,128)S(1)} collective-permute-done((f32[8,256]{1,0:T(8,128)S(1)}, f32[8,256]{1,0:T(8,128)S(1)}, u32[]{:S(2)}, u32[]{:S(2)}) %collective-permute-start.9) | collective-permute-done | bytes 8224 | tf_op jit(solution)/shard_map/ppermute | solution.py:357
  70.9 8.9 %all-to-all-done.1 = bf16[16,3,3968]{2,1,0:T(4,128)(2,1)S(1)} async-done(((bf16[16,3,3968]{2,1,0:T(4,128)(2,1)}), bf16[16,3,3968]{2,1,0:T(4,128)(2,1)S(1)}, u32[]{:S(2)}, u32[]{:S(2)}) %all-to-all-start.1) | async-done | bytes 380960 | tf_op jit(solution)/shard_map/all_to_all | solution.py:362
  80.2 2.0 %shard_map.93 = bf16[10,3,384]{2,1,0:T(4,128)(2,1)} custom-call(s32[1]{0:T(128)} %bitcast.first_ref, s32[192]{0:T(256)S(1)} %copy-done, bf16[48,3968]{1,0:T(8,128)(2,1)S(1)} %reshape.25.msg_ref, f32[1,10]{1,0:T(1,128)S(1)} %bitcast.10), custom_call_target="tpu_custom_call" | custom-call | tf_op jit(solution)/shard_map/pallas_call | solution.py:410
  (21 shorter events, 2.6 us)
Async XLA Ops:
  3.2 12.4 %collective-permute-start.2 = (bf16[16,3968]{1,0:T(8,128)(2,1)}, bf16[16,3968]{1,0:T(8,128)(2,1)S(1)}, u32[]{:S(2)}, u32[]{:S(2)}) collective-permute-start(bf16[16,3968]{1,0:T(8,128)(2,1)} %get-tuple-element.14.f0), channel_id=1, source_target_pairs={{0,48},{4,52},{8,56},{12,60},{16,32},{20,36},{24,40},{28,44},{32,1... | collective-permute-start | bytes 380936 | tf_op jit(solution)/shard_map/ppermute | solution.py:354
  8.3 10.0 %collective-permute-start.1 = (bf16[16,3968]{1,0:T(8,128)(2,1)}, bf16[16,3968]{1,0:T(8,128)(2,1)S(1)}, u32[]{:S(2)}, u32[]{:S(2)}) collective-permute-start(bf16[16,3968]{1,0:T(8,128)(2,1)} %get-tuple-element.14.f0), channel_id=1, source_target_pairs={{0,32},{4,36},{8,40},{12,44},{16,48},{20,52},{24,56},{28,60},{32,0... | collective-permute-start | bytes 380936 | tf_op jit(solution)/shard_map/ppermute | solution.py:354
  8.3 10.0 %collective-permute-start = (bf16[16,3968]{1,0:T(8,128)(2,1)}, bf16[16,3968]{1,0:T(8,128)(2,1)S(1)}, u32[]{:S(2)}, u32[]{:S(2)}) collective-permute-start(bf16[16,3968]{1,0:T(8,128)(2,1)} %get-tuple-element.14.f0), channel_id=1, source_target_pairs={{0,16},{4,20},{8,24},{12,28},{16,0},{20,4},{24,8},{28,12},{32,48},... | collective-permute-start | bytes 380936 | tf_op jit(solution)/shard_map/ppermute | solution.py:354
  8.6 16.9 %all-to-all-start = ((bf16[16,3,3968]{2,1,0:T(4,128)(2,1)}), bf16[16,3,3968]{2,1,0:T(4,128)(2,1)}, u32[]{:S(2)}, u32[]{:S(2)}) async-start(bf16[16,3,3968]{2,1,0:T(4,128)(2,1)} %get-tuple-element.15), calls=%async_computation | async-start | bytes 1015808 | tf_op jit(solution)/shard_map/all_to_all | solution.py:362
  18.4 0.9 %copy-start.2 = (bf16[16,3968]{1,0:T(8,128)(2,1)S(1)}, bf16[16,3968]{1,0:T(8,128)(2,1)}, u32[]{:S(2)}) copy-start(bf16[16,3968]{1,0:T(8,128)(2,1)} %get-tuple-element.14.f0) | copy-start | bytes 380932
  30.6 3.6 %collective-permute-start.3 = (f32[288,256]{1,0:T(8,128)S(1)}, f32[288,256]{1,0:T(8,128)S(1)}, u32[]{:S(2)}, u32[]{:S(2)}) collective-permute-start(f32[288,256]{1,0:T(8,128)S(1)} %get-tuple-element.17), channel_id=1, source_target_pairs={{0,1},{1,0},{2,3},{3,2},{4,5},{5,4},{6,7},{7,6},{8,9},{9,8},{10,11... | collective-permute-start | bytes 884744 | tf_op jit(solution)/shard_map/ppermute | solution.py:357
  34.3 14.8 %collective-permute-start.4 = (f32[288,256]{1,0:T(8,128)S(1)}, f32[288,256]{1,0:T(8,128)S(1)}, u32[]{:S(2)}, u32[]{:S(2)}) collective-permute-start(f32[288,256]{1,0:T(8,128)S(1)} %add.20.mine_ref), channel_id=1, source_target_pairs={{0,2},{1,3},{2,0},{3,1},{4,6},{5,7},{6,4},{7,5},{8,10},{9,11},{10,... | collective-permute-start | bytes 884744 | tf_op jit(solution)/shard_map/ppermute | solution.py:357
  49.5 7.3 %collective-permute-start.7 = (f32[8,256]{1,0:T(8,128)S(1)}, f32[8,256]{1,0:T(8,128)S(1)}, u32[]{:S(2)}, u32[]{:S(2)}) collective-permute-start(f32[8,256]{1,0:T(8,128)S(1)} %get-tuple-element.23.s0), channel_id=1, source_target_pairs={{0,48},{4,52},{8,56},{12,60},{16,32},{20,36},{24,40},{28,44},{32,1... | collective-permute-start | bytes 24584 | tf_op jit(solution)/shard_map/ppermute | solution.py:354
  55.7 3.4 %collective-permute-start.6 = (f32[8,256]{1,0:T(8,128)S(1)}, f32[8,256]{1,0:T(8,128)S(1)}, u32[]{:S(2)}, u32[]{:S(2)}) collective-permute-start(f32[8,256]{1,0:T(8,128)S(1)} %get-tuple-element.23.s0), channel_id=1, source_target_pairs={{0,32},{4,36},{8,40},{12,44},{16,48},{20,52},{24,56},{28,60},{32,0... | collective-permute-start | bytes 24584 | tf_op jit(solution)/shard_map/ppermute | solution.py:354
  55.7 3.4 %collective-permute-start.5 = (f32[8,256]{1,0:T(8,128)S(1)}, f32[8,256]{1,0:T(8,128)S(1)}, u32[]{:S(2)}, u32[]{:S(2)}) collective-permute-start(f32[8,256]{1,0:T(8,128)S(1)} %get-tuple-element.23.s0), channel_id=1, source_target_pairs={{0,16},{4,20},{8,24},{12,28},{16,0},{20,4},{24,8},{28,12},{32,48},... | collective-permute-start | bytes 24584 | tf_op jit(solution)/shard_map/ppermute | solution.py:354
  59.2 21.0 %copy-start = (s32[192]{0:T(256)S(1)}, s32[192]{0:T(256)}, u32[]{:S(2)}) copy-start(s32[192]{0:T(256)} %offset_ref.3) | copy-start | bytes 2308
  59.2 21.0 %copy-start.1 = (f32[10]{0:T(128)S(1)}, f32[10]{0:T(128)}, u32[]{:S(2)}) copy-start(f32[10]{0:T(128)} %param.13) | copy-start | bytes 124
  59.2 3.8 %collective-permute-start.8 = (bf16[288,256]{1,0:T(8,128)(2,1)S(1)}, bf16[288,256]{1,0:T(8,128)(2,1)S(1)}, u32[]{:S(2)}, u32[]{:S(2)}) collective-permute-start(bf16[288,256]{1,0:T(8,128)(2,1)S(1)} %get-tuple-element.24.keep_ref), channel_id=1, source_target_pairs={{0,1},{1,0},{2,3},{3,2},{4,5},{5,4},{6,7},{7,6},{8,9},{9,8},{10,11... | collective-permute-start | bytes 442376 | tf_op jit(solution)/shard_map/ppermute | solution.py:357
  65.5 14.4 %all-to-all-start.1 = ((bf16[16,3,3968]{2,1,0:T(4,128)(2,1)}), bf16[16,3,3968]{2,1,0:T(4,128)(2,1)S(1)}, u32[]{:S(2)}, u32[]{:S(2)}) async-start(bf16[16,3,3968]{2,1,0:T(4,128)(2,1)} %shard_map.92), calls=%async_computation.1 | async-start | bytes 1015808 | tf_op jit(solution)/shard_map/all_to_all | solution.py:362
  69.1 1.3 %collective-permute-start.9 = (f32[8,256]{1,0:T(8,128)S(1)}, f32[8,256]{1,0:T(8,128)S(1)}, u32[]{:S(2)}, u32[]{:S(2)}) collective-permute-start(f32[8,256]{1,0:T(8,128)S(1)} %get-tuple-element.25), channel_id=1, source_target_pairs={{0,1},{1,0},{2,3},{3,2},{4,5},{5,4},{6,7},{7,6},{8,9},{9,8},{10,11... | collective-permute-start | bytes 24584 | tf_op jit(solution)/shard_map/ppermute | solution.py:357

commit v3 on v2

--- a/solution.py
+++ b/solution.py
@@ -23,6 +23,9 @@
 IMG_PEERS = 4
 CLS_PEERS = 16
 CLS = OWN_CLASSES * CLS_PEERS
+TILES = WIDE // 128
+SLOT = 32
+CHUNK = OWN_CLASSES * SLOT
 ROWS = TURNS * CLS
 HALF = FINE * OWN_IMAGES * 2
 F32 = jnp.float32
@@ -104,21 +107,23 @@
     for p in range(CYC):
         power = jnp.where(lane8 == p, jnp.sum(rows[p] * rows[p], axis=1, keepdims=True), power)
     mixing = interleaving()
+    own[...] = jnp.zeros_like(own)
     for w in range(TURNS):
         tiles = [turned_tile(rows, w, j, lane8) for j in range(5)]
         tiles = jnp.concatenate(tiles, axis=0).astype(BF16)
         tiles = jnp.dot(tiles, mixing, preferred_element_type=F32)
         for j in range(5):
-            at = w * BLOCK + j * 128
-            own[:, at : at + 128] = tiles[j * 8 : j * 8 + 8]
+            own[pl.ds(w * 5 + j, OWN_CLASSES, stride=SLOT), :] = tiles[
+                j * 8 : j * 8 + OWN_CLASSES
+            ]
     hi, mid, lo = three_parts(-0.5 * power)
     extra = hi
     for k, part in enumerate((hi, mid, hi, mid, lo)):
         extra = extra + pltpu.roll(part, 10 * (k + 1), 1)
-    own[:, COEF:] = extra
-    held = own[:OWN_CLASSES, :].astype(BF16)
+    own[pl.ds(TILES - 1, OWN_CLASSES, stride=SLOT), :] = extra[:OWN_CLASSES]
+    held = own[...].astype(BF16)
     for d in range(CLS_PEERS):
-        class_msg[d] = held
+        class_msg[d * CHUNK : (d + 1) * CHUNK, :] = held
 
     weight = 1.0 / noise_ref[...]
     ctf = ctf_ref[...]
@@ -159,6 +164,14 @@
     return pltpu.roll(jnp.where(lane >= s, cur, nxt), 128 - s, 1)
 
 
+def tile_pairs():
+    for w in range(TURNS):
+        for j in range(5):
+            here = w * BLOCK + j * 128
+            there = (w + 1) % TURNS * BLOCK + j * 128
+            yield slice(here, here + 128), slice(there, there + 128)
+
+
 def early_kernel(place_ref, f0, f1, f2, f3, early_ref):
     image_refs = (f0, f1, f2, f3)
     bases = []
@@ -171,47 +184,33 @@
         for rho in range(FINE // 2):
             early_ref[pl.ds(pl.multiple_of(bases[k] + 32 * rho, 16), 16), COEF:] = extra
 
-    def step(w, carry):
-        after = jnp.where(w == TURNS - 1, 0, w + 1)
-        for j in range(5):
-            here = pl.ds(pl.multiple_of(w * BLOCK + j * 128, 128), 128)
-            there = pl.ds(pl.multiple_of(after * BLOCK + j * 128, 128), 128)
-            for k in range(IMG_PEERS):
-                cur = image_refs[k][:, here]
-                nxt = image_refs[k][:, there]
-                for rho in range(FINE // 2):
-                    val = turned_on(cur, nxt, rho) if rho else cur
-                    early_ref[pl.ds(pl.multiple_of(bases[k] + 32 * rho, 16), 16), here] = val
-        return carry
-
-    lax.fori_loop(0, TURNS, step, 0)
+    for here, there in tile_pairs():
+        for k in range(IMG_PEERS):
+            cur = image_refs[k][:, here]
+            nxt = image_refs[k][:, there]
+            for rho in range(FINE // 2):
+                val = turned_on(cur, nxt, rho) if rho else cur
+                early_ref[pl.ds(pl.multiple_of(bases[k] + 32 * rho, 16), 16), here] = val
 
 
 def make_late(early_ref, late_ref):
     late_ref[:, COEF:] = early_ref[:, COEF:]
-
-    def step(w, carry):
-        after = jnp.where(w == TURNS - 1, 0, w + 1)
-        for j in range(5):
-            here = pl.ds(pl.multiple_of(w * BLOCK + j * 128, 128), 128)
-            there = pl.ds(pl.multiple_of(after * BLOCK + j * 128, 128), 128)
-            late_ref[:, here] = turned_on(early_ref[:, here], early_ref[:, there], FINE // 2)
-        return carry
-
-    lax.fori_loop(0, TURNS, step, 0)
+    for here, there in tile_pairs():
+        late_ref[:, here] = turned_on(early_ref[:, here], early_ref[:, there], FINE // 2)
 
 
 NT = (((1,), (1,)), ((), ()))
 
 
-def scores_kernel(early_ref, class_ref, keep_ref, send_ref, stack, late):
-    for g in range(TURNS):
-        rows = slice(g * CLS, (g + 1) * CLS)
-        cut = COEF - g * BLOCK
-        stack[rows, g * BLOCK : COEF] = class_ref[:, :cut]
-        if g:
-            stack[rows, : g * BLOCK] = class_ref[:, cut:COEF]
-        stack[rows, COEF:] = class_ref[:, COEF:]
+def scores_kernel(early_ref, class_ref, keep_ref, send_ref, wide, stack, late):
+    wide[...] = class_ref[...].astype(F32)
+    for v in range(TILES):
+        for c in range(OWN_CLASSES):
+            tile = wide[pl.ds(c * SLOT + v, CLS_PEERS, stride=CHUNK), :].astype(BF16)
+            for g in range(TURNS):
+                row = g * CLS + c * CLS_PEERS
+                at = v * 128 if v == TILES - 1 else (v * 128 + g * BLOCK) % COEF
+                stack[row : row + CLS_PEERS, at : at + 128] = tile
     part = lax.dot_general(stack[...], early_ref[...], NT, preferred_element_type=F32)
     keep_ref[:, :QUARTER] = part[:, :QUARTER]
     send_ref[:, :QUARTER] = part[:, QUARTER:]
@@ -249,7 +248,7 @@
     evidence_ref[...] = jnp.broadcast_to(evidence, (8, HALF))
 
 
-def sums_kernel(early_ref, late_ref, keep_ref, other_ref, out_ref, probs, sums):
+def sums_kernel(early_ref, late_ref, keep_ref, other_ref, out_ref, probs, sums, packed):
     probs[:, :QUARTER] = keep_ref[:, :QUARTER]
     probs[:, QUARTER:HALF] = other_ref[:, :QUARTER]
     probs[:, HALF : HALF + QUARTER] = keep_ref[:, QUARTER:]
@@ -276,17 +275,22 @@
     mass = jnp.where(lanes_of((CLS, 128)) < CYC, mass, 0.0)
     hi, mid, lo = three_parts(mass)
     sums[:, COEF:] = hi + pltpu.roll(mid, 10, 1) + pltpu.roll(lo, 20, 1)
-    for d in range(CLS_PEERS):
-        out_ref[d] = sums[d * OWN_CLASSES : (d + 1) * OWN_CLASSES, :].astype(BF16)
-
-
-def final_kernel(first_ref, offset_ref, msg_ref, prior_ref, out_ref):
-    r = lax.broadcasted_iota(jnp.int32, (16, CLS), 0)
-    k = lax.broadcasted_iota(jnp.int32, (16, CLS), 1)
-    chosen = jnp.where(k % OWN_CLASSES == r, 1.0, 0.0).astype(BF16)
-    total = jnp.dot(chosen, msg_ref[...], preferred_element_type=F32)[:8]
+    for c in range(OWN_CLASSES):
+        rows = slice(c * CLS_PEERS, (c + 1) * CLS_PEERS)
+        for v in range(SLOT):
+            tile = sums[rows, v * 128 : v * 128 + 128] if v < TILES else jnp.zeros((16, 128), F32)
+            packed[pl.ds(c * SLOT + v, CLS_PEERS, stride=CHUNK), :] = tile
+    out_ref[...] = packed[...].astype(BF16)
+
+
+def final_kernel(first_ref, offset_ref, msg_ref, prior_ref, out_ref, summed):
+    total = msg_ref[:CHUNK, :].astype(F32)
+    for d in range(1, CLS_PEERS):
+        total = total + msg_ref[d * CHUNK : (d + 1) * CHUNK, :].astype(F32)
+    summed[:CHUNK, :] = total
+    summed[CHUNK:, :] = jnp.zeros((8 * SLOT - CHUNK, 128), F32)
     lane = lanes_of((8, 128))
-    extra = total[:, COEF:]
+    extra = summed[pl.ds(TILES - 1, 8, stride=SLOT), :]
     den = extra + pltpu.roll(extra, 118, 1) + pltpu.roll(extra, 108, 1)
     tiles = {}
     for j in range(5):
@@ -295,8 +299,7 @@
             below.append(den[:, p : p + 1] + prior_ref[0:1, p : p + 1])
         below = jnp.where(lane % 4 < 2, below[0], below[1])
         for w in range(TURNS):
-            at = w * BLOCK + j * 128
-            tiles[w, j] = total[:, at : at + 128] / below
+            tiles[w, j] = summed[pl.ds(w * 5 + j, 8, stride=SLOT), :] / below
     keys = list(tiles)
     flat = jnp.concatenate([tiles[k] for k in keys], axis=0).astype(BF16)
     flat = jnp.dot(flat, interleaving(back=True), preferred_element_type=F32)
@@ -363,8 +366,8 @@
 
     image_msg, class_msg = call(
         prologue_kernel,
-        [shaped((OWN_IMAGES, WIDE), BF16), shaped((CLS_PEERS, OWN_CLASSES, WIDE), BF16)],
-        [V((16, 128), F32)] * 4 + [V((CYC * 8, ROW), F32), V((8, WIDE), F32)],
+        [shaped((OWN_IMAGES, WIDE), BF16), shaped((CLS_PEERS * CHUNK, 128), BF16)],
+        [V((16, 128), F32)] * 4 + [V((CYC * 8, ROW), F32), V((CHUNK, 128), F32)],
         [S, S, S, V, V, V, V],
         VMEM_MOST,
     )(
@@ -372,7 +375,7 @@
         jnp.transpose(references, (1, 0, 2)), ctf, noise_power.reshape(1, CYC),
     )
     held = [image_msg] + [along_peers(image_msg, k) for k in (1, 2, 3)]
-    class_all = over_classes(class_msg).reshape(CLS, WIDE)
+    class_all = over_classes(class_msg)
     early = call(
         early_kernel,
         shaped((HALF, WIDE), BF16),
@@ -383,7 +386,7 @@
     keep, send = call(
         scores_kernel,
         [shaped((ROWS, HALF), F32)] * 2,
-        [V((ROWS, WIDE), BF16), V((HALF, WIDE), BF16)],
+        [V((CLS_PEERS * CHUNK, 128), F32), V((ROWS, WIDE), BF16), V((HALF, WIDE), BF16)],
         [V, V],
     )(early, class_all)
     pair = keep + along_shell(send, 1)
@@ -402,15 +405,15 @@
     evidence_other = along_shell(evidence, 1)
     sums = call(
         sums_kernel,
-        shaped((CLS_PEERS, OWN_CLASSES, WIDE), BF16),
-        [V((ROWS, 2 * HALF), BF16), V((CLS, WIDE), F32)],
+        shaped((CLS_PEERS * CHUNK, 128), BF16),
+        [V((ROWS, 2 * HALF), BF16), V((CLS, WIDE), F32), V((CLS_PEERS * CHUNK, 128), F32)],
         [V] * 4,
     )(early, late, probs, probs_other)
-    own = over_classes(sums).reshape(CLS, WIDE)
+    own = over_classes(sums)
     new_references = call(
         final_kernel,
         shaped((CYC, OWN_CLASSES, ROW), BF16),
-        [],
+        [V((8 * SLOT, 128), F32)],
         [S, S, V, V],
     )(first, class_offset, own, prior_precision.reshape(1, CYC))
     mine = jnp.where(core == level // 2, evidence[0], evidence_other[0])

time: 82.6 us -> 78.2 us (0.947)
  waiting for transfers between devices: 30.3 us -> 28.6 us
  local copies, waits for them, and re-layouts: 2.6 us -> 0.92 us
  Pallas kernels: 13.9 us -> 12.4 us
    all_to_all x2, waiting for transfers between devices: 13.5 us -> 11.3 us  [over_classes(): return lax.all_to_all(x, 'img', 0, 0, axis_index_groups=groups, tiled=True)]
    reshape x2 -> x0, local copies, waits for them, and re-layouts: 1.68 us -> none  [the longest x1 1.36 us: local(): class_all = over_classes(class_msg).reshape(CLS, WIDE)]
  transfers between devices with their start and end apart: 12 -> 12, of which waited for: 9 -> 9; matrix products, arithmetic and copies ran while one was open for 1% -> 1% of each run, Pallas kernels for 3% -> 2%
where the time goes in v3:
time: 78.2 us; the launch traced here: 77.8 us
  starting transfers between devices  34.5 us (44%)
  waiting for transfers between devices  28.6 us (37%)
  Pallas kernels  12.4 us (16%)
  local copies, waits for them, and re-layouts  0.92 us (1%)
    ppermute x6, starting transfers between devices, along_peers(): return lax.ppermute(x, 'img', [(i, i ^ 4 * k) for i in range(64)])  12.1 us
    ppermute x4, starting transfers between devices, along_shell(): return lax.ppermute(x, 'shell', [(i, i ^ k) for i in range(4)])  12 us
    ppermute x4, waiting for transfers between devices, along_shell(): return lax.ppermute(x, 'shell', [(i, i ^ k) for i in range(4)])  11.4 us
    all_to_all x2, waiting for transfers between devices, over_classes(): return lax.all_to_all(x, 'img', 0, 0, axis_index_groups=groups, tiled=True)  11.3 us
    all_to_all x2, starting transfers between devices, over_classes(): return lax.all_to_all(x, 'img', 0, 0, axis_index_groups=groups, tiled=True)  10.4 us
    ppermute x6, waiting for transfers between devices, along_peers(): return lax.ppermute(x, 'img', [(i, i ^ 4 * k) for i in range(64)])  5.88 us
    pallas_call x1, Pallas kernels, local(): call(scores_kernel, [shaped((ROWS, HALF), F32)] * 2, [V((CLS_PEERS * CHUN...  3.33 us
    pallas_call x1, Pallas kernels, local(): call(sums_kernel, shaped((CLS_PEERS * CHUNK, 128), BF16), [V((ROWS, 2 * H...  2.73 us
  transfers between devices with their start and end apart: 12, of which 9 were waited for; matrix products, arithmetic and copies ran while one was open for 1% of the time, Pallas kernels for 2%

profile of v3, /device:TPU:1, one launch (start us, length us, event | category | flops | bytes accessed | tf_op | source)
XLA Modules:
  0.0 77.8 jit_solution(4502805339159912661)
XLA Ops:
  0.6 2.5 %shard_map.86 = (bf16[16,3968]{1,0:T(8,128)(2,1)}, bf16[1536,128]{1,0:T(8,128)(2,1)}) custom-call(s32[1]{0:T(128)} %bitcast.first_ref, s32[192]{0:T(256)} %offset_ref.3, s32[16]{0:T(128)} %group_ref.1, f32[10,16,384]{2,1,0:T(8,128)} %bitcast.17, bf16[10,3,384]{2,1,0:T(4,128)(2,1)} %bitcast.18, f32[16,10]{1,0:T(8,128)} %ctf_ref.1, f32[1,10]{1,0:T(1,128)} %bitcast.20), custom_call_target="tpu_custom_call" | custom-call | tf_op jit(solution)/shard_map/pallas_call | solution.py:367
  3.1 5.2 %collective-permute-start.2 = (bf16[16,3968]{1,0:T(8,128)(2,1)}, bf16[16,3968]{1,0:T(8,128)(2,1)S(1)}, u32[]{:S(2)}, u32[]{:S(2)}) collective-permute-start(bf16[16,3968]{1,0:T(8,128)(2,1)} %get-tuple-element.14.f0), channel_id=1, source_target_pairs={{0,48},{4,52},{8,56},{12,60},{16,32},{20,36},{24,40},{28,44},{32,1... | collective-permute-start | bytes 380936 | tf_op jit(solution)/shard_map/ppermute | solution.py:357
  8.6 6.8 %all-to-all-start = ((bf16[16,96,128]{2,1,0:T(8,128)(2,1)}), bf16[16,96,128]{2,1,0:T(8,128)(2,1)}, u32[]{:S(2)}, u32[]{:S(2)}) async-start(bf16[16,96,128]{2,1,0:T(8,128)(2,1)} %bitcast.16), calls=%async_computation | async-start | bytes 786432 | tf_op jit(solution)/shard_map/all_to_all | solution.py:365
  15.5 2.8 %collective-permute-done.1.f2 = bf16[16,3968]{1,0:T(8,128)(2,1)S(1)} collective-permute-done((bf16[16,3968]{1,0:T(8,128)(2,1)}, bf16[16,3968]{1,0:T(8,128)(2,1)S(1)}, u32[]{:S(2)}, u32[]{:S(2)}) %collective-permute-start.1) | collective-permute-done | bytes 127008 | tf_op jit(solution)/shard_map/ppermute | solution.py:357
  18.3 0.9 %copy-done.2 = bf16[16,3968]{1,0:T(8,128)(2,1)S(1)} copy-done((bf16[16,3968]{1,0:T(8,128)(2,1)S(1)}, bf16[16,3968]{1,0:T(8,128)(2,1)}, u32[]{:S(2)}) %copy-start.2) | copy-done | bytes 127000
  19.2 1.0 %shard_map.87.early_ref = bf16[256,3968]{1,0:T(8,128)(2,1)S(1)} custom-call(s32[2]{0:T(128)S(1)} %pad_add_fusion.place_ref, bf16[16,3968]{1,0:T(8,128)(2,1)S(1)} %copy-done.2, bf16[16,3968]{1,0:T(8,128)(2,1)S(1)} %collective-permute-done.f1, bf16[16,3968]{1,0:T(8,128)(2,1)S(1)} %collective-permute-done.1.f2, bf16[16,3968]{1,0:T(8,128)(2,1)S(1)} %collective-permute-done.2.f3), custom_call_target="tpu_custom_call" | custom-call | flops 9999999827968 | bytes 10000000000 | tf_op jit(solution)/shard_map/pallas_call | solution.py:379
  20.2 3.6 %all-to-all-done = bf16[16,96,128]{2,1,0:T(8,128)(2,1)} async-done(((bf16[16,96,128]{2,1,0:T(8,128)(2,1)}), bf16[16,96,128]{2,1,0:T(8,128)(2,1)}, u32[]{:S(2)}, u32[]{:S(2)}) %all-to-all-start) | async-done | bytes 393248 | tf_op jit(solution)/shard_map/all_to_all | solution.py:365
  23.9 3.3 %shard_map.88 = (f32[288,256]{1,0:T(8,128)S(1)}, f32[288,256]{1,0:T(8,128)S(1)}) custom-call(bf16[256,3968]{1,0:T(8,128)(2,1)S(1)} %shard_map.87.early_ref, bf16[1536,128]{1,0:T(8,128)(2,1)} %bitcast.7.class_ref), custom_call_target="tpu_custom_call" | custom-call | tf_op jit(solution)/shard_map/pallas_call | solution.py:386
  27.2 2.7 %collective-permute-start.3 = (f32[288,256]{1,0:T(8,128)S(1)}, f32[288,256]{1,0:T(8,128)S(1)}, u32[]{:S(2)}, u32[]{:S(2)}) collective-permute-start(f32[288,256]{1,0:T(8,128)S(1)} %get-tuple-element.17), channel_id=1, source_target_pairs={{0,1},{1,0},{2,3},{3,2},{4,5},{5,4},{6,7},{7,6},{8,9},{9,8},{10,11... | collective-permute-start | bytes 884744 | tf_op jit(solution)/shard_map/ppermute | solution.py:360
  29.9 1.2 %collective-permute-done.3 = f32[288,256]{1,0:T(8,128)S(1)} collective-permute-done((f32[288,256]{1,0:T(8,128)S(1)}, f32[288,256]{1,0:T(8,128)S(1)}, u32[]{:S(2)}, u32[]{:S(2)}) %collective-permute-start.3) | collective-permute-done | bytes 294944 | tf_op jit(solution)/shard_map/ppermute | solution.py:360
  31.2 6.1 %collective-permute-start.4 = (f32[288,256]{1,0:T(8,128)S(1)}, f32[288,256]{1,0:T(8,128)S(1)}, u32[]{:S(2)}, u32[]{:S(2)}) collective-permute-start(f32[288,256]{1,0:T(8,128)S(1)} %add.20.mine_ref), channel_id=1, source_target_pairs={{0,2},{1,3},{2,0},{3,1},{4,6},{5,7},{6,4},{7,5},{8,10},{9,11},{10,... | collective-permute-start | bytes 884744 | tf_op jit(solution)/shard_map/ppermute | solution.py:360
  37.2 0.6 shard_map.89.late_ref
  37.8 8.4 %collective-permute-done.4.other_ref = f32[288,256]{1,0:T(8,128)S(1)} collective-permute-done((f32[288,256]{1,0:T(8,128)S(1)}, f32[288,256]{1,0:T(8,128)S(1)}, u32[]{:S(2)}, u32[]{:S(2)}) %collective-permute-start.4) | collective-permute-done | bytes 294944 | tf_op jit(solution)/shard_map/ppermute | solution.py:360
  46.6 6.3 %collective-permute-start.7 = (f32[8,256]{1,0:T(8,128)S(1)}, f32[8,256]{1,0:T(8,128)S(1)}, u32[]{:S(2)}, u32[]{:S(2)}) collective-permute-start(f32[8,256]{1,0:T(8,128)S(1)} %get-tuple-element.23.s0), channel_id=1, source_target_pairs={{0,48},{4,52},{8,56},{12,60},{16,32},{20,36},{24,40},{28,44},{32,1... | collective-permute-start | bytes 24584 | tf_op jit(solution)/shard_map/ppermute | solution.py:357
  53.3 0.7 collective-permute-done.7.s3
  54.0 2.4 %collective-permute-done.6.s2 = f32[8,256]{1,0:T(8,128)S(1)} collective-permute-done((f32[8,256]{1,0:T(8,128)S(1)}, f32[8,256]{1,0:T(8,128)S(1)}, u32[]{:S(2)}, u32[]{:S(2)}) %collective-permute-start.6) | collective-permute-done | bytes 8224 | tf_op jit(solution)/shard_map/ppermute | solution.py:357
  56.4 2.8 %collective-permute-start.8 = (bf16[288,256]{1,0:T(8,128)(2,1)S(1)}, bf16[288,256]{1,0:T(8,128)(2,1)S(1)}, u32[]{:S(2)}, u32[]{:S(2)}) collective-permute-start(bf16[288,256]{1,0:T(8,128)(2,1)S(1)} %get-tuple-element.24.keep_ref), channel_id=1, source_target_pairs={{0,1},{1,0},{2,3},{3,2},{4,5},{5,4},{6,7},{7,6},{8,9},{9,8},{10,11... | collective-permute-start | bytes 442376 | tf_op jit(solution)/shard_map/ppermute | solution.py:360
  59.2 1.0 %collective-permute-done.8.other_ref = bf16[288,256]{1,0:T(8,128)(2,1)S(1)} collective-permute-done((bf16[288,256]{1,0:T(8,128)(2,1)S(1)}, bf16[288,256]{1,0:T(8,128)(2,1)S(1)}, u32[]{:S(2)}, u32[]{:S(2)}) %collective-permute-start.8) | collective-permute-done | bytes 147488 | tf_op jit(solution)/shard_map/ppermute | solution.py:360
  60.2 2.7 %shard_map.92 = bf16[1536,128]{1,0:T(8,128)(2,1)} custom-call(bf16[256,3968]{1,0:T(8,128)(2,1)S(1)} %shard_map.87.early_ref, bf16[256,3968]{1,0:T(8,128)(2,1)S(1)} %shard_map.89.late_ref, bf16[288,256]{1,0:T(8,128)(2,1)S(1)} %get-tuple-element.24.keep_ref, bf16[288,256]{1,0:T(8,128)(2,1)S(1)} %collective-permute-done.8.other_ref), custom_call_target="tpu_custom_call" | custom-call | tf_op jit(solution)/shard_map/pallas_call | solution.py:406
  62.9 3.6 %all-to-all-start.1 = ((bf16[16,96,128]{2,1,0:T(8,128)(2,1)}), bf16[16,96,128]{2,1,0:T(8,128)(2,1)S(1)}, u32[]{:S(2)}, u32[]{:S(2)}) async-start(bf16[16,96,128]{2,1,0:T(8,128)(2,1)} %bitcast.8), calls=%async_computation.1 | async-start | bytes 786432 | tf_op jit(solution)/shard_map/all_to_all | solution.py:365
  66.9 0.8 %collective-permute-done.9 = f32[8,256]{1,0:T(8,128)S(1)} collective-permute-done((f32[8,256]{1,0:T(8,128)S(1)}, f32[8,256]{1,0:T(8,128)S(1)}, u32[]{:S(2)}, u32[]{:S(2)}) %collective-permute-start.9) | collective-permute-done | bytes 8224 | tf_op jit(solution)/shard_map/ppermute | solution.py:360
  67.8 0.6 fusion
  68.3 7.6 %all-to-all-done.1 = bf16[16,96,128]{2,1,0:T(8,128)(2,1)S(1)} async-done(((bf16[16,96,128]{2,1,0:T(8,128)(2,1)}), bf16[16,96,128]{2,1,0:T(8,128)(2,1)S(1)}, u32[]{:S(2)}, u32[]{:S(2)}) %all-to-all-start.1) | async-done | bytes 393248 | tf_op jit(solution)/shard_map/all_to_all | solution.py:365
  76.0 1.8 %shard_map.93 = bf16[10,3,384]{2,1,0:T(4,128)(2,1)} custom-call(s32[1]{0:T(128)} %bitcast.first_ref, s32[192]{0:T(256)S(1)} %copy-done, bf16[1536,128]{1,0:T(8,128)(2,1)S(1)} %bitcast.14, f32[1,10]{1,0:T(1,128)S(1)} %bitcast.15), custom_call_target="tpu_custom_call" | custom-call | tf_op jit(solution)/shard_map/pallas_call | solution.py:413
  (19 shorter events, 1.7 us)
Async XLA Ops:
  3.1 12.4 %collective-permute-start.2 = (bf16[16,3968]{1,0:T(8,128)(2,1)}, bf16[16,3968]{1,0:T(8,128)(2,1)S(1)}, u32[]{:S(2)}, u32[]{:S(2)}) collective-permute-start(bf16[16,3968]{1,0:T(8,128)(2,1)} %get-tuple-element.14.f0), channel_id=1, source_target_pairs={{0,48},{4,52},{8,56},{12,60},{16,32},{20,36},{24,40},{28,44},{32,1... | collective-permute-start | bytes 380936 | tf_op jit(solution)/shard_map/ppermute | solution.py:357
  8.3 10.0 %collective-permute-start.1 = (bf16[16,3968]{1,0:T(8,128)(2,1)}, bf16[16,3968]{1,0:T(8,128)(2,1)S(1)}, u32[]{:S(2)}, u32[]{:S(2)}) collective-permute-start(bf16[16,3968]{1,0:T(8,128)(2,1)} %get-tuple-element.14.f0), channel_id=1, source_target_pairs={{0,32},{4,36},{8,40},{12,44},{16,48},{20,52},{24,56},{28,60},{32,0... | collective-permute-start | bytes 380936 | tf_op jit(solution)/shard_map/ppermute | solution.py:357
  8.3 10.0 %collective-permute-start = (bf16[16,3968]{1,0:T(8,128)(2,1)}, bf16[16,3968]{1,0:T(8,128)(2,1)S(1)}, u32[]{:S(2)}, u32[]{:S(2)}) collective-permute-start(bf16[16,3968]{1,0:T(8,128)(2,1)} %get-tuple-element.14.f0), channel_id=1, source_target_pairs={{0,16},{4,20},{8,24},{12,28},{16,0},{20,4},{24,8},{28,12},{32,48},... | collective-permute-start | bytes 380936 | tf_op jit(solution)/shard_map/ppermute | solution.py:357
  8.6 15.3 %all-to-all-start = ((bf16[16,96,128]{2,1,0:T(8,128)(2,1)}), bf16[16,96,128]{2,1,0:T(8,128)(2,1)}, u32[]{:S(2)}, u32[]{:S(2)}) async-start(bf16[16,96,128]{2,1,0:T(8,128)(2,1)} %bitcast.16), calls=%async_computation | async-start | bytes 786432 | tf_op jit(solution)/shard_map/all_to_all | solution.py:365
  18.3 0.9 %copy-start.2 = (bf16[16,3968]{1,0:T(8,128)(2,1)S(1)}, bf16[16,3968]{1,0:T(8,128)(2,1)}, u32[]{:S(2)}) copy-start(bf16[16,3968]{1,0:T(8,128)(2,1)} %get-tuple-element.14.f0) | copy-start | bytes 380932
  27.2 3.9 %collective-permute-start.3 = (f32[288,256]{1,0:T(8,128)S(1)}, f32[288,256]{1,0:T(8,128)S(1)}, u32[]{:S(2)}, u32[]{:S(2)}) collective-permute-start(f32[288,256]{1,0:T(8,128)S(1)} %get-tuple-element.17), channel_id=1, source_target_pairs={{0,1},{1,0},{2,3},{3,2},{4,5},{5,4},{6,7},{7,6},{8,9},{9,8},{10,11... | collective-permute-start | bytes 884744 | tf_op jit(solution)/shard_map/ppermute | solution.py:360
  31.2 15.0 %collective-permute-start.4 = (f32[288,256]{1,0:T(8,128)S(1)}, f32[288,256]{1,0:T(8,128)S(1)}, u32[]{:S(2)}, u32[]{:S(2)}) collective-permute-start(f32[288,256]{1,0:T(8,128)S(1)} %add.20.mine_ref), channel_id=1, source_target_pairs={{0,2},{1,3},{2,0},{3,1},{4,6},{5,7},{6,4},{7,5},{8,10},{9,11},{10,... | collective-permute-start | bytes 884744 | tf_op jit(solution)/shard_map/ppermute | solution.py:360
  46.6 7.4 %collective-permute-start.7 = (f32[8,256]{1,0:T(8,128)S(1)}, f32[8,256]{1,0:T(8,128)S(1)}, u32[]{:S(2)}, u32[]{:S(2)}) collective-permute-start(f32[8,256]{1,0:T(8,128)S(1)} %get-tuple-element.23.s0), channel_id=1, source_target_pairs={{0,48},{4,52},{8,56},{12,60},{16,32},{20,36},{24,40},{28,44},{32,1... | collective-permute-start | bytes 24584 | tf_op jit(solution)/shard_map/ppermute | solution.py:357
  52.9 3.4 %collective-permute-start.6 = (f32[8,256]{1,0:T(8,128)S(1)}, f32[8,256]{1,0:T(8,128)S(1)}, u32[]{:S(2)}, u32[]{:S(2)}) collective-permute-start(f32[8,256]{1,0:T(8,128)S(1)} %get-tuple-element.23.s0), channel_id=1, source_target_pairs={{0,32},{4,36},{8,40},{12,44},{16,48},{20,52},{24,56},{28,60},{32,0... | collective-permute-start | bytes 24584 | tf_op jit(solution)/shard_map/ppermute | solution.py:357
  52.9 3.4 %collective-permute-start.5 = (f32[8,256]{1,0:T(8,128)S(1)}, f32[8,256]{1,0:T(8,128)S(1)}, u32[]{:S(2)}, u32[]{:S(2)}) collective-permute-start(f32[8,256]{1,0:T(8,128)S(1)} %get-tuple-element.23.s0), channel_id=1, source_target_pairs={{0,16},{4,20},{8,24},{12,28},{16,0},{20,4},{24,8},{28,12},{32,48},... | collective-permute-start | bytes 24584 | tf_op jit(solution)/shard_map/ppermute | solution.py:357
  56.4 19.6 %copy-start = (s32[192]{0:T(256)S(1)}, s32[192]{0:T(256)}, u32[]{:S(2)}) copy-start(s32[192]{0:T(256)} %offset_ref.3) | copy-start | bytes 2308
  56.4 19.6 %copy-start.1 = (f32[10]{0:T(128)S(1)}, f32[10]{0:T(128)}, u32[]{:S(2)}) copy-start(f32[10]{0:T(128)} %param.13) | copy-start | bytes 124
  56.4 3.8 %collective-permute-start.8 = (bf16[288,256]{1,0:T(8,128)(2,1)S(1)}, bf16[288,256]{1,0:T(8,128)(2,1)S(1)}, u32[]{:S(2)}, u32[]{:S(2)}) collective-permute-start(bf16[288,256]{1,0:T(8,128)(2,1)S(1)} %get-tuple-element.24.keep_ref), channel_id=1, source_target_pairs={{0,1},{1,0},{2,3},{3,2},{4,5},{5,4},{6,7},{7,6},{8,9},{9,8},{10,11... | collective-permute-start | bytes 442376 | tf_op jit(solution)/shard_map/ppermute | solution.py:360
  62.9 13.1 %all-to-all-start.1 = ((bf16[16,96,128]{2,1,0:T(8,128)(2,1)}), bf16[16,96,128]{2,1,0:T(8,128)(2,1)S(1)}, u32[]{:S(2)}, u32[]{:S(2)}) async-start(bf16[16,96,128]{2,1,0:T(8,128)(2,1)} %bitcast.8), calls=%async_computation.1 | async-start | bytes 786432 | tf_op jit(solution)/shard_map/all_to_all | solution.py:365
  66.5 1.3 %collective-permute-start.9 = (f32[8,256]{1,0:T(8,128)S(1)}, f32[8,256]{1,0:T(8,128)S(1)}, u32[]{:S(2)}, u32[]{:S(2)}) collective-permute-start(f32[8,256]{1,0:T(8,128)S(1)} %get-tuple-element.25), channel_id=1, source_target_pairs={{0,1},{1,0},{2,3},{3,2},{4,5},{5,4},{6,7},{7,6},{8,9},{9,8},{10,11... | collective-permute-start | bytes 24584 | tf_op jit(solution)/shard_map/ppermute | solution.py:360

commit v4 on v3

--- a/solution.py
+++ b/solution.py
@@ -26,6 +26,7 @@
 TILES = WIDE // 128
 SLOT = 32
 CHUNK = OWN_CLASSES * SLOT
+PITCH = CHUNK + 8
 ROWS = TURNS * CLS
 HALF = FINE * OWN_IMAGES * 2
 F32 = jnp.float32
@@ -155,9 +156,6 @@
     image_msg[:, COEF:] = extra.astype(BF16)
 
 
-QUARTER = HALF // 2
-
-
 def turned_on(cur, nxt, steps):
     s = 4 * STEP * steps
     lane = lanes_of(cur.shape)
@@ -172,52 +170,58 @@
             yield slice(here, here + 128), slice(there, there + 128)
 
 
-def early_kernel(place_ref, f0, f1, f2, f3, early_ref):
-    image_refs = (f0, f1, f2, f3)
-    bases = []
-    for k in range(IMG_PEERS):
-        owner = place_ref[0] ^ k
-        half = (owner >> 1) ^ place_ref[1]
-        bases.append(half * QUARTER + (owner & 1) * OWN_IMAGES)
-    for k in range(IMG_PEERS):
-        extra = image_refs[k][:, COEF:]
-        for rho in range(FINE // 2):
-            early_ref[pl.ds(pl.multiple_of(bases[k] + 32 * rho, 16), 16), COEF:] = extra
-
+def fill_fine(images_ref, fine_ref):
+    for rho in range(FINE):
+        fine_ref[32 * rho : 32 * rho + 32, COEF:] = images_ref[:, COEF:]
     for here, there in tile_pairs():
-        for k in range(IMG_PEERS):
-            cur = image_refs[k][:, here]
-            nxt = image_refs[k][:, there]
-            for rho in range(FINE // 2):
-                val = turned_on(cur, nxt, rho) if rho else cur
-                early_ref[pl.ds(pl.multiple_of(bases[k] + 32 * rho, 16), 16), here] = val
-
-
-def make_late(early_ref, late_ref):
-    late_ref[:, COEF:] = early_ref[:, COEF:]
-    for here, there in tile_pairs():
-        late_ref[:, here] = turned_on(early_ref[:, here], early_ref[:, there], FINE // 2)
+        cur, nxt = images_ref[:, here], images_ref[:, there]
+        fine_ref[:32, here] = cur
+        for rho in range(1, FINE):
+            fine_ref[32 * rho : 32 * rho + 32, here] = turned_on(cur, nxt, rho)
+
+
+def early_kernel(place_ref, f0, f1, f2, f3, fine_ref, rest_ref, mine):
+    swapped = place_ref[0] & 1
+    near = (place_ref[0] >> 1) == place_ref[1]
+
+    def put(to_ref, pair):
+        for k, ref in enumerate(pair):
+            at = pl.multiple_of((swapped ^ k) * OWN_IMAGES, 16)
+            to_ref[pl.ds(at, OWN_IMAGES), :] = ref[...]
+
+    @pl.when(near)
+    def _():
+        put(mine, (f0, f1))
+        put(rest_ref, (f2, f3))
+
+    @pl.when(jnp.logical_not(near))
+    def _():
+        put(mine, (f2, f3))
+        put(rest_ref, (f0, f1))
+
+    fill_fine(mine, fine_ref)
 
 
 NT = (((1,), (1,)), ((), ()))
 
 
-def scores_kernel(early_ref, class_ref, keep_ref, send_ref, wide, stack, late):
-    wide[...] = class_ref[...].astype(F32)
+def scores_kernel(
+    fine_ref, rest_ref, class_ref, keep_ref, send_ref, fine_rest, wide, stack
+):
+    for d in range(CLS_PEERS):
+        wide[d * PITCH : d * PITCH + CHUNK, :] = class_ref[d * CHUNK : (d + 1) * CHUNK, :].astype(F32)
     for v in range(TILES):
         for c in range(OWN_CLASSES):
-            tile = wide[pl.ds(c * SLOT + v, CLS_PEERS, stride=CHUNK), :].astype(BF16)
+            tile = wide[pl.ds(c * SLOT + v, CLS_PEERS, stride=PITCH), :].astype(BF16)
             for g in range(TURNS):
                 row = g * CLS + c * CLS_PEERS
                 at = v * 128 if v == TILES - 1 else (v * 128 + g * BLOCK) % COEF
                 stack[row : row + CLS_PEERS, at : at + 128] = tile
-    part = lax.dot_general(stack[...], early_ref[...], NT, preferred_element_type=F32)
-    keep_ref[:, :QUARTER] = part[:, :QUARTER]
-    send_ref[:, :QUARTER] = part[:, QUARTER:]
-    make_late(early_ref, late)
-    part = lax.dot_general(stack[...], late[...], NT, preferred_element_type=F32)
-    keep_ref[:, QUARTER:] = part[:, :QUARTER]
-    send_ref[:, QUARTER:] = part[:, QUARTER:]
+    keep_ref[...] = lax.dot_general(stack[...], fine_ref[...], NT, preferred_element_type=F32)
+    fill_fine(rest_ref, fine_rest)
+    send_ref[...] = lax.dot_general(
+        stack[...], fine_rest[...], NT, preferred_element_type=F32
+    )
 
 
 def over_rotations(op, x):
@@ -248,22 +252,16 @@
     evidence_ref[...] = jnp.broadcast_to(evidence, (8, HALF))
 
 
-def sums_kernel(early_ref, late_ref, keep_ref, other_ref, out_ref, probs, sums, packed):
-    probs[:, :QUARTER] = keep_ref[:, :QUARTER]
-    probs[:, QUARTER:HALF] = other_ref[:, :QUARTER]
-    probs[:, HALF : HALF + QUARTER] = keep_ref[:, QUARTER:]
-    probs[:, HALF + QUARTER :] = other_ref[:, QUARTER:]
+def add_turns(probs_ref, fine_ref, sums, fresh):
     for w in range(0, TURNS, 2):
         span = slice(w * BLOCK, (w + 2) * BLOCK + (128 if w == TURNS - 2 else 0))
-        turned = jnp.dot(
-            probs[:, :HALF], early_ref[:, span], preferred_element_type=F32
-        ) + jnp.dot(probs[:, HALF:], late_ref[:, span], preferred_element_type=F32)
+        turned = jnp.dot(probs_ref[...], fine_ref[:, span], preferred_element_type=F32)
         for b in (w, w + 1):
             for g in range(TURNS):
                 back = (b - g) % TURNS
                 at = slice(back * BLOCK, (back + 1) * BLOCK)
                 term = turned[g * CLS : (g + 1) * CLS, (b - w) * BLOCK : (b - w + 1) * BLOCK]
-                if b == 0:
+                if b == 0 and fresh:
                     sums[:, at] = term
                 else:
                     sums[:, at] += term
@@ -271,6 +269,16 @@
             mass = turned[:CLS, 2 * BLOCK :]
             for g in range(1, TURNS):
                 mass = mass + turned[g * CLS : (g + 1) * CLS, 2 * BLOCK :]
+    return mass
+
+
+def own_sums_kernel(probs_ref, fine_ref, sums_ref):
+    sums_ref[:, COEF:] = add_turns(probs_ref, fine_ref, sums_ref, True)
+
+
+def all_sums_kernel(probs_ref, fine_ref, own_ref, out_ref, sums, packed):
+    sums[...] = own_ref[...]
+    mass = sums[:, COEF:] + add_turns(probs_ref, fine_ref, sums, False)
     mass = mass + pltpu.roll(mass, 118, 1) + pltpu.roll(mass, 98, 1)
     mass = jnp.where(lanes_of((CLS, 128)) < CYC, mass, 0.0)
     hi, mid, lo = three_parts(mass)
@@ -279,11 +287,12 @@
         rows = slice(c * CLS_PEERS, (c + 1) * CLS_PEERS)
         for v in range(SLOT):
             tile = sums[rows, v * 128 : v * 128 + 128] if v < TILES else jnp.zeros((16, 128), F32)
-            packed[pl.ds(c * SLOT + v, CLS_PEERS, stride=CHUNK), :] = tile
-    out_ref[...] = packed[...].astype(BF16)
-
-
-def final_kernel(first_ref, offset_ref, msg_ref, prior_ref, out_ref, summed):
+            packed[pl.ds(c * SLOT + v, CLS_PEERS, stride=PITCH), :] = tile
+    for d in range(CLS_PEERS):
+        out_ref[d * CHUNK : (d + 1) * CHUNK, :] = packed[d * PITCH : d * PITCH + CHUNK, :].astype(BF16)
+
+
+def final_kernel(offset_ref, msg_ref, prior_ref, out_ref, summed):
     total = msg_ref[:CHUNK, :].astype(F32)
     for d in range(1, CLS_PEERS):
         total = total + msg_ref[d * CHUNK : (d + 1) * CHUNK, :].astype(F32)
@@ -320,7 +329,7 @@
         rows.append(jnp.concatenate(vregs, axis=1))
     shifts = []
     for c in range(OWN_CLASSES):
-        off = offset_ref[first_ref[0] + c]
+        off = offset_ref[0, c]
         shifts.append(jnp.where(off == 0, 0, ROW - off))
     turned = turn_classes(jnp.concatenate(rows, axis=0), shifts)
     for p in range(CYC):
@@ -351,6 +360,7 @@
     core = lax.axis_index("shell") % 2
     level = (img // 4) % 4
     first = (img * OWN_CLASSES).astype(jnp.int32).reshape(1)
+    offsets = lax.dynamic_slice_in_dim(class_offset, img * OWN_CLASSES, OWN_CLASSES).reshape(1, -1)
     place = jnp.stack([level, core]).astype(jnp.int32)
 
     def along_peers(x, k):
@@ -376,24 +386,21 @@
     )
     held = [image_msg] + [along_peers(image_msg, k) for k in (1, 2, 3)]
     class_all = over_classes(class_msg)
-    early = call(
+    fine, rest = call(
         early_kernel,
-        shaped((HALF, WIDE), BF16),
-        [],
+        [shaped((HALF, WIDE), BF16), shaped((2 * OWN_IMAGES, WIDE), BF16)],
+        [V((2 * OWN_IMAGES, WIDE), BF16)],
         [S] + [V] * 4,
-        cost=pl.CostEstimate(flops=10**13, transcendentals=0, bytes_accessed=10**10),
+        cost=pl.CostEstimate(flops=5 * 10**10, transcendentals=0, bytes_accessed=10**6),
     )(place, *held)
-    keep, send = call(
+    keep, send, fine_rest = call(
         scores_kernel,
-        [shaped((ROWS, HALF), F32)] * 2,
-        [V((CLS_PEERS * CHUNK, 128), F32), V((ROWS, WIDE), BF16), V((HALF, WIDE), BF16)],
-        [V, V],
-    )(early, class_all)
+        [shaped((ROWS, HALF), F32)] * 2 + [shaped((HALF, WIDE), BF16)],
+        [V((CLS_PEERS * PITCH, 128), F32), V((ROWS, WIDE), BF16)],
+        [V, V, V],
+    )(fine, rest, class_all)
     pair = keep + along_shell(send, 1)
     other = along_shell(pair, 2)
-    early, pair = lax.optimization_barrier((early, pair))
-    late = call(make_late, shaped((HALF, WIDE), BF16), [], [V])(early)
-    late, other = lax.optimization_barrier((late, other))
     scores, stats = call(
         stats_kernel, [shaped((ROWS, HALF), F32), shaped((8, HALF), F32)], [], [V, V]
     )(pair, other)
@@ -403,19 +410,20 @@
     )(scores, *all_stats)
     probs_other = along_shell(probs, 1)
     evidence_other = along_shell(evidence, 1)
+    own_sums = call(own_sums_kernel, shaped((CLS, WIDE), F32), [], [V, V])(probs, fine)
     sums = call(
-        sums_kernel,
+        all_sums_kernel,
         shaped((CLS_PEERS * CHUNK, 128), BF16),
-        [V((ROWS, 2 * HALF), BF16), V((CLS, WIDE), F32), V((CLS_PEERS * CHUNK, 128), F32)],
-        [V] * 4,
-    )(early, late, probs, probs_other)
+        [V((CLS, WIDE), F32), V((CLS_PEERS * PITCH, 128), F32)],
+        [V] * 3,
+    )(probs_other, fine_rest, own_sums)
     own = over_classes(sums)
     new_references = call(
         final_kernel,
         shaped((CYC, OWN_CLASSES, ROW), BF16),
         [V((8 * SLOT, 128), F32)],
-        [S, S, V, V],
-    )(first, class_offset, own, prior_precision.reshape(1, CYC))
+        [V, V, V],
+    )(offsets, own, prior_precision.reshape(1, CYC))
     mine = jnp.where(core == level // 2, evidence[0], evidence_other[0])
     log_evidence = lax.dynamic_slice_in_dim(mine, (level % 2) * OWN_IMAGES, OWN_IMAGES)
     return jnp.transpose(new_references, (1, 0, 2)), log_evidence

time: 78.2 us -> 75 us (0.959)
  Pallas kernels: 12.4 us -> 9.69 us
    pallas_call x4, Pallas kernels: 7.62 us -> 5.45 us  [the longest x1 1.76 us: local(): call(all_sums_kernel, shaped((CLS_PEERS * CHUNK, 128), BF16), [V((CLS, WI...]
  transfers between devices with their start and end apart: 12 -> 12, of which waited for: 9 -> 9; matrix products, arithmetic and copies ran while one was open for 1% -> 1% of each run, Pallas kernels for 2% -> 3%
where the time goes in v4:
time: 75 us; the launch traced here: 74.6 us
  starting transfers between devices  34.4 us (46%)
  waiting for transfers between devices  28.1 us (37%)
  Pallas kernels  9.69 us (13%)
  local copies, waits for them, and re-layouts  0.99 us (1%)
    ppermute x6, starting transfers between devices, along_peers(): return lax.ppermute(x, 'img', [(i, i ^ 4 * k) for i in range(64)])  12.1 us
    ppermute x4, starting transfers between devices, along_shell(): return lax.ppermute(x, 'shell', [(i, i ^ k) for i in range(4)])  12 us
    ppermute x4, waiting for transfers between devices, along_shell(): return lax.ppermute(x, 'shell', [(i, i ^ k) for i in range(4)])  11.1 us
    all_to_all x2, waiting for transfers between devices, over_classes(): return lax.all_to_all(x, 'img', 0, 0, axis_index_groups=groups, tiled=True)  11.1 us
    all_to_all x2, starting transfers between devices, over_classes(): return lax.all_to_all(x, 'img', 0, 0, axis_index_groups=groups, tiled=True)  10.3 us
    ppermute x6, waiting for transfers between devices, along_peers(): return lax.ppermute(x, 'img', [(i, i ^ 4 * k) for i in range(64)])  5.93 us
    pallas_call x1, Pallas kernels, local(): call(prologue_kernel, [shaped((OWN_IMAGES, WIDE), BF16), shaped((CLS_PEER...  2.49 us
    pallas_call x1, Pallas kernels, local(): call(all_sums_kernel, shaped((CLS_PEERS * CHUNK, 128), BF16), [V((CLS, WI...  1.76 us
  transfers between devices with their start and end apart: 12, of which 9 were waited for; matrix products, arithmetic and copies ran while one was open for 1% of the time, Pallas kernels for 3%

profile of v4, /device:TPU:1, one launch (start us, length us, event | category | flops | bytes accessed | tf_op | source)
XLA Modules:
  0.0 74.6 jit_solution(17479344885892583294)
XLA Ops:
  0.6 2.5 %shard_map.86 = (bf16[16,3968]{1,0:T(8,128)(2,1)}, bf16[1536,128]{1,0:T(8,128)(2,1)}) custom-call(s32[1]{0:T(128)} %bitcast.3.first_ref, s32[192]{0:T(256)} %offset_ref.1, s32[16]{0:T(128)} %group_ref.1, f32[10,16,384]{2,1,0:T(8,128)} %bitcast.20, bf16[10,3,384]{2,1,0:T(4,128)(2,1)} %bitcast.21, f32[16,10]{1,0:T(8,128)} %ctf_ref.1, f32[1,10]{1,0:T(1,128)} %bitcast.23), custom_call_target="tpu_custom_call" | custom-call | tf_op jit(solution)/shard_map/pallas_call | solution.py:377
  3.1 5.2 %collective-permute-start.2 = (bf16[16,3968]{1,0:T(8,128)(2,1)}, bf16[16,3968]{1,0:T(8,128)(2,1)S(1)}, u32[]{:S(2)}, u32[]{:S(2)}) collective-permute-start(bf16[16,3968]{1,0:T(8,128)(2,1)} %get-tuple-element.13.f0), channel_id=1, source_target_pairs={{0,48},{4,52},{8,56},{12,60},{16,32},{20,36},{24,40},{28,44},{32,1... | collective-permute-start | bytes 380936 | tf_op jit(solution)/shard_map/ppermute | solution.py:367
  8.6 6.8 %all-to-all-start = ((bf16[16,96,128]{2,1,0:T(8,128)(2,1)}), bf16[16,96,128]{2,1,0:T(8,128)(2,1)S(1)}, u32[]{:S(2)}, u32[]{:S(2)}) async-start(bf16[16,96,128]{2,1,0:T(8,128)(2,1)} %bitcast.19), calls=%async_computation | async-start | bytes 786432 | tf_op jit(solution)/shard_map/all_to_all | solution.py:375
  15.5 2.9 %collective-permute-done.1.f2 = bf16[16,3968]{1,0:T(8,128)(2,1)S(1)} collective-permute-done((bf16[16,3968]{1,0:T(8,128)(2,1)}, bf16[16,3968]{1,0:T(8,128)(2,1)S(1)}, u32[]{:S(2)}, u32[]{:S(2)}) %collective-permute-start.1) | collective-permute-done | bytes 127008 | tf_op jit(solution)/shard_map/ppermute | solution.py:367
  18.3 0.9 %copy-done.1 = bf16[16,3968]{1,0:T(8,128)(2,1)S(1)} copy-done((bf16[16,3968]{1,0:T(8,128)(2,1)S(1)}, bf16[16,3968]{1,0:T(8,128)(2,1)}, u32[]{:S(2)}) %copy-start.1) | copy-done | bytes 127000
  19.2 1.1 %shard_map.87 = (bf16[256,3968]{1,0:T(8,128)(2,1)S(1)}, bf16[32,3968]{1,0:T(8,128)(2,1)S(1)}) custom-call(s32[2]{0:T(128)S(1)} %pad_add_fusion.place_ref, bf16[16,3968]{1,0:T(8,128)(2,1)S(1)} %copy-done.1, bf16[16,3968]{1,0:T(8,128)(2,1)S(1)} %collective-permute-done.f1, bf16[16,3968]{1,0:T(8,128)(2,1)S(1)} %collective-permute-done.1.f2, ...), custom_call_target="tpu_custom_call" | custom-call | flops 49999998976 | bytes 1000000 | tf_op jit(solution)/shard_map/pallas_call | solution.py:389
  20.3 3.4 %all-to-all-done = bf16[16,96,128]{2,1,0:T(8,128)(2,1)S(1)} async-done(((bf16[16,96,128]{2,1,0:T(8,128)(2,1)}), bf16[16,96,128]{2,1,0:T(8,128)(2,1)S(1)}, u32[]{:S(2)}, u32[]{:S(2)}) %all-to-all-start) | async-done | bytes 393248 | tf_op jit(solution)/shard_map/all_to_all | solution.py:375
  23.8 1.8 %shard_map.88 = (f32[288,256]{1,0:T(8,128)S(1)}, f32[288,256]{1,0:T(8,128)S(1)}, bf16[256,3968]{1,0:T(8,128)(2,1)S(1)}) custom-call(bf16[256,3968]{1,0:T(8,128)(2,1)S(1)} %get-tuple-element.14.fine_ref, bf16[32,3968]{1,0:T(8,128)(2,1)S(1)} %get-tuple-element.15.rest_ref, bf16[1536,128]{1,0:T(8,128)(2,1)S(1)} %bitcast.17), custom_call_target="tpu_custom_call" | custom-call | tf_op jit(solution)/shard_map/pallas_call | solution.py:396
  25.5 2.7 %collective-permute-start.3 = (f32[288,256]{1,0:T(8,128)S(1)}, f32[288,256]{1,0:T(8,128)S(1)}, u32[]{:S(2)}, u32[]{:S(2)}) collective-permute-start(f32[288,256]{1,0:T(8,128)S(1)} %get-tuple-element.18), channel_id=1, source_target_pairs={{0,1},{1,0},{2,3},{3,2},{4,5},{5,4},{6,7},{7,6},{8,9},{9,8},{10,11... | collective-permute-start | bytes 884744 | tf_op jit(solution)/shard_map/ppermute | solution.py:370
  28.2 1.2 %collective-permute-done.3 = f32[288,256]{1,0:T(8,128)S(1)} collective-permute-done((f32[288,256]{1,0:T(8,128)S(1)}, f32[288,256]{1,0:T(8,128)S(1)}, u32[]{:S(2)}, u32[]{:S(2)}) %collective-permute-start.3) | collective-permute-done | bytes 294944 | tf_op jit(solution)/shard_map/ppermute | solution.py:370
  29.5 6.1 %collective-permute-start.4 = (f32[288,256]{1,0:T(8,128)S(1)}, f32[288,256]{1,0:T(8,128)S(1)}, u32[]{:S(2)}, u32[]{:S(2)}) collective-permute-start(f32[288,256]{1,0:T(8,128)S(1)} %add.24.mine_ref), channel_id=1, source_target_pairs={{0,2},{1,3},{2,0},{3,1},{4,6},{5,7},{6,4},{7,5},{8,10},{9,11},{10,... | collective-permute-start | bytes 884744 | tf_op jit(solution)/shard_map/ppermute | solution.py:370
  35.6 9.0 %collective-permute-done.4.other_ref = f32[288,256]{1,0:T(8,128)S(1)} collective-permute-done((f32[288,256]{1,0:T(8,128)S(1)}, f32[288,256]{1,0:T(8,128)S(1)}, u32[]{:S(2)}, u32[]{:S(2)}) %collective-permute-start.4) | collective-permute-done | bytes 294944 | tf_op jit(solution)/shard_map/ppermute | solution.py:370
  44.9 6.3 %collective-permute-start.7 = (f32[8,256]{1,0:T(8,128)S(1)}, f32[8,256]{1,0:T(8,128)S(1)}, u32[]{:S(2)}, u32[]{:S(2)}) collective-permute-start(f32[8,256]{1,0:T(8,128)S(1)} %get-tuple-element.20.s0), channel_id=1, source_target_pairs={{0,48},{4,52},{8,56},{12,60},{16,32},{20,36},{24,40},{28,44},{32,1... | collective-permute-start | bytes 24584 | tf_op jit(solution)/shard_map/ppermute | solution.py:367
  51.6 0.7 collective-permute-done.7.s3
  52.3 2.4 %collective-permute-done.6.s2 = f32[8,256]{1,0:T(8,128)S(1)} collective-permute-done((f32[8,256]{1,0:T(8,128)S(1)}, f32[8,256]{1,0:T(8,128)S(1)}, u32[]{:S(2)}, u32[]{:S(2)}) %collective-permute-start.6) | collective-permute-done | bytes 8224 | tf_op jit(solution)/shard_map/ppermute | solution.py:367
  54.7 2.8 %collective-permute-start.8 = (bf16[288,256]{1,0:T(8,128)(2,1)S(1)}, bf16[288,256]{1,0:T(8,128)(2,1)S(1)}, u32[]{:S(2)}, u32[]{:S(2)}) collective-permute-start(bf16[288,256]{1,0:T(8,128)(2,1)S(1)} %get-tuple-element.21.probs_ref), channel_id=1, source_target_pairs={{0,1},{1,0},{2,3},{3,2},{4,5},{5,4},{6,7},{7,6},{8,9},{9,8},{10,11... | collective-permute-start | bytes 442376 | tf_op jit(solution)/shard_map/ppermute | solution.py:370
  57.5 0.8 %shard_map.91.own_ref = f32[48,3968]{1,0:T(8,128)S(1)} custom-call(bf16[288,256]{1,0:T(8,128)(2,1)S(1)} %get-tuple-element.21.probs_ref, bf16[256,3968]{1,0:T(8,128)(2,1)S(1)} %get-tuple-element.14.fine_ref), custom_call_target="tpu_custom_call" | custom-call | tf_op jit(solution)/shard_map/pallas_call | solution.py:413
  58.5 1.8 %shard_map.92 = bf16[1536,128]{1,0:T(8,128)(2,1)} custom-call(bf16[288,256]{1,0:T(8,128)(2,1)S(1)} %collective-permute-done.8.probs_ref, bf16[256,3968]{1,0:T(8,128)(2,1)S(1)} %get-tuple-element.22.fine_ref, f32[48,3968]{1,0:T(8,128)S(1)} %shard_map.91.own_ref), custom_call_target="tpu_custom_call" | custom-call | tf_op jit(solution)/shard_map/pallas_call | solution.py:414
  60.3 3.6 %all-to-all-start.1 = ((bf16[16,96,128]{2,1,0:T(8,128)(2,1)}), bf16[16,96,128]{2,1,0:T(8,128)(2,1)S(1)}, u32[]{:S(2)}, u32[]{:S(2)}) async-start(bf16[16,96,128]{2,1,0:T(8,128)(2,1)} %bitcast.9), calls=%async_computation.1 | async-start | bytes 786432 | tf_op jit(solution)/shard_map/all_to_all | solution.py:375
  63.8 0.5 collective-permute-start.9
  64.4 0.7 %collective-permute-done.9 = f32[8,256]{1,0:T(8,128)S(1)} collective-permute-done((f32[8,256]{1,0:T(8,128)S(1)}, f32[8,256]{1,0:T(8,128)S(1)}, u32[]{:S(2)}, u32[]{:S(2)}) %collective-permute-start.9) | collective-permute-done | bytes 8224 | tf_op jit(solution)/shard_map/ppermute | solution.py:370
  65.1 0.6 fusion
  65.7 7.6 %all-to-all-done.1 = bf16[16,96,128]{2,1,0:T(8,128)(2,1)S(1)} async-done(((bf16[16,96,128]{2,1,0:T(8,128)(2,1)}), bf16[16,96,128]{2,1,0:T(8,128)(2,1)S(1)}, u32[]{:S(2)}, u32[]{:S(2)}) %all-to-all-start.1) | async-done | bytes 393248 | tf_op jit(solution)/shard_map/all_to_all | solution.py:375
  73.3 1.3 %shard_map.93 = bf16[10,3,384]{2,1,0:T(4,128)(2,1)} custom-call(s32[1,3]{1,0:T(1,128)S(1)} %dynamic-slice_bitcast_fusion.offset_ref, bf16[1536,128]{1,0:T(8,128)(2,1)S(1)} %bitcast.16, f32[1,10]{1,0:T(1,128)S(1)} %bitcast.18), custom_call_target="tpu_custom_call" | custom-call | tf_op jit(solution)/shard_map/pallas_call | solution.py:421
  (20 shorter events, 1.5 us)
Async XLA Ops:
  3.1 12.3 %collective-permute-start.2 = (bf16[16,3968]{1,0:T(8,128)(2,1)}, bf16[16,3968]{1,0:T(8,128)(2,1)S(1)}, u32[]{:S(2)}, u32[]{:S(2)}) collective-permute-start(bf16[16,3968]{1,0:T(8,128)(2,1)} %get-tuple-element.13.f0), channel_id=1, source_target_pairs={{0,48},{4,52},{8,56},{12,60},{16,32},{20,36},{24,40},{28,44},{32,1... | collective-permute-start | bytes 380936 | tf_op jit(solution)/shard_map/ppermute | solution.py:367
  8.3 10.0 %collective-permute-start.1 = (bf16[16,3968]{1,0:T(8,128)(2,1)}, bf16[16,3968]{1,0:T(8,128)(2,1)S(1)}, u32[]{:S(2)}, u32[]{:S(2)}) collective-permute-start(bf16[16,3968]{1,0:T(8,128)(2,1)} %get-tuple-element.13.f0), channel_id=1, source_target_pairs={{0,32},{4,36},{8,40},{12,44},{16,48},{20,52},{24,56},{28,60},{32,0... | collective-permute-start | bytes 380936 | tf_op jit(solution)/shard_map/ppermute | solution.py:367
  8.3 10.0 %collective-permute-start = (bf16[16,3968]{1,0:T(8,128)(2,1)}, bf16[16,3968]{1,0:T(8,128)(2,1)S(1)}, u32[]{:S(2)}, u32[]{:S(2)}) collective-permute-start(bf16[16,3968]{1,0:T(8,128)(2,1)} %get-tuple-element.13.f0), channel_id=1, source_target_pairs={{0,16},{4,20},{8,24},{12,28},{16,0},{20,4},{24,8},{28,12},{32,48},... | collective-permute-start | bytes 380936 | tf_op jit(solution)/shard_map/ppermute | solution.py:367
  8.6 15.2 %all-to-all-start = ((bf16[16,96,128]{2,1,0:T(8,128)(2,1)}), bf16[16,96,128]{2,1,0:T(8,128)(2,1)S(1)}, u32[]{:S(2)}, u32[]{:S(2)}) async-start(bf16[16,96,128]{2,1,0:T(8,128)(2,1)} %bitcast.19), calls=%async_computation | async-start | bytes 786432 | tf_op jit(solution)/shard_map/all_to_all | solution.py:375
  18.3 0.9 %copy-start.1 = (bf16[16,3968]{1,0:T(8,128)(2,1)S(1)}, bf16[16,3968]{1,0:T(8,128)(2,1)}, u32[]{:S(2)}) copy-start(bf16[16,3968]{1,0:T(8,128)(2,1)} %get-tuple-element.13.f0) | copy-start | bytes 380932
  25.5 3.9 %collective-permute-start.3 = (f32[288,256]{1,0:T(8,128)S(1)}, f32[288,256]{1,0:T(8,128)S(1)}, u32[]{:S(2)}, u32[]{:S(2)}) collective-permute-start(f32[288,256]{1,0:T(8,128)S(1)} %get-tuple-element.18), channel_id=1, source_target_pairs={{0,1},{1,0},{2,3},{3,2},{4,5},{5,4},{6,7},{7,6},{8,9},{9,8},{10,11... | collective-permute-start | bytes 884744 | tf_op jit(solution)/shard_map/ppermute | solution.py:370
  29.5 15.0 %collective-permute-start.4 = (f32[288,256]{1,0:T(8,128)S(1)}, f32[288,256]{1,0:T(8,128)S(1)}, u32[]{:S(2)}, u32[]{:S(2)}) collective-permute-start(f32[288,256]{1,0:T(8,128)S(1)} %add.24.mine_ref), channel_id=1, source_target_pairs={{0,2},{1,3},{2,0},{3,1},{4,6},{5,7},{6,4},{7,5},{8,10},{9,11},{10,... | collective-permute-start | bytes 884744 | tf_op jit(solution)/shard_map/ppermute | solution.py:370
  44.9 7.4 %collective-permute-start.7 = (f32[8,256]{1,0:T(8,128)S(1)}, f32[8,256]{1,0:T(8,128)S(1)}, u32[]{:S(2)}, u32[]{:S(2)}) collective-permute-start(f32[8,256]{1,0:T(8,128)S(1)} %get-tuple-element.20.s0), channel_id=1, source_target_pairs={{0,48},{4,52},{8,56},{12,60},{16,32},{20,36},{24,40},{28,44},{32,1... | collective-permute-start | bytes 24584 | tf_op jit(solution)/shard_map/ppermute | solution.py:367
  51.2 3.4 %collective-permute-start.6 = (f32[8,256]{1,0:T(8,128)S(1)}, f32[8,256]{1,0:T(8,128)S(1)}, u32[]{:S(2)}, u32[]{:S(2)}) collective-permute-start(f32[8,256]{1,0:T(8,128)S(1)} %get-tuple-element.20.s0), channel_id=1, source_target_pairs={{0,32},{4,36},{8,40},{12,44},{16,48},{20,52},{24,56},{28,60},{32,0... | collective-permute-start | bytes 24584 | tf_op jit(solution)/shard_map/ppermute | solution.py:367
  51.2 3.4 %collective-permute-start.5 = (f32[8,256]{1,0:T(8,128)S(1)}, f32[8,256]{1,0:T(8,128)S(1)}, u32[]{:S(2)}, u32[]{:S(2)}) collective-permute-start(f32[8,256]{1,0:T(8,128)S(1)} %get-tuple-element.20.s0), channel_id=1, source_target_pairs={{0,16},{4,20},{8,24},{12,28},{16,0},{20,4},{24,8},{28,12},{32,48},... | collective-permute-start | bytes 24584 | tf_op jit(solution)/shard_map/ppermute | solution.py:367
  54.7 3.8 %collective-permute-start.8 = (bf16[288,256]{1,0:T(8,128)(2,1)S(1)}, bf16[288,256]{1,0:T(8,128)(2,1)S(1)}, u32[]{:S(2)}, u32[]{:S(2)}) collective-permute-start(bf16[288,256]{1,0:T(8,128)(2,1)S(1)} %get-tuple-element.21.probs_ref), channel_id=1, source_target_pairs={{0,1},{1,0},{2,3},{3,2},{4,5},{5,4},{6,7},{7,6},{8,9},{9,8},{10,11... | collective-permute-start | bytes 442376 | tf_op jit(solution)/shard_map/ppermute | solution.py:370
  58.5 5.8 %copy-start.2 = (s32[192]{0:T(256)S(1)}, s32[192]{0:T(256)}, u32[]{:S(2)}) copy-start(s32[192]{0:T(256)} %offset_ref.1) | copy-start | bytes 2308
  58.5 14.8 %copy-start = (f32[10]{0:T(128)S(1)}, f32[10]{0:T(128)}, u32[]{:S(2)}) copy-start(f32[10]{0:T(128)} %param.13) | copy-start | bytes 124
  60.3 13.1 %all-to-all-start.1 = ((bf16[16,96,128]{2,1,0:T(8,128)(2,1)}), bf16[16,96,128]{2,1,0:T(8,128)(2,1)S(1)}, u32[]{:S(2)}, u32[]{:S(2)}) async-start(bf16[16,96,128]{2,1,0:T(8,128)(2,1)} %bitcast.9), calls=%async_computation.1 | async-start | bytes 786432 | tf_op jit(solution)/shard_map/all_to_all | solution.py:375
  63.8 1.3 %collective-permute-start.9 = (f32[8,256]{1,0:T(8,128)S(1)}, f32[8,256]{1,0:T(8,128)S(1)}, u32[]{:S(2)}, u32[]{:S(2)}) collective-permute-start(f32[8,256]{1,0:T(8,128)S(1)} %get-tuple-element.23), channel_id=1, source_target_pairs={{0,1},{1,0},{2,3},{3,2},{4,5},{5,4},{6,7},{7,6},{8,9},{9,8},{10,11... | collective-permute-start | bytes 24584 | tf_op jit(solution)/shard_map/ppermute | solution.py:370

commit v5 on v4

--- a/solution.py
+++ b/solution.py
@@ -180,34 +180,34 @@
             fine_ref[32 * rho : 32 * rho + 32, here] = turned_on(cur, nxt, rho)
 
 
-def early_kernel(place_ref, f0, f1, f2, f3, fine_ref, rest_ref, mine):
-    swapped = place_ref[0] & 1
-    near = (place_ref[0] >> 1) == place_ref[1]
-
-    def put(to_ref, pair):
-        for k, ref in enumerate(pair):
-            at = pl.multiple_of((swapped ^ k) * OWN_IMAGES, 16)
-            to_ref[pl.ds(at, OWN_IMAGES), :] = ref[...]
-
-    @pl.when(near)
-    def _():
-        put(mine, (f0, f1))
-        put(rest_ref, (f2, f3))
-
-    @pl.when(jnp.logical_not(near))
-    def _():
-        put(mine, (f2, f3))
-        put(rest_ref, (f0, f1))
-
-    fill_fine(mine, fine_ref)
+def place():
+    return lax.axis_index("img") // IMG_PEERS % IMG_PEERS, lax.axis_index("shell") % 2
+
+
+def gather_pair(pair, to_ref):
+    level, _ = place()
+    for k, ref in enumerate(pair):
+        at = pl.multiple_of(((level & 1) ^ k) * OWN_IMAGES, 16)
+        to_ref[pl.ds(at, OWN_IMAGES), :] = ref[...]
+
+
+def early_kernel(f2, f3, fine_ref, pair):
+    gather_pair((f2, f3), pair)
+    fill_fine(pair, fine_ref)
+
+
+def is_near():
+    level, core = place()
+    return (level >> 1) == core
 
 
 NT = (((1,), (1,)), ((), ()))
 
 
 def scores_kernel(
-    fine_ref, rest_ref, class_ref, keep_ref, send_ref, fine_rest, wide, stack
+    far_ref, f0, f1, class_ref, keep_ref, send_ref, fine_ref, pair, wide, stack, part
 ):
+    gather_pair((f0, f1), pair)
     for d in range(CLS_PEERS):
         wide[d * PITCH : d * PITCH + CHUNK, :] = class_ref[d * CHUNK : (d + 1) * CHUNK, :].astype(F32)
     for v in range(TILES):
@@ -217,11 +217,14 @@
                 row = g * CLS + c * CLS_PEERS
                 at = v * 128 if v == TILES - 1 else (v * 128 + g * BLOCK) % COEF
                 stack[row : row + CLS_PEERS, at : at + 128] = tile
-    keep_ref[...] = lax.dot_general(stack[...], fine_ref[...], NT, preferred_element_type=F32)
-    fill_fine(rest_ref, fine_rest)
-    send_ref[...] = lax.dot_general(
-        stack[...], fine_rest[...], NT, preferred_element_type=F32
-    )
+    part[...] = lax.dot_general(stack[...], far_ref[...], NT, preferred_element_type=F32)
+    fill_fine(pair, fine_ref.at[0])
+    fine_ref[1] = far_ref[...]
+    last = lax.dot_general(stack[...], fine_ref[0], NT, preferred_element_type=F32)
+    first = part[...]
+    near = is_near()
+    keep_ref[...] = jnp.where(near, last, first)
+    send_ref[...] = jnp.where(near, first, last)
 
 
 def over_rotations(op, x):
@@ -273,12 +276,14 @@
 
 
 def own_sums_kernel(probs_ref, fine_ref, sums_ref):
-    sums_ref[:, COEF:] = add_turns(probs_ref, fine_ref, sums_ref, True)
+    mine = fine_ref.at[jnp.where(is_near(), 0, 1)]
+    sums_ref[:, COEF:] = add_turns(probs_ref, mine, sums_ref, True)
 
 
 def all_sums_kernel(probs_ref, fine_ref, own_ref, out_ref, sums, packed):
     sums[...] = own_ref[...]
-    mass = sums[:, COEF:] + add_turns(probs_ref, fine_ref, sums, False)
+    rest = fine_ref.at[jnp.where(is_near(), 1, 0)]
+    mass = sums[:, COEF:] + add_turns(probs_ref, rest, sums, False)
     mass = mass + pltpu.roll(mass, 118, 1) + pltpu.roll(mass, 98, 1)
     mass = jnp.where(lanes_of((CLS, 128)) < CYC, mass, 0.0)
     hi, mid, lo = three_parts(mass)
@@ -357,11 +362,9 @@
 
 def local(images, references, class_offset, ctf_group, ctf, noise_power, prior_precision):
     img = lax.axis_index("img")
-    core = lax.axis_index("shell") % 2
-    level = (img // 4) % 4
+    level, core = place()
     first = (img * OWN_CLASSES).astype(jnp.int32).reshape(1)
     offsets = lax.dynamic_slice_in_dim(class_offset, img * OWN_CLASSES, OWN_CLASSES).reshape(1, -1)
-    place = jnp.stack([level, core]).astype(jnp.int32)
 
     def along_peers(x, k):
         return lax.ppermute(x, "img", [(i, i ^ (4 * k)) for i in range(64)])
@@ -386,19 +389,22 @@
     )
     held = [image_msg] + [along_peers(image_msg, k) for k in (1, 2, 3)]
     class_all = over_classes(class_msg)
-    fine, rest = call(
+    far = call(
         early_kernel,
-        [shaped((HALF, WIDE), BF16), shaped((2 * OWN_IMAGES, WIDE), BF16)],
+        shaped((HALF, WIDE), BF16),
         [V((2 * OWN_IMAGES, WIDE), BF16)],
-        [S] + [V] * 4,
-        cost=pl.CostEstimate(flops=5 * 10**10, transcendentals=0, bytes_accessed=10**6),
-    )(place, *held)
-    keep, send, fine_rest = call(
+        [V, V],
+        cost=pl.CostEstimate(flops=26 * 10**8, transcendentals=0, bytes_accessed=10**6),
+    )(held[2], held[3])
+    keep, send, fine = call(
         scores_kernel,
-        [shaped((ROWS, HALF), F32)] * 2 + [shaped((HALF, WIDE), BF16)],
-        [V((CLS_PEERS * PITCH, 128), F32), V((ROWS, WIDE), BF16)],
-        [V, V, V],
-    )(fine, rest, class_all)
+        [shaped((ROWS, HALF), F32)] * 2 + [shaped((2, HALF, WIDE), BF16)],
+        [
+            V((2 * OWN_IMAGES, WIDE), BF16), V((CLS_PEERS * PITCH, 128), F32),
+            V((ROWS, WIDE), BF16), V((ROWS, HALF), F32),
+        ],
+        [V] * 4,
+    )(far, held[0], held[1], class_all)
     pair = keep + along_shell(send, 1)
     other = along_shell(pair, 2)
     scores, stats = call(
@@ -416,7 +422,7 @@
         shaped((CLS_PEERS * CHUNK, 128), BF16),
         [V((CLS, WIDE), F32), V((CLS_PEERS * PITCH, 128), F32)],
         [V] * 3,
-    )(probs_other, fine_rest, own_sums)
+    )(probs_other, fine, own_sums)
     own = over_classes(sums)
     new_references = call(
         final_kernel,

time: 75 us -> 73.4 us (0.979)
  local copies, waits for them, and re-layouts: 0.99 us -> 0.09 us
    ppermute x6, starting transfers between devices: 12.1 us -> 14.9 us  [along_peers(): return lax.ppermute(x, 'img', [(i, i ^ 4 * k) for i in range(64)])]
    ppermute x4, starting transfers between devices: 12 us -> 9.47 us  [along_shell(): return lax.ppermute(x, 'shell', [(i, i ^ k) for i in range(4)])]
    ppermute x6, waiting for transfers between devices: 5.93 us -> 7.71 us  [along_peers(): return lax.ppermute(x, 'img', [(i, i ^ 4 * k) for i in range(64)])]
    ppermute x4, waiting for transfers between devices: 11.1 us -> 9.85 us  [along_shell(): return lax.ppermute(x, 'shell', [(i, i ^ k) for i in range(4)])]
    all_to_all x2, waiting for transfers between devices: 11.1 us -> 10.1 us  [over_classes(): return lax.all_to_all(x, 'img', 0, 0, axis_index_groups=groups, tiled=True)]
    unnamed x6, local copies, waits for them, and re-layouts: 0.91 us -> 0.02 us
  transfers between devices with their start and end apart: 12 -> 12, of which waited for: 9 -> 10; matrix products, arithmetic and copies ran while one was open for 1% -> 1% of each run, Pallas kernels for 3% -> 2%
where the time goes in v5:
time: 73.4 us; the launch traced here: 73.1 us
  starting transfers between devices  34.7 us (47%)
  waiting for transfers between devices  27.7 us (38%)
  Pallas kernels  9.27 us (13%)
  between operations  0.74 us (1%)
    ppermute x6, starting transfers between devices, along_peers(): return lax.ppermute(x, 'img', [(i, i ^ 4 * k) for i in range(64)])  14.9 us
    all_to_all x2, starting transfers between devices, over_classes(): return lax.all_to_all(x, 'img', 0, 0, axis_index_groups=groups, tiled=True)  10.3 us
    all_to_all x2, waiting for transfers between devices, over_classes(): return lax.all_to_all(x, 'img', 0, 0, axis_index_groups=groups, tiled=True)  10.1 us
    ppermute x4, waiting for transfers between devices, along_shell(): return lax.ppermute(x, 'shell', [(i, i ^ k) for i in range(4)])  9.85 us
    ppermute x4, starting transfers between devices, along_shell(): return lax.ppermute(x, 'shell', [(i, i ^ k) for i in range(4)])  9.47 us
    ppermute x6, waiting for transfers between devices, along_peers(): return lax.ppermute(x, 'img', [(i, i ^ 4 * k) for i in range(64)])  7.71 us
    pallas_call x1, Pallas kernels, local(): call(prologue_kernel, [shaped((OWN_IMAGES, WIDE), BF16), shaped((CLS_PEER...  2.47 us
    pallas_call x1, Pallas kernels, local(): call(scores_kernel, [shaped((ROWS, HALF), F32)] * 2 + [shaped((2, HALF, W...  1.94 us
  transfers between devices with their start and end apart: 12, of which 10 were waited for; matrix products, arithmetic and copies ran while one was open for 1% of the time, Pallas kernels for 2%

profile of v5, /device:TPU:1, one launch (start us, length us, event | category | flops | bytes accessed | tf_op | source)
XLA Modules:
  0.0 73.1 jit_solution(3051141707817111579)
XLA Ops:
  0.6 2.5 %shard_map.86 = (bf16[16,3968]{1,0:T(8,128)(2,1)}, bf16[1536,128]{1,0:T(8,128)(2,1)}) custom-call(s32[1]{0:T(128)} %bitcast.1.first_ref, s32[192]{0:T(256)} %offset_ref.1, s32[16]{0:T(128)} %group_ref.1, f32[10,16,384]{2,1,0:T(8,128)} %bitcast.18, bf16[10,3,384]{2,1,0:T(4,128)(2,1)} %bitcast.19, f32[16,10]{1,0:T(8,128)} %ctf_ref.1, f32[1,10]{1,0:T(1,128)} %bitcast.21), custom_call_target="tpu_custom_call" | custom-call | tf_op jit(solution)/shard_map/pallas_call | solution.py:380
  3.1 5.2 %collective-permute-start.1 = (bf16[16,3968]{1,0:T(8,128)(2,1)}, bf16[16,3968]{1,0:T(8,128)(2,1)S(1)}, u32[]{:S(2)}, u32[]{:S(2)}) collective-permute-start(bf16[16,3968]{1,0:T(8,128)(2,1)} %get-tuple-element.11.f0), channel_id=1, source_target_pairs={{0,48},{4,52},{8,56},{12,60},{16,32},{20,36},{24,40},{28,44},{32,1... | collective-permute-start | bytes 380936 | tf_op jit(solution)/shard_map/ppermute | solution.py:370
  8.3 6.8 %all-to-all-start = ((bf16[16,96,128]{2,1,0:T(8,128)(2,1)}), bf16[16,96,128]{2,1,0:T(8,128)(2,1)S(1)}, u32[]{:S(2)}, u32[]{:S(2)}) async-start(bf16[16,96,128]{2,1,0:T(8,128)(2,1)} %bitcast.17), calls=%async_computation | async-start | bytes 786432 | tf_op jit(solution)/shard_map/all_to_all | solution.py:378
  15.4 2.9 %collective-permute-done.f2 = bf16[16,3968]{1,0:T(8,128)(2,1)S(1)} collective-permute-done((bf16[16,3968]{1,0:T(8,128)(2,1)}, bf16[16,3968]{1,0:T(8,128)(2,1)S(1)}, u32[]{:S(2)}, u32[]{:S(2)}) %collective-permute-start) | collective-permute-done | bytes 127008 | tf_op jit(solution)/shard_map/ppermute | solution.py:370
  18.3 0.5 shard_map.87.far_ref
  18.9 2.6 %collective-permute-done.2.f1 = bf16[16,3968]{1,0:T(8,128)(2,1)S(1)} collective-permute-done((bf16[16,3968]{1,0:T(8,128)(2,1)}, bf16[16,3968]{1,0:T(8,128)(2,1)S(1)}, u32[]{:S(2)}, u32[]{:S(2)}) %collective-permute-start.2) | collective-permute-done | bytes 127008 | tf_op jit(solution)/shard_map/ppermute | solution.py:370
  21.4 2.5 %all-to-all-done = bf16[16,96,128]{2,1,0:T(8,128)(2,1)S(1)} async-done(((bf16[16,96,128]{2,1,0:T(8,128)(2,1)}), bf16[16,96,128]{2,1,0:T(8,128)(2,1)S(1)}, u32[]{:S(2)}, u32[]{:S(2)}) %all-to-all-start) | async-done | bytes 393248 | tf_op jit(solution)/shard_map/all_to_all | solution.py:378
  23.9 1.9 %shard_map.88 = (f32[288,256]{1,0:T(8,128)S(1)}, f32[288,256]{1,0:T(8,128)S(1)}, bf16[2,256,3968]{2,1,0:T(8,128)(2,1)S(1)}) custom-call(bf16[256,3968]{1,0:T(8,128)(2,1)S(1)} %shard_map.87.far_ref, bf16[16,3968]{1,0:T(8,128)(2,1)S(1)} %copy-done, bf16[16,3968]{1,0:T(8,128)(2,1)S(1)} %collective-permute-done.2.f1, bf16[1536,128]{1,0:T(8,128)(2,1)S(1)} %bitcast.15), custom_call_target="tpu_custom_call" | custom-call | tf_op jit(solution)/shard_map/pallas_call | solution.py:399
  25.9 2.2 %collective-permute-start.3 = (f32[288,256]{1,0:T(8,128)S(1)}, f32[288,256]{1,0:T(8,128)S(1)}, u32[]{:S(2)}, u32[]{:S(2)}) collective-permute-start(f32[288,256]{1,0:T(8,128)S(1)} %get-tuple-element.14), channel_id=1, source_target_pairs={{0,1},{1,0},{2,3},{3,2},{4,5},{5,4},{6,7},{7,6},{8,9},{9,8},{10,11... | collective-permute-start | bytes 884744 | tf_op jit(solution)/shard_map/ppermute | solution.py:373
  28.1 1.2 %collective-permute-done.3 = f32[288,256]{1,0:T(8,128)S(1)} collective-permute-done((f32[288,256]{1,0:T(8,128)S(1)}, f32[288,256]{1,0:T(8,128)S(1)}, u32[]{:S(2)}, u32[]{:S(2)}) %collective-permute-start.3) | collective-permute-done | bytes 294944 | tf_op jit(solution)/shard_map/ppermute | solution.py:373
  29.4 4.6 %collective-permute-start.4 = (f32[288,256]{1,0:T(8,128)S(1)}, f32[288,256]{1,0:T(8,128)S(1)}, u32[]{:S(2)}, u32[]{:S(2)}) collective-permute-start(f32[288,256]{1,0:T(8,128)S(1)} %add.22.mine_ref), channel_id=1, source_target_pairs={{0,2},{1,3},{2,0},{3,1},{4,6},{5,7},{6,4},{7,5},{8,10},{9,11},{10,... | collective-permute-start | bytes 884744 | tf_op jit(solution)/shard_map/ppermute | solution.py:373
  33.9 7.7 %collective-permute-done.4.other_ref = f32[288,256]{1,0:T(8,128)S(1)} collective-permute-done((f32[288,256]{1,0:T(8,128)S(1)}, f32[288,256]{1,0:T(8,128)S(1)}, u32[]{:S(2)}, u32[]{:S(2)}) %collective-permute-start.4) | collective-permute-done | bytes 294944 | tf_op jit(solution)/shard_map/ppermute | solution.py:373
  42.1 1.1 %collective-permute-start.7 = (f32[8,256]{1,0:T(8,128)S(1)}, f32[8,256]{1,0:T(8,128)S(1)}, u32[]{:S(2)}, u32[]{:S(2)}) collective-permute-start(f32[8,256]{1,0:T(8,128)S(1)} %get-tuple-element.16.s0), channel_id=1, source_target_pairs={{0,48},{4,52},{8,56},{12,60},{16,32},{20,36},{24,40},{28,44},{32,1... | collective-permute-start | bytes 24584 | tf_op jit(solution)/shard_map/ppermute | solution.py:370
  43.2 8.0 %collective-permute-start.6 = (f32[8,256]{1,0:T(8,128)S(1)}, f32[8,256]{1,0:T(8,128)S(1)}, u32[]{:S(2)}, u32[]{:S(2)}) collective-permute-start(f32[8,256]{1,0:T(8,128)S(1)} %get-tuple-element.16.s0), channel_id=1, source_target_pairs={{0,32},{4,36},{8,40},{12,44},{16,48},{20,52},{24,56},{28,60},{32,0... | collective-permute-start | bytes 24584 | tf_op jit(solution)/shard_map/ppermute | solution.py:370
  51.4 0.8 %collective-permute-done.6.s2 = f32[8,256]{1,0:T(8,128)S(1)} collective-permute-done((f32[8,256]{1,0:T(8,128)S(1)}, f32[8,256]{1,0:T(8,128)S(1)}, u32[]{:S(2)}, u32[]{:S(2)}) %collective-permute-start.6) | collective-permute-done | bytes 8224 | tf_op jit(solution)/shard_map/ppermute | solution.py:370
  52.3 1.4 %collective-permute-done.5.s1 = f32[8,256]{1,0:T(8,128)S(1)} collective-permute-done((f32[8,256]{1,0:T(8,128)S(1)}, f32[8,256]{1,0:T(8,128)S(1)}, u32[]{:S(2)}, u32[]{:S(2)}) %collective-permute-start.5) | collective-permute-done | bytes 8224 | tf_op jit(solution)/shard_map/ppermute | solution.py:370
  53.8 2.2 %collective-permute-start.8 = (bf16[288,256]{1,0:T(8,128)(2,1)S(1)}, bf16[288,256]{1,0:T(8,128)(2,1)S(1)}, u32[]{:S(2)}, u32[]{:S(2)}) collective-permute-start(bf16[288,256]{1,0:T(8,128)(2,1)S(1)} %get-tuple-element.17.probs_ref), channel_id=1, source_target_pairs={{0,1},{1,0},{2,3},{3,2},{4,5},{5,4},{6,7},{7,6},{8,9},{9,8},{10,11... | collective-permute-start | bytes 442376 | tf_op jit(solution)/shard_map/ppermute | solution.py:373
  56.0 0.8 %shard_map.91.own_ref = f32[48,3968]{1,0:T(8,128)S(1)} custom-call(bf16[288,256]{1,0:T(8,128)(2,1)S(1)} %get-tuple-element.17.probs_ref, bf16[2,256,3968]{2,1,0:T(8,128)(2,1)S(1)} %get-tuple-element.18.fine_ref), custom_call_target="tpu_custom_call" | custom-call | tf_op jit(solution)/shard_map/pallas_call | solution.py:419
  57.0 1.7 %shard_map.92 = bf16[1536,128]{1,0:T(8,128)(2,1)} custom-call(bf16[288,256]{1,0:T(8,128)(2,1)S(1)} %collective-permute-done.8.probs_ref, bf16[2,256,3968]{2,1,0:T(8,128)(2,1)S(1)} %get-tuple-element.18.fine_ref, f32[48,3968]{1,0:T(8,128)S(1)} %shard_map.91.own_ref), custom_call_target="tpu_custom_call" | custom-call | tf_op jit(solution)/shard_map/pallas_call | solution.py:420
  58.7 3.6 %all-to-all-start.1 = ((bf16[16,96,128]{2,1,0:T(8,128)(2,1)}), bf16[16,96,128]{2,1,0:T(8,128)(2,1)S(1)}, u32[]{:S(2)}, u32[]{:S(2)}) async-start(bf16[16,96,128]{2,1,0:T(8,128)(2,1)} %bitcast.7), calls=%async_computation.1 | async-start | bytes 786432 | tf_op jit(solution)/shard_map/all_to_all | solution.py:378
  62.8 0.7 %collective-permute-done.9 = f32[8,256]{1,0:T(8,128)S(1)} collective-permute-done((f32[8,256]{1,0:T(8,128)S(1)}, f32[8,256]{1,0:T(8,128)S(1)}, u32[]{:S(2)}, u32[]{:S(2)}) %collective-permute-start.9) | collective-permute-done | bytes 8224 | tf_op jit(solution)/shard_map/ppermute | solution.py:373
  63.6 0.6 fusion
  64.1 7.6 %all-to-all-done.1 = bf16[16,96,128]{2,1,0:T(8,128)(2,1)S(1)} async-done(((bf16[16,96,128]{2,1,0:T(8,128)(2,1)}), bf16[16,96,128]{2,1,0:T(8,128)(2,1)S(1)}, u32[]{:S(2)}, u32[]{:S(2)}) %all-to-all-start.1) | async-done | bytes 393248 | tf_op jit(solution)/shard_map/all_to_all | solution.py:378
  71.8 1.3 %shard_map.93 = bf16[10,3,384]{2,1,0:T(4,128)(2,1)} custom-call(s32[1,3]{1,0:T(1,128)S(1)} %dynamic-slice_bitcast_fusion.offset_ref, bf16[1536,128]{1,0:T(8,128)(2,1)S(1)} %bitcast.14, f32[1,10]{1,0:T(1,128)S(1)} %bitcast.16), custom_call_target="tpu_custom_call" | custom-call | tf_op jit(solution)/shard_map/pallas_call | solution.py:427
  (19 shorter events, 1.8 us)
Async XLA Ops:
  3.1 12.3 %collective-permute-start.1 = (bf16[16,3968]{1,0:T(8,128)(2,1)}, bf16[16,3968]{1,0:T(8,128)(2,1)S(1)}, u32[]{:S(2)}, u32[]{:S(2)}) collective-permute-start(bf16[16,3968]{1,0:T(8,128)(2,1)} %get-tuple-element.11.f0), channel_id=1, source_target_pairs={{0,48},{4,52},{8,56},{12,60},{16,32},{20,36},{24,40},{28,44},{32,1... | collective-permute-start | bytes 380936 | tf_op jit(solution)/shard_map/ppermute | solution.py:370
  8.3 10.0 %collective-permute-start = (bf16[16,3968]{1,0:T(8,128)(2,1)}, bf16[16,3968]{1,0:T(8,128)(2,1)S(1)}, u32[]{:S(2)}, u32[]{:S(2)}) collective-permute-start(bf16[16,3968]{1,0:T(8,128)(2,1)} %get-tuple-element.11.f0), channel_id=1, source_target_pairs={{0,32},{4,36},{8,40},{12,44},{16,48},{20,52},{24,56},{28,60},{32,0... | collective-permute-start | bytes 380936 | tf_op jit(solution)/shard_map/ppermute | solution.py:370
  8.3 15.6 %all-to-all-start = ((bf16[16,96,128]{2,1,0:T(8,128)(2,1)}), bf16[16,96,128]{2,1,0:T(8,128)(2,1)S(1)}, u32[]{:S(2)}, u32[]{:S(2)}) async-start(bf16[16,96,128]{2,1,0:T(8,128)(2,1)} %bitcast.17), calls=%async_computation | async-start | bytes 786432 | tf_op jit(solution)/shard_map/all_to_all | solution.py:378
  15.1 8.9 %copy-start = (bf16[16,3968]{1,0:T(8,128)(2,1)S(1)}, bf16[16,3968]{1,0:T(8,128)(2,1)}, u32[]{:S(2)}) copy-start(bf16[16,3968]{1,0:T(8,128)(2,1)} %get-tuple-element.11.f0) | copy-start | bytes 380932
  15.1 6.4 %collective-permute-start.2 = (bf16[16,3968]{1,0:T(8,128)(2,1)}, bf16[16,3968]{1,0:T(8,128)(2,1)S(1)}, u32[]{:S(2)}, u32[]{:S(2)}) collective-permute-start(bf16[16,3968]{1,0:T(8,128)(2,1)} %get-tuple-element.11.f0), channel_id=1, source_target_pairs={{0,16},{4,20},{8,24},{12,28},{16,0},{20,4},{24,8},{28,12},{32,48},... | collective-permute-start | bytes 380936 | tf_op jit(solution)/shard_map/ppermute | solution.py:370
  25.9 3.5 %collective-permute-start.3 = (f32[288,256]{1,0:T(8,128)S(1)}, f32[288,256]{1,0:T(8,128)S(1)}, u32[]{:S(2)}, u32[]{:S(2)}) collective-permute-start(f32[288,256]{1,0:T(8,128)S(1)} %get-tuple-element.14), channel_id=1, source_target_pairs={{0,1},{1,0},{2,3},{3,2},{4,5},{5,4},{6,7},{7,6},{8,9},{9,8},{10,11... | collective-permute-start | bytes 884744 | tf_op jit(solution)/shard_map/ppermute | solution.py:373
  29.4 12.3 %collective-permute-start.4 = (f32[288,256]{1,0:T(8,128)S(1)}, f32[288,256]{1,0:T(8,128)S(1)}, u32[]{:S(2)}, u32[]{:S(2)}) collective-permute-start(f32[288,256]{1,0:T(8,128)S(1)} %add.22.mine_ref), channel_id=1, source_target_pairs={{0,2},{1,3},{2,0},{3,1},{4,6},{5,7},{6,4},{7,5},{8,10},{9,11},{10,... | collective-permute-start | bytes 884744 | tf_op jit(solution)/shard_map/ppermute | solution.py:373
  42.1 9.3 %collective-permute-start.7 = (f32[8,256]{1,0:T(8,128)S(1)}, f32[8,256]{1,0:T(8,128)S(1)}, u32[]{:S(2)}, u32[]{:S(2)}) collective-permute-start(f32[8,256]{1,0:T(8,128)S(1)} %get-tuple-element.16.s0), channel_id=1, source_target_pairs={{0,48},{4,52},{8,56},{12,60},{16,32},{20,36},{24,40},{28,44},{32,1... | collective-permute-start | bytes 24584 | tf_op jit(solution)/shard_map/ppermute | solution.py:370
  43.2 9.0 %collective-permute-start.6 = (f32[8,256]{1,0:T(8,128)S(1)}, f32[8,256]{1,0:T(8,128)S(1)}, u32[]{:S(2)}, u32[]{:S(2)}) collective-permute-start(f32[8,256]{1,0:T(8,128)S(1)} %get-tuple-element.16.s0), channel_id=1, source_target_pairs={{0,32},{4,36},{8,40},{12,44},{16,48},{20,52},{24,56},{28,60},{32,0... | collective-permute-start | bytes 24584 | tf_op jit(solution)/shard_map/ppermute | solution.py:370
  51.2 2.5 %collective-permute-start.5 = (f32[8,256]{1,0:T(8,128)S(1)}, f32[8,256]{1,0:T(8,128)S(1)}, u32[]{:S(2)}, u32[]{:S(2)}) collective-permute-start(f32[8,256]{1,0:T(8,128)S(1)} %get-tuple-element.16.s0), channel_id=1, source_target_pairs={{0,16},{4,20},{8,24},{12,28},{16,0},{20,4},{24,8},{28,12},{32,48},... | collective-permute-start | bytes 24584 | tf_op jit(solution)/shard_map/ppermute | solution.py:370
  53.8 3.2 %collective-permute-start.8 = (bf16[288,256]{1,0:T(8,128)(2,1)S(1)}, bf16[288,256]{1,0:T(8,128)(2,1)S(1)}, u32[]{:S(2)}, u32[]{:S(2)}) collective-permute-start(bf16[288,256]{1,0:T(8,128)(2,1)S(1)} %get-tuple-element.17.probs_ref), channel_id=1, source_target_pairs={{0,1},{1,0},{2,3},{3,2},{4,5},{5,4},{6,7},{7,6},{8,9},{9,8},{10,11... | collective-permute-start | bytes 442376 | tf_op jit(solution)/shard_map/ppermute | solution.py:373
  56.8 5.9 %copy-start.2 = (s32[192]{0:T(256)S(1)}, s32[192]{0:T(256)}, u32[]{:S(2)}) copy-start(s32[192]{0:T(256)} %offset_ref.1) | copy-start | bytes 2308
  56.8 15.0 %copy-start.1 = (f32[10]{0:T(128)S(1)}, f32[10]{0:T(128)}, u32[]{:S(2)}) copy-start(f32[10]{0:T(128)} %param.13) | copy-start | bytes 124
  58.7 13.1 %all-to-all-start.1 = ((bf16[16,96,128]{2,1,0:T(8,128)(2,1)}), bf16[16,96,128]{2,1,0:T(8,128)(2,1)S(1)}, u32[]{:S(2)}, u32[]{:S(2)}) async-start(bf16[16,96,128]{2,1,0:T(8,128)(2,1)} %bitcast.7), calls=%async_computation.1 | async-start | bytes 786432 | tf_op jit(solution)/shard_map/all_to_all | solution.py:378
  62.3 1.3 %collective-permute-start.9 = (f32[8,256]{1,0:T(8,128)S(1)}, f32[8,256]{1,0:T(8,128)S(1)}, u32[]{:S(2)}, u32[]{:S(2)}) collective-permute-start(f32[8,256]{1,0:T(8,128)S(1)} %get-tuple-element.19), channel_id=1, source_target_pairs={{0,1},{1,0},{2,3},{3,2},{4,5},{5,4},{6,7},{7,6},{8,9},{9,8},{10,11... | collective-permute-start | bytes 24584 | tf_op jit(solution)/shard_map/ppermute | solution.py:373

commit v6 on v5

--- a/solution.py
+++ b/solution.py
@@ -83,26 +83,34 @@
     return jnp.where(first, a0, a1)
 
 
-def turn_classes(stacked, shifts):
-    row = lax.broadcasted_iota(jnp.int32, stacked.shape, 0) % 8
-    turned = doubled_roll(stacked, shifts[0])
-    for c in range(1, OWN_CLASSES):
-        turned = jnp.where(row == c, doubled_roll(stacked, shifts[c]), turned)
-    return turned
+LANES = [slice(v * 128, v * 128 + 128) for v in range(ROW // 128)]
+STEP_ROWS = 24
+
+
+def turn_classes(grouped, shifts):
+    for c, shift in enumerate(shifts):
+        rows = slice(c * STEP_ROWS, c * STEP_ROWS + 16)
+        wide = jnp.concatenate([grouped[v, rows, :] for v in range(3)], axis=1)
+        wide = doubled_roll(wide, shift)
+        for v, at in enumerate(LANES):
+            grouped[v, rows, :] = wide[:, at]
 
 
 def prologue_kernel(
     first_ref, offset_ref, group_ref, images_ref, refs_ref, ctf_ref, noise_ref,
     image_msg, class_msg,
-    table_f, table_s, filt, square, stacked, own,
+    table_f, table_s, filt, square, grouped, own,
 ):
-    stacked[...] = jnp.zeros_like(stacked)
-    for p in range(CYC):
-        stacked[p * 8 : p * 8 + OWN_CLASSES, :] = refs_ref[p].astype(F32)
-    turned = turn_classes(
-        stacked[...], [offset_ref[first_ref[0] + c] for c in range(OWN_CLASSES)]
-    )
-    rows = [turned[p * 8 : p * 8 + 8] for p in range(CYC)]
+    grouped[...] = jnp.zeros_like(grouped)
+    for p in range(CYC):
+        row = refs_ref[p].astype(F32)
+        for v, at in enumerate(LANES):
+            grouped[v, pl.ds(p, OWN_CLASSES, stride=STEP_ROWS), :] = row[:, at]
+    turn_classes(grouped, [offset_ref[first_ref[0] + c] for c in range(OWN_CLASSES)])
+    rows = []
+    for p in range(CYC):
+        parts = [grouped[v, pl.ds(p, 8, stride=STEP_ROWS), :] for v in range(3)]
+        rows.append(jnp.concatenate(parts, axis=1))
     lane8 = lanes_of((8, 128))
     power = jnp.zeros((8, 128), F32)
     for p in range(CYC):
@@ -255,7 +263,7 @@
     evidence_ref[...] = jnp.broadcast_to(evidence, (8, HALF))
 
 
-def add_turns(probs_ref, fine_ref, sums, fresh):
+def add_turns(probs_ref, fine_ref, sums, base):
     for w in range(0, TURNS, 2):
         span = slice(w * BLOCK, (w + 2) * BLOCK + (128 if w == TURNS - 2 else 0))
         turned = jnp.dot(probs_ref[...], fine_ref[:, span], preferred_element_type=F32)
@@ -264,8 +272,8 @@
                 back = (b - g) % TURNS
                 at = slice(back * BLOCK, (back + 1) * BLOCK)
                 term = turned[g * CLS : (g + 1) * CLS, (b - w) * BLOCK : (b - w + 1) * BLOCK]
-                if b == 0 and fresh:
-                    sums[:, at] = term
+                if b == 0:
+                    sums[:, at] = term if base is None else base[:, at] + term
                 else:
                     sums[:, at] += term
         if w == TURNS - 2:
@@ -277,13 +285,12 @@
 
 def own_sums_kernel(probs_ref, fine_ref, sums_ref):
     mine = fine_ref.at[jnp.where(is_near(), 0, 1)]
-    sums_ref[:, COEF:] = add_turns(probs_ref, mine, sums_ref, True)
+    sums_ref[:, COEF:] = add_turns(probs_ref, mine, sums_ref, None)
 
 
 def all_sums_kernel(probs_ref, fine_ref, own_ref, out_ref, sums, packed):
-    sums[...] = own_ref[...]
     rest = fine_ref.at[jnp.where(is_near(), 1, 0)]
-    mass = sums[:, COEF:] + add_turns(probs_ref, rest, sums, False)
+    mass = own_ref[:, COEF:] + add_turns(probs_ref, rest, sums, own_ref)
     mass = mass + pltpu.roll(mass, 118, 1) + pltpu.roll(mass, 98, 1)
     mass = jnp.where(lanes_of((CLS, 128)) < CYC, mass, 0.0)
     hi, mid, lo = three_parts(mass)
@@ -297,7 +304,7 @@
         out_ref[d * CHUNK : (d + 1) * CHUNK, :] = packed[d * PITCH : d * PITCH + CHUNK, :].astype(BF16)
 
 
-def final_kernel(offset_ref, msg_ref, prior_ref, out_ref, summed):
+def final_kernel(offset_ref, msg_ref, prior_ref, out_ref, summed, grouped):
     total = msg_ref[:CHUNK, :].astype(F32)
     for d in range(1, CLS_PEERS):
         total = total + msg_ref[d * CHUNK : (d + 1) * CHUNK, :].astype(F32)
@@ -318,9 +325,8 @@
     flat = jnp.concatenate([tiles[k] for k in keys], axis=0).astype(BF16)
     flat = jnp.dot(flat, interleaving(back=True), preferred_element_type=F32)
     tiles = {k: flat[8 * n : 8 * n + 8] for n, k in enumerate(keys)}
-    rows = []
-    for p in range(CYC):
-        vregs = []
+    grouped[...] = jnp.zeros_like(grouped)
+    for p in range(CYC):
         for v in range(3):
             parts = []
             for u in range(4):
@@ -330,15 +336,17 @@
                 shift = (32 * u - 32 * t) % 128
                 piece = tiles[w, p // 2]
                 parts.append(pltpu.roll(piece, shift, 1) if shift else piece)
-            vregs.append(pick4(lane, parts))
-        rows.append(jnp.concatenate(vregs, axis=1))
+            grouped[v, pl.ds(p, OWN_CLASSES, stride=STEP_ROWS), :] = pick4(lane, parts)[
+                :OWN_CLASSES
+            ]
     shifts = []
     for c in range(OWN_CLASSES):
         off = offset_ref[0, c]
         shifts.append(jnp.where(off == 0, 0, ROW - off))
-    turned = turn_classes(jnp.concatenate(rows, axis=0), shifts)
-    for p in range(CYC):
-        out_ref[p] = turned[p * 8 : p * 8 + OWN_CLASSES].astype(BF16)
+    turn_classes(grouped, shifts)
+    for p in range(CYC):
+        for v, at in enumerate(LANES):
+            out_ref[p, :, at] = grouped[v, pl.ds(p, OWN_CLASSES, stride=STEP_ROWS), :].astype(BF16)
 
 
 def call(kernel, outs, scratch, specs, limit=VMEM_LIMIT, cost=None):
@@ -380,7 +388,7 @@
     image_msg, class_msg = call(
         prologue_kernel,
         [shaped((OWN_IMAGES, WIDE), BF16), shaped((CLS_PEERS * CHUNK, 128), BF16)],
-        [V((16, 128), F32)] * 4 + [V((CYC * 8, ROW), F32), V((CHUNK, 128), F32)],
+        [V((16, 128), F32)] * 4 + [V((3, 8 * STEP_ROWS, 128), F32), V((CHUNK, 128), F32)],
         [S, S, S, V, V, V, V],
         VMEM_MOST,
     )(
@@ -427,7 +435,7 @@
     new_references = call(
         final_kernel,
         shaped((CYC, OWN_CLASSES, ROW), BF16),
-        [V((8 * SLOT, 128), F32)],
+        [V((8 * SLOT, 128), F32), V((3, OWN_CLASSES * STEP_ROWS, 128), F32)],
         [V, V, V],
     )(offsets, own, prior_precision.reshape(1, CYC))
     mine = jnp.where(core == level // 2, evidence[0], evidence_other[0])

time: 73.4 us -> 73.2 us (level)
  no operation moved by 1% of the time
where the time goes in v6:
time: 73.2 us; the launch traced here: 72.9 us
  starting transfers between devices  34.7 us (47%)
  waiting for transfers between devices  27.7 us (38%)
  Pallas kernels  9.07 us (12%)
  between operations  0.74 us (1%)
    ppermute x6, starting transfers between devices, along_peers(): return lax.ppermute(x, 'img', [(i, i ^ 4 * k) for i in range(64)])  14.9 us
    all_to_all x2, starting transfers between devices, over_classes(): return lax.all_to_all(x, 'img', 0, 0, axis_index_groups=groups, tiled=True)  10.3 us
    all_to_all x2, waiting for transfers between devices, over_classes(): return lax.all_to_all(x, 'img', 0, 0, axis_index_groups=groups, tiled=True)  10.1 us
    ppermute x4, waiting for transfers between devices, along_shell(): return lax.ppermute(x, 'shell', [(i, i ^ k) for i in range(4)])  9.85 us
    ppermute x4, starting transfers between devices, along_shell(): return lax.ppermute(x, 'shell', [(i, i ^ k) for i in range(4)])  9.47 us
    ppermute x6, waiting for transfers between devices, along_peers(): return lax.ppermute(x, 'img', [(i, i ^ 4 * k) for i in range(64)])  7.71 us
    pallas_call x1, Pallas kernels, local(): call(prologue_kernel, [shaped((OWN_IMAGES, WIDE), BF16), shaped((CLS_PEER...  2.3 us
    pallas_call x1, Pallas kernels, local(): call(scores_kernel, [shaped((ROWS, HALF), F32)] * 2 + [shaped((2, HALF, W...  1.94 us
  transfers between devices with their start and end apart: 12, of which 10 were waited for; matrix products, arithmetic and copies ran while one was open for 1% of the time, Pallas kernels for 2%

profile of v6, /device:TPU:1, one launch (start us, length us, event | category | flops | bytes accessed | tf_op | source)
XLA Modules:
  0.0 72.9 jit_solution(16104348996753398547)
XLA Ops:
  0.6 2.3 %shard_map.86 = (bf16[16,3968]{1,0:T(8,128)(2,1)}, bf16[1536,128]{1,0:T(8,128)(2,1)}) custom-call(s32[1]{0:T(128)} %bitcast.1.first_ref, s32[192]{0:T(256)} %offset_ref.1, s32[16]{0:T(128)} %group_ref.1, f32[10,16,384]{2,1,0:T(8,128)} %bitcast.18, bf16[10,3,384]{2,1,0:T(4,128)(2,1)} %bitcast.19, f32[16,10]{1,0:T(8,128)} %ctf_ref.1, f32[1,10]{1,0:T(1,128)} %bitcast.21), custom_call_target="tpu_custom_call" | custom-call | tf_op jit(solution)/shard_map/pallas_call | solution.py:388
  2.9 5.2 %collective-permute-start.1 = (bf16[16,3968]{1,0:T(8,128)(2,1)}, bf16[16,3968]{1,0:T(8,128)(2,1)S(1)}, u32[]{:S(2)}, u32[]{:S(2)}) collective-permute-start(bf16[16,3968]{1,0:T(8,128)(2,1)} %get-tuple-element.11.f0), channel_id=1, source_target_pairs={{0,48},{4,52},{8,56},{12,60},{16,32},{20,36},{24,40},{28,44},{32,1... | collective-permute-start | bytes 380936 | tf_op jit(solution)/shard_map/ppermute | solution.py:378
  8.1 6.8 %all-to-all-start = ((bf16[16,96,128]{2,1,0:T(8,128)(2,1)}), bf16[16,96,128]{2,1,0:T(8,128)(2,1)S(1)}, u32[]{:S(2)}, u32[]{:S(2)}) async-start(bf16[16,96,128]{2,1,0:T(8,128)(2,1)} %bitcast.17), calls=%async_computation | async-start | bytes 786432 | tf_op jit(solution)/shard_map/all_to_all | solution.py:386
  15.3 2.9 %collective-permute-done.f2 = bf16[16,3968]{1,0:T(8,128)(2,1)S(1)} collective-permute-done((bf16[16,3968]{1,0:T(8,128)(2,1)}, bf16[16,3968]{1,0:T(8,128)(2,1)S(1)}, u32[]{:S(2)}, u32[]{:S(2)}) %collective-permute-start) | collective-permute-done | bytes 127008 | tf_op jit(solution)/shard_map/ppermute | solution.py:378
  18.1 0.5 shard_map.87.far_ref
  18.7 2.6 %collective-permute-done.2.f1 = bf16[16,3968]{1,0:T(8,128)(2,1)S(1)} collective-permute-done((bf16[16,3968]{1,0:T(8,128)(2,1)}, bf16[16,3968]{1,0:T(8,128)(2,1)S(1)}, u32[]{:S(2)}, u32[]{:S(2)}) %collective-permute-start.2) | collective-permute-done | bytes 127008 | tf_op jit(solution)/shard_map/ppermute | solution.py:378
  21.3 2.5 %all-to-all-done = bf16[16,96,128]{2,1,0:T(8,128)(2,1)S(1)} async-done(((bf16[16,96,128]{2,1,0:T(8,128)(2,1)}), bf16[16,96,128]{2,1,0:T(8,128)(2,1)S(1)}, u32[]{:S(2)}, u32[]{:S(2)}) %all-to-all-start) | async-done | bytes 393248 | tf_op jit(solution)/shard_map/all_to_all | solution.py:386
  23.8 1.9 %shard_map.88 = (f32[288,256]{1,0:T(8,128)S(1)}, f32[288,256]{1,0:T(8,128)S(1)}, bf16[2,256,3968]{2,1,0:T(8,128)(2,1)S(1)}) custom-call(bf16[256,3968]{1,0:T(8,128)(2,1)S(1)} %shard_map.87.far_ref, bf16[16,3968]{1,0:T(8,128)(2,1)S(1)} %copy-done, bf16[16,3968]{1,0:T(8,128)(2,1)S(1)} %collective-permute-done.2.f1, bf16[1536,128]{1,0:T(8,128)(2,1)S(1)} %bitcast.15), custom_call_target="tpu_custom_call" | custom-call | tf_op jit(solution)/shard_map/pallas_call | solution.py:407
  25.7 2.2 %collective-permute-start.3 = (f32[288,256]{1,0:T(8,128)S(1)}, f32[288,256]{1,0:T(8,128)S(1)}, u32[]{:S(2)}, u32[]{:S(2)}) collective-permute-start(f32[288,256]{1,0:T(8,128)S(1)} %get-tuple-element.14), channel_id=1, source_target_pairs={{0,1},{1,0},{2,3},{3,2},{4,5},{5,4},{6,7},{7,6},{8,9},{9,8},{10,11... | collective-permute-start | bytes 884744 | tf_op jit(solution)/shard_map/ppermute | solution.py:381
  28.0 1.2 %collective-permute-done.3 = f32[288,256]{1,0:T(8,128)S(1)} collective-permute-done((f32[288,256]{1,0:T(8,128)S(1)}, f32[288,256]{1,0:T(8,128)S(1)}, u32[]{:S(2)}, u32[]{:S(2)}) %collective-permute-start.3) | collective-permute-done | bytes 294944 | tf_op jit(solution)/shard_map/ppermute | solution.py:381
  29.2 4.6 %collective-permute-start.4 = (f32[288,256]{1,0:T(8,128)S(1)}, f32[288,256]{1,0:T(8,128)S(1)}, u32[]{:S(2)}, u32[]{:S(2)}) collective-permute-start(f32[288,256]{1,0:T(8,128)S(1)} %add.22.mine_ref), channel_id=1, source_target_pairs={{0,2},{1,3},{2,0},{3,1},{4,6},{5,7},{6,4},{7,5},{8,10},{9,11},{10,... | collective-permute-start | bytes 884744 | tf_op jit(solution)/shard_map/ppermute | solution.py:381
  33.8 7.7 %collective-permute-done.4.other_ref = f32[288,256]{1,0:T(8,128)S(1)} collective-permute-done((f32[288,256]{1,0:T(8,128)S(1)}, f32[288,256]{1,0:T(8,128)S(1)}, u32[]{:S(2)}, u32[]{:S(2)}) %collective-permute-start.4) | collective-permute-done | bytes 294944 | tf_op jit(solution)/shard_map/ppermute | solution.py:381
  41.9 1.1 %collective-permute-start.7 = (f32[8,256]{1,0:T(8,128)S(1)}, f32[8,256]{1,0:T(8,128)S(1)}, u32[]{:S(2)}, u32[]{:S(2)}) collective-permute-start(f32[8,256]{1,0:T(8,128)S(1)} %get-tuple-element.16.s0), channel_id=1, source_target_pairs={{0,48},{4,52},{8,56},{12,60},{16,32},{20,36},{24,40},{28,44},{32,1... | collective-permute-start | bytes 24584 | tf_op jit(solution)/shard_map/ppermute | solution.py:378
  43.0 8.0 %collective-permute-start.6 = (f32[8,256]{1,0:T(8,128)S(1)}, f32[8,256]{1,0:T(8,128)S(1)}, u32[]{:S(2)}, u32[]{:S(2)}) collective-permute-start(f32[8,256]{1,0:T(8,128)S(1)} %get-tuple-element.16.s0), channel_id=1, source_target_pairs={{0,32},{4,36},{8,40},{12,44},{16,48},{20,52},{24,56},{28,60},{32,0... | collective-permute-start | bytes 24584 | tf_op jit(solution)/shard_map/ppermute | solution.py:378
  51.2 0.8 %collective-permute-done.6.s2 = f32[8,256]{1,0:T(8,128)S(1)} collective-permute-done((f32[8,256]{1,0:T(8,128)S(1)}, f32[8,256]{1,0:T(8,128)S(1)}, u32[]{:S(2)}, u32[]{:S(2)}) %collective-permute-start.6) | collective-permute-done | bytes 8224 | tf_op jit(solution)/shard_map/ppermute | solution.py:378
  52.1 1.4 %collective-permute-done.5.s1 = f32[8,256]{1,0:T(8,128)S(1)} collective-permute-done((f32[8,256]{1,0:T(8,128)S(1)}, f32[8,256]{1,0:T(8,128)S(1)}, u32[]{:S(2)}, u32[]{:S(2)}) %collective-permute-start.5) | collective-permute-done | bytes 8224 | tf_op jit(solution)/shard_map/ppermute | solution.py:378
  53.6 2.2 %collective-permute-start.8 = (bf16[288,256]{1,0:T(8,128)(2,1)S(1)}, bf16[288,256]{1,0:T(8,128)(2,1)S(1)}, u32[]{:S(2)}, u32[]{:S(2)}) collective-permute-start(bf16[288,256]{1,0:T(8,128)(2,1)S(1)} %get-tuple-element.17.probs_ref), channel_id=1, source_target_pairs={{0,1},{1,0},{2,3},{3,2},{4,5},{5,4},{6,7},{7,6},{8,9},{9,8},{10,11... | collective-permute-start | bytes 442376 | tf_op jit(solution)/shard_map/ppermute | solution.py:381
  55.8 0.8 %shard_map.91.own_ref = f32[48,3968]{1,0:T(8,128)S(1)} custom-call(bf16[288,256]{1,0:T(8,128)(2,1)S(1)} %get-tuple-element.17.probs_ref, bf16[2,256,3968]{2,1,0:T(8,128)(2,1)S(1)} %get-tuple-element.18.fine_ref), custom_call_target="tpu_custom_call" | custom-call | tf_op jit(solution)/shard_map/pallas_call | solution.py:427
  56.8 1.7 %shard_map.92 = bf16[1536,128]{1,0:T(8,128)(2,1)} custom-call(bf16[288,256]{1,0:T(8,128)(2,1)S(1)} %collective-permute-done.8.probs_ref, bf16[2,256,3968]{2,1,0:T(8,128)(2,1)S(1)} %get-tuple-element.18.fine_ref, f32[48,3968]{1,0:T(8,128)S(1)} %shard_map.91.own_ref), custom_call_target="tpu_custom_call" | custom-call | tf_op jit(solution)/shard_map/pallas_call | solution.py:428
  58.5 3.6 %all-to-all-start.1 = ((bf16[16,96,128]{2,1,0:T(8,128)(2,1)}), bf16[16,96,128]{2,1,0:T(8,128)(2,1)S(1)}, u32[]{:S(2)}, u32[]{:S(2)}) async-start(bf16[16,96,128]{2,1,0:T(8,128)(2,1)} %bitcast.7), calls=%async_computation.1 | async-start | bytes 786432 | tf_op jit(solution)/shard_map/all_to_all | solution.py:386
  62.7 0.7 %collective-permute-done.9 = f32[8,256]{1,0:T(8,128)S(1)} collective-permute-done((f32[8,256]{1,0:T(8,128)S(1)}, f32[8,256]{1,0:T(8,128)S(1)}, u32[]{:S(2)}, u32[]{:S(2)}) %collective-permute-start.9) | collective-permute-done | bytes 8224 | tf_op jit(solution)/shard_map/ppermute | solution.py:381
  63.4 0.6 fusion
  64.0 7.6 %all-to-all-done.1 = bf16[16,96,128]{2,1,0:T(8,128)(2,1)S(1)} async-done(((bf16[16,96,128]{2,1,0:T(8,128)(2,1)}), bf16[16,96,128]{2,1,0:T(8,128)(2,1)S(1)}, u32[]{:S(2)}, u32[]{:S(2)}) %all-to-all-start.1) | async-done | bytes 393248 | tf_op jit(solution)/shard_map/all_to_all | solution.py:386
  71.6 1.3 %shard_map.93 = bf16[10,3,384]{2,1,0:T(4,128)(2,1)} custom-call(s32[1,3]{1,0:T(1,128)S(1)} %dynamic-slice_bitcast_fusion.offset_ref, bf16[1536,128]{1,0:T(8,128)(2,1)S(1)} %bitcast.14, f32[1,10]{1,0:T(1,128)S(1)} %bitcast.16), custom_call_target="tpu_custom_call" | custom-call | tf_op jit(solution)/shard_map/pallas_call | solution.py:435
  (19 shorter events, 1.8 us)
Async XLA Ops:
  2.9 12.3 %collective-permute-start.1 = (bf16[16,3968]{1,0:T(8,128)(2,1)}, bf16[16,3968]{1,0:T(8,128)(2,1)S(1)}, u32[]{:S(2)}, u32[]{:S(2)}) collective-permute-start(bf16[16,3968]{1,0:T(8,128)(2,1)} %get-tuple-element.11.f0), channel_id=1, source_target_pairs={{0,48},{4,52},{8,56},{12,60},{16,32},{20,36},{24,40},{28,44},{32,1... | collective-permute-start | bytes 380936 | tf_op jit(solution)/shard_map/ppermute | solution.py:378
  8.1 10.0 %collective-permute-start = (bf16[16,3968]{1,0:T(8,128)(2,1)}, bf16[16,3968]{1,0:T(8,128)(2,1)S(1)}, u32[]{:S(2)}, u32[]{:S(2)}) collective-permute-start(bf16[16,3968]{1,0:T(8,128)(2,1)} %get-tuple-element.11.f0), channel_id=1, source_target_pairs={{0,32},{4,36},{8,40},{12,44},{16,48},{20,52},{24,56},{28,60},{32,0... | collective-permute-start | bytes 380936 | tf_op jit(solution)/shard_map/ppermute | solution.py:378
  8.1 15.6 %all-to-all-start = ((bf16[16,96,128]{2,1,0:T(8,128)(2,1)}), bf16[16,96,128]{2,1,0:T(8,128)(2,1)S(1)}, u32[]{:S(2)}, u32[]{:S(2)}) async-start(bf16[16,96,128]{2,1,0:T(8,128)(2,1)} %bitcast.17), calls=%async_computation | async-start | bytes 786432 | tf_op jit(solution)/shard_map/all_to_all | solution.py:386
  14.9 8.9 %copy-start = (bf16[16,3968]{1,0:T(8,128)(2,1)S(1)}, bf16[16,3968]{1,0:T(8,128)(2,1)}, u32[]{:S(2)}) copy-start(bf16[16,3968]{1,0:T(8,128)(2,1)} %get-tuple-element.11.f0) | copy-start | bytes 380932
  14.9 6.4 %collective-permute-start.2 = (bf16[16,3968]{1,0:T(8,128)(2,1)}, bf16[16,3968]{1,0:T(8,128)(2,1)S(1)}, u32[]{:S(2)}, u32[]{:S(2)}) collective-permute-start(bf16[16,3968]{1,0:T(8,128)(2,1)} %get-tuple-element.11.f0), channel_id=1, source_target_pairs={{0,16},{4,20},{8,24},{12,28},{16,0},{20,4},{24,8},{28,12},{32,48},... | collective-permute-start | bytes 380936 | tf_op jit(solution)/shard_map/ppermute | solution.py:378
  25.7 3.5 %collective-permute-start.3 = (f32[288,256]{1,0:T(8,128)S(1)}, f32[288,256]{1,0:T(8,128)S(1)}, u32[]{:S(2)}, u32[]{:S(2)}) collective-permute-start(f32[288,256]{1,0:T(8,128)S(1)} %get-tuple-element.14), channel_id=1, source_target_pairs={{0,1},{1,0},{2,3},{3,2},{4,5},{5,4},{6,7},{7,6},{8,9},{9,8},{10,11... | collective-permute-start | bytes 884744 | tf_op jit(solution)/shard_map/ppermute | solution.py:381
  29.2 12.3 %collective-permute-start.4 = (f32[288,256]{1,0:T(8,128)S(1)}, f32[288,256]{1,0:T(8,128)S(1)}, u32[]{:S(2)}, u32[]{:S(2)}) collective-permute-start(f32[288,256]{1,0:T(8,128)S(1)} %add.22.mine_ref), channel_id=1, source_target_pairs={{0,2},{1,3},{2,0},{3,1},{4,6},{5,7},{6,4},{7,5},{8,10},{9,11},{10,... | collective-permute-start | bytes 884744 | tf_op jit(solution)/shard_map/ppermute | solution.py:381
  41.9 9.3 %collective-permute-start.7 = (f32[8,256]{1,0:T(8,128)S(1)}, f32[8,256]{1,0:T(8,128)S(1)}, u32[]{:S(2)}, u32[]{:S(2)}) collective-permute-start(f32[8,256]{1,0:T(8,128)S(1)} %get-tuple-element.16.s0), channel_id=1, source_target_pairs={{0,48},{4,52},{8,56},{12,60},{16,32},{20,36},{24,40},{28,44},{32,1... | collective-permute-start | bytes 24584 | tf_op jit(solution)/shard_map/ppermute | solution.py:378
  43.0 9.0 %collective-permute-start.6 = (f32[8,256]{1,0:T(8,128)S(1)}, f32[8,256]{1,0:T(8,128)S(1)}, u32[]{:S(2)}, u32[]{:S(2)}) collective-permute-start(f32[8,256]{1,0:T(8,128)S(1)} %get-tuple-element.16.s0), channel_id=1, source_target_pairs={{0,32},{4,36},{8,40},{12,44},{16,48},{20,52},{24,56},{28,60},{32,0... | collective-permute-start | bytes 24584 | tf_op jit(solution)/shard_map/ppermute | solution.py:378
  51.0 2.5 %collective-permute-start.5 = (f32[8,256]{1,0:T(8,128)S(1)}, f32[8,256]{1,0:T(8,128)S(1)}, u32[]{:S(2)}, u32[]{:S(2)}) collective-permute-start(f32[8,256]{1,0:T(8,128)S(1)} %get-tuple-element.16.s0), channel_id=1, source_target_pairs={{0,16},{4,20},{8,24},{12,28},{16,0},{20,4},{24,8},{28,12},{32,48},... | collective-permute-start | bytes 24584 | tf_op jit(solution)/shard_map/ppermute | solution.py:378
  53.6 3.2 %collective-permute-start.8 = (bf16[288,256]{1,0:T(8,128)(2,1)S(1)}, bf16[288,256]{1,0:T(8,128)(2,1)S(1)}, u32[]{:S(2)}, u32[]{:S(2)}) collective-permute-start(bf16[288,256]{1,0:T(8,128)(2,1)S(1)} %get-tuple-element.17.probs_ref), channel_id=1, source_target_pairs={{0,1},{1,0},{2,3},{3,2},{4,5},{5,4},{6,7},{7,6},{8,9},{9,8},{10,11... | collective-permute-start | bytes 442376 | tf_op jit(solution)/shard_map/ppermute | solution.py:381
  56.6 5.9 %copy-start.2 = (s32[192]{0:T(256)S(1)}, s32[192]{0:T(256)}, u32[]{:S(2)}) copy-start(s32[192]{0:T(256)} %offset_ref.1) | copy-start | bytes 2308
  56.6 15.0 %copy-start.1 = (f32[10]{0:T(128)S(1)}, f32[10]{0:T(128)}, u32[]{:S(2)}) copy-start(f32[10]{0:T(128)} %param.13) | copy-start | bytes 124
  58.5 13.1 %all-to-all-start.1 = ((bf16[16,96,128]{2,1,0:T(8,128)(2,1)}), bf16[16,96,128]{2,1,0:T(8,128)(2,1)S(1)}, u32[]{:S(2)}, u32[]{:S(2)}) async-start(bf16[16,96,128]{2,1,0:T(8,128)(2,1)} %bitcast.7), calls=%async_computation.1 | async-start | bytes 786432 | tf_op jit(solution)/shard_map/all_to_all | solution.py:386
  62.1 1.3 %collective-permute-start.9 = (f32[8,256]{1,0:T(8,128)S(1)}, f32[8,256]{1,0:T(8,128)S(1)}, u32[]{:S(2)}, u32[]{:S(2)}) collective-permute-start(f32[8,256]{1,0:T(8,128)S(1)} %get-tuple-element.19), channel_id=1, source_target_pairs={{0,1},{1,0},{2,3},{3,2},{4,5},{5,4},{6,7},{7,6},{8,9},{9,8},{10,11... | collective-permute-start | bytes 24584 | tf_op jit(solution)/shard_map/ppermute | solution.py:381

commit v7 on v6

--- a/solution.py
+++ b/solution.py
@@ -97,7 +97,7 @@
 
 
 def prologue_kernel(
-    first_ref, offset_ref, group_ref, images_ref, refs_ref, ctf_ref, noise_ref,
+    offset_ref, group_ref, images_ref, refs_ref, ctf_ref, noise_ref,
     image_msg, class_msg,
     table_f, table_s, filt, square, grouped, own,
 ):
@@ -106,7 +106,7 @@
         row = refs_ref[p].astype(F32)
         for v, at in enumerate(LANES):
             grouped[v, pl.ds(p, OWN_CLASSES, stride=STEP_ROWS), :] = row[:, at]
-    turn_classes(grouped, [offset_ref[first_ref[0] + c] for c in range(OWN_CLASSES)])
+    turn_classes(grouped, [offset_ref[lax.axis_index("img") * OWN_CLASSES + c] for c in range(OWN_CLASSES)])
     rows = []
     for p in range(CYC):
         parts = [grouped[v, pl.ds(p, 8, stride=STEP_ROWS), :] for v in range(3)]
@@ -371,7 +371,6 @@
 def local(images, references, class_offset, ctf_group, ctf, noise_power, prior_precision):
     img = lax.axis_index("img")
     level, core = place()
-    first = (img * OWN_CLASSES).astype(jnp.int32).reshape(1)
     offsets = lax.dynamic_slice_in_dim(class_offset, img * OWN_CLASSES, OWN_CLASSES).reshape(1, -1)
 
     def along_peers(x, k):
@@ -389,10 +388,10 @@
         prologue_kernel,
         [shaped((OWN_IMAGES, WIDE), BF16), shaped((CLS_PEERS * CHUNK, 128), BF16)],
         [V((16, 128), F32)] * 4 + [V((3, 8 * STEP_ROWS, 128), F32), V((CHUNK, 128), F32)],
-        [S, S, S, V, V, V, V],
+        [S, S, V, V, V, V],
         VMEM_MOST,
     )(
-        first, class_offset, ctf_group, jnp.transpose(images, (1, 0, 2)),
+        class_offset, ctf_group, jnp.transpose(images, (1, 0, 2)),
         jnp.transpose(references, (1, 0, 2)), ctf, noise_power.reshape(1, CYC),
     )
     held = [image_msg] + [along_peers(image_msg, k) for k in (1, 2, 3)]

time: 73.2 us -> 73.3 us (level)
  no operation moved by 1% of the time
where the time goes in v7:
time: 73.3 us; the launch traced here: 73 us
  starting transfers between devices  34.7 us (47%)
  waiting for transfers between devices  27.7 us (38%)
  Pallas kernels  9.12 us (12%)
  between operations  0.74 us (1%)
    ppermute x6, starting transfers between devices, along_peers(): return lax.ppermute(x, 'img', [(i, i ^ 4 * k) for i in range(64)])  14.9 us
    all_to_all x2, starting transfers between devices, over_classes(): return lax.all_to_all(x, 'img', 0, 0, axis_index_groups=groups, tiled=True)  10.3 us
    all_to_all x2, waiting for transfers between devices, over_classes(): return lax.all_to_all(x, 'img', 0, 0, axis_index_groups=groups, tiled=True)  10.1 us
    ppermute x4, waiting for transfers between devices, along_shell(): return lax.ppermute(x, 'shell', [(i, i ^ k) for i in range(4)])  9.89 us
    ppermute x4, starting transfers between devices, along_shell(): return lax.ppermute(x, 'shell', [(i, i ^ k) for i in range(4)])  9.48 us
    ppermute x6, waiting for transfers between devices, along_peers(): return lax.ppermute(x, 'img', [(i, i ^ 4 * k) for i in range(64)])  7.71 us
    pallas_call x1, Pallas kernels, local(): call(prologue_kernel, [shaped((OWN_IMAGES, WIDE), BF16), shaped((CLS_PEER...  2.3 us
    pallas_call x1, Pallas kernels, local(): call(scores_kernel, [shaped((ROWS, HALF), F32)] * 2 + [shaped((2, HALF, W...  2.01 us
  transfers between devices with their start and end apart: 12, of which 10 were waited for; matrix products, arithmetic and copies ran while one was open for 1% of the time, Pallas kernels for 2%

profile of v7, /device:TPU:1, one launch (start us, length us, event | category | flops | bytes accessed | tf_op | source)
XLA Modules:
  0.0 73.0 jit_solution(9356769986393586684)
XLA Ops:
  0.6 2.3 %shard_map.86 = (bf16[16,3968]{1,0:T(8,128)(2,1)}, bf16[1536,128]{1,0:T(8,128)(2,1)}) custom-call(s32[192]{0:T(256)} %offset_ref.1, s32[16]{0:T(128)} %group_ref.1, f32[10,16,384]{2,1,0:T(8,128)} %bitcast.17, bf16[10,3,384]{2,1,0:T(4,128)(2,1)} %bitcast.18, f32[16,10]{1,0:T(8,128)} %ctf_ref.1, f32[1,10]{1,0:T(1,128)} %bitcast.20), custom_call_target="tpu_custom_call" | custom-call | tf_op jit(solution)/shard_map/pallas_call | solution.py:387
  2.9 5.2 %collective-permute-start.1 = (bf16[16,3968]{1,0:T(8,128)(2,1)}, bf16[16,3968]{1,0:T(8,128)(2,1)S(1)}, u32[]{:S(2)}, u32[]{:S(2)}) collective-permute-start(bf16[16,3968]{1,0:T(8,128)(2,1)} %get-tuple-element.11.f0), channel_id=1, source_target_pairs={{0,48},{4,52},{8,56},{12,60},{16,32},{20,36},{24,40},{28,44},{32,1... | collective-permute-start | bytes 380936 | tf_op jit(solution)/shard_map/ppermute | solution.py:377
  8.1 6.8 %all-to-all-start = ((bf16[16,96,128]{2,1,0:T(8,128)(2,1)}), bf16[16,96,128]{2,1,0:T(8,128)(2,1)S(1)}, u32[]{:S(2)}, u32[]{:S(2)}) async-start(bf16[16,96,128]{2,1,0:T(8,128)(2,1)} %bitcast.16), calls=%async_computation | async-start | bytes 786432 | tf_op jit(solution)/shard_map/all_to_all | solution.py:385
  15.3 2.9 %collective-permute-done.f2 = bf16[16,3968]{1,0:T(8,128)(2,1)S(1)} collective-permute-done((bf16[16,3968]{1,0:T(8,128)(2,1)}, bf16[16,3968]{1,0:T(8,128)(2,1)S(1)}, u32[]{:S(2)}, u32[]{:S(2)}) %collective-permute-start) | collective-permute-done | bytes 127008 | tf_op jit(solution)/shard_map/ppermute | solution.py:377
  18.1 0.5 shard_map.87.far_ref
  18.7 2.6 %collective-permute-done.2.f1 = bf16[16,3968]{1,0:T(8,128)(2,1)S(1)} collective-permute-done((bf16[16,3968]{1,0:T(8,128)(2,1)}, bf16[16,3968]{1,0:T(8,128)(2,1)S(1)}, u32[]{:S(2)}, u32[]{:S(2)}) %collective-permute-start.2) | collective-permute-done | bytes 127008 | tf_op jit(solution)/shard_map/ppermute | solution.py:377
  21.2 2.5 %all-to-all-done = bf16[16,96,128]{2,1,0:T(8,128)(2,1)S(1)} async-done(((bf16[16,96,128]{2,1,0:T(8,128)(2,1)}), bf16[16,96,128]{2,1,0:T(8,128)(2,1)S(1)}, u32[]{:S(2)}, u32[]{:S(2)}) %all-to-all-start) | async-done | bytes 393248 | tf_op jit(solution)/shard_map/all_to_all | solution.py:385
  23.7 2.0 %shard_map.88 = (f32[288,256]{1,0:T(8,128)S(1)}, f32[288,256]{1,0:T(8,128)S(1)}, bf16[2,256,3968]{2,1,0:T(8,128)(2,1)S(1)}) custom-call(bf16[256,3968]{1,0:T(8,128)(2,1)S(1)} %shard_map.87.far_ref, bf16[16,3968]{1,0:T(8,128)(2,1)S(1)} %copy-done, bf16[16,3968]{1,0:T(8,128)(2,1)S(1)} %collective-permute-done.2.f1, bf16[1536,128]{1,0:T(8,128)(2,1)S(1)} %bitcast.14), custom_call_target="tpu_custom_call" | custom-call | tf_op jit(solution)/shard_map/pallas_call | solution.py:406
  25.8 2.2 %collective-permute-start.3 = (f32[288,256]{1,0:T(8,128)S(1)}, f32[288,256]{1,0:T(8,128)S(1)}, u32[]{:S(2)}, u32[]{:S(2)}) collective-permute-start(f32[288,256]{1,0:T(8,128)S(1)} %get-tuple-element.14), channel_id=1, source_target_pairs={{0,1},{1,0},{2,3},{3,2},{4,5},{5,4},{6,7},{7,6},{8,9},{9,8},{10,11... | collective-permute-start | bytes 884744 | tf_op jit(solution)/shard_map/ppermute | solution.py:380
  28.0 1.2 %collective-permute-done.3 = f32[288,256]{1,0:T(8,128)S(1)} collective-permute-done((f32[288,256]{1,0:T(8,128)S(1)}, f32[288,256]{1,0:T(8,128)S(1)}, u32[]{:S(2)}, u32[]{:S(2)}) %collective-permute-start.3) | collective-permute-done | bytes 294944 | tf_op jit(solution)/shard_map/ppermute | solution.py:380
  29.3 4.6 %collective-permute-start.4 = (f32[288,256]{1,0:T(8,128)S(1)}, f32[288,256]{1,0:T(8,128)S(1)}, u32[]{:S(2)}, u32[]{:S(2)}) collective-permute-start(f32[288,256]{1,0:T(8,128)S(1)} %add.22.mine_ref), channel_id=1, source_target_pairs={{0,2},{1,3},{2,0},{3,1},{4,6},{5,7},{6,4},{7,5},{8,10},{9,11},{10,... | collective-permute-start | bytes 884744 | tf_op jit(solution)/shard_map/ppermute | solution.py:380
  33.8 7.7 %collective-permute-done.4.other_ref = f32[288,256]{1,0:T(8,128)S(1)} collective-permute-done((f32[288,256]{1,0:T(8,128)S(1)}, f32[288,256]{1,0:T(8,128)S(1)}, u32[]{:S(2)}, u32[]{:S(2)}) %collective-permute-start.4) | collective-permute-done | bytes 294944 | tf_op jit(solution)/shard_map/ppermute | solution.py:380
  42.0 1.1 %collective-permute-start.7 = (f32[8,256]{1,0:T(8,128)S(1)}, f32[8,256]{1,0:T(8,128)S(1)}, u32[]{:S(2)}, u32[]{:S(2)}) collective-permute-start(f32[8,256]{1,0:T(8,128)S(1)} %get-tuple-element.16.s0), channel_id=1, source_target_pairs={{0,48},{4,52},{8,56},{12,60},{16,32},{20,36},{24,40},{28,44},{32,1... | collective-permute-start | bytes 24584 | tf_op jit(solution)/shard_map/ppermute | solution.py:377
  43.1 8.0 %collective-permute-start.6 = (f32[8,256]{1,0:T(8,128)S(1)}, f32[8,256]{1,0:T(8,128)S(1)}, u32[]{:S(2)}, u32[]{:S(2)}) collective-permute-start(f32[8,256]{1,0:T(8,128)S(1)} %get-tuple-element.16.s0), channel_id=1, source_target_pairs={{0,32},{4,36},{8,40},{12,44},{16,48},{20,52},{24,56},{28,60},{32,0... | collective-permute-start | bytes 24584 | tf_op jit(solution)/shard_map/ppermute | solution.py:377
  51.3 0.8 %collective-permute-done.6.s2 = f32[8,256]{1,0:T(8,128)S(1)} collective-permute-done((f32[8,256]{1,0:T(8,128)S(1)}, f32[8,256]{1,0:T(8,128)S(1)}, u32[]{:S(2)}, u32[]{:S(2)}) %collective-permute-start.6) | collective-permute-done | bytes 8224 | tf_op jit(solution)/shard_map/ppermute | solution.py:377
  52.1 1.4 %collective-permute-done.5.s1 = f32[8,256]{1,0:T(8,128)S(1)} collective-permute-done((f32[8,256]{1,0:T(8,128)S(1)}, f32[8,256]{1,0:T(8,128)S(1)}, u32[]{:S(2)}, u32[]{:S(2)}) %collective-permute-start.5) | collective-permute-done | bytes 8224 | tf_op jit(solution)/shard_map/ppermute | solution.py:377
  53.6 2.2 %collective-permute-start.8 = (bf16[288,256]{1,0:T(8,128)(2,1)S(1)}, bf16[288,256]{1,0:T(8,128)(2,1)S(1)}, u32[]{:S(2)}, u32[]{:S(2)}) collective-permute-start(bf16[288,256]{1,0:T(8,128)(2,1)S(1)} %get-tuple-element.17.probs_ref), channel_id=1, source_target_pairs={{0,1},{1,0},{2,3},{3,2},{4,5},{5,4},{6,7},{7,6},{8,9},{9,8},{10,11... | collective-permute-start | bytes 442376 | tf_op jit(solution)/shard_map/ppermute | solution.py:380
  55.9 0.8 %shard_map.91.own_ref = f32[48,3968]{1,0:T(8,128)S(1)} custom-call(bf16[288,256]{1,0:T(8,128)(2,1)S(1)} %get-tuple-element.17.probs_ref, bf16[2,256,3968]{2,1,0:T(8,128)(2,1)S(1)} %get-tuple-element.18.fine_ref), custom_call_target="tpu_custom_call" | custom-call | tf_op jit(solution)/shard_map/pallas_call | solution.py:426
  56.9 1.8 %shard_map.92 = bf16[1536,128]{1,0:T(8,128)(2,1)} custom-call(bf16[288,256]{1,0:T(8,128)(2,1)S(1)} %collective-permute-done.8.probs_ref, bf16[2,256,3968]{2,1,0:T(8,128)(2,1)S(1)} %get-tuple-element.18.fine_ref, f32[48,3968]{1,0:T(8,128)S(1)} %shard_map.91.own_ref), custom_call_target="tpu_custom_call" | custom-call | tf_op jit(solution)/shard_map/pallas_call | solution.py:427
  58.6 3.6 %all-to-all-start.1 = ((bf16[16,96,128]{2,1,0:T(8,128)(2,1)}), bf16[16,96,128]{2,1,0:T(8,128)(2,1)S(1)}, u32[]{:S(2)}, u32[]{:S(2)}) async-start(bf16[16,96,128]{2,1,0:T(8,128)(2,1)} %bitcast.6), calls=%async_computation.1 | async-start | bytes 786432 | tf_op jit(solution)/shard_map/all_to_all | solution.py:385
  62.7 0.7 %collective-permute-done.9 = f32[8,256]{1,0:T(8,128)S(1)} collective-permute-done((f32[8,256]{1,0:T(8,128)S(1)}, f32[8,256]{1,0:T(8,128)S(1)}, u32[]{:S(2)}, u32[]{:S(2)}) %collective-permute-start.9) | collective-permute-done | bytes 8224 | tf_op jit(solution)/shard_map/ppermute | solution.py:380
  63.5 0.6 fusion
  64.1 7.6 %all-to-all-done.1 = bf16[16,96,128]{2,1,0:T(8,128)(2,1)S(1)} async-done(((bf16[16,96,128]{2,1,0:T(8,128)(2,1)}), bf16[16,96,128]{2,1,0:T(8,128)(2,1)S(1)}, u32[]{:S(2)}, u32[]{:S(2)}) %all-to-all-start.1) | async-done | bytes 393248 | tf_op jit(solution)/shard_map/all_to_all | solution.py:385
  71.7 1.3 %shard_map.93 = bf16[10,3,384]{2,1,0:T(4,128)(2,1)} custom-call(s32[1,3]{1,0:T(1,128)S(1)} %dynamic-slice_bitcast_fusion.offset_ref, bf16[1536,128]{1,0:T(8,128)(2,1)S(1)} %bitcast.13, f32[1,10]{1,0:T(1,128)S(1)} %bitcast.15), custom_call_target="tpu_custom_call" | custom-call | tf_op jit(solution)/shard_map/pallas_call | solution.py:434
  (19 shorter events, 1.9 us)
Async XLA Ops:
  2.9 12.3 %collective-permute-start.1 = (bf16[16,3968]{1,0:T(8,128)(2,1)}, bf16[16,3968]{1,0:T(8,128)(2,1)S(1)}, u32[]{:S(2)}, u32[]{:S(2)}) collective-permute-start(bf16[16,3968]{1,0:T(8,128)(2,1)} %get-tuple-element.11.f0), channel_id=1, source_target_pairs={{0,48},{4,52},{8,56},{12,60},{16,32},{20,36},{24,40},{28,44},{32,1... | collective-permute-start | bytes 380936 | tf_op jit(solution)/shard_map/ppermute | solution.py:377
  8.1 10.0 %collective-permute-start = (bf16[16,3968]{1,0:T(8,128)(2,1)}, bf16[16,3968]{1,0:T(8,128)(2,1)S(1)}, u32[]{:S(2)}, u32[]{:S(2)}) collective-permute-start(bf16[16,3968]{1,0:T(8,128)(2,1)} %get-tuple-element.11.f0), channel_id=1, source_target_pairs={{0,32},{4,36},{8,40},{12,44},{16,48},{20,52},{24,56},{28,60},{32,0... | collective-permute-start | bytes 380936 | tf_op jit(solution)/shard_map/ppermute | solution.py:377
  8.1 15.6 %all-to-all-start = ((bf16[16,96,128]{2,1,0:T(8,128)(2,1)}), bf16[16,96,128]{2,1,0:T(8,128)(2,1)S(1)}, u32[]{:S(2)}, u32[]{:S(2)}) async-start(bf16[16,96,128]{2,1,0:T(8,128)(2,1)} %bitcast.16), calls=%async_computation | async-start | bytes 786432 | tf_op jit(solution)/shard_map/all_to_all | solution.py:385
  14.9 8.9 %copy-start = (bf16[16,3968]{1,0:T(8,128)(2,1)S(1)}, bf16[16,3968]{1,0:T(8,128)(2,1)}, u32[]{:S(2)}) copy-start(bf16[16,3968]{1,0:T(8,128)(2,1)} %get-tuple-element.11.f0) | copy-start | bytes 380932
  14.9 6.4 %collective-permute-start.2 = (bf16[16,3968]{1,0:T(8,128)(2,1)}, bf16[16,3968]{1,0:T(8,128)(2,1)S(1)}, u32[]{:S(2)}, u32[]{:S(2)}) collective-permute-start(bf16[16,3968]{1,0:T(8,128)(2,1)} %get-tuple-element.11.f0), channel_id=1, source_target_pairs={{0,16},{4,20},{8,24},{12,28},{16,0},{20,4},{24,8},{28,12},{32,48},... | collective-permute-start | bytes 380936 | tf_op jit(solution)/shard_map/ppermute | solution.py:377
  25.8 3.5 %collective-permute-start.3 = (f32[288,256]{1,0:T(8,128)S(1)}, f32[288,256]{1,0:T(8,128)S(1)}, u32[]{:S(2)}, u32[]{:S(2)}) collective-permute-start(f32[288,256]{1,0:T(8,128)S(1)} %get-tuple-element.14), channel_id=1, source_target_pairs={{0,1},{1,0},{2,3},{3,2},{4,5},{5,4},{6,7},{7,6},{8,9},{9,8},{10,11... | collective-permute-start | bytes 884744 | tf_op jit(solution)/shard_map/ppermute | solution.py:380
  29.3 12.3 %collective-permute-start.4 = (f32[288,256]{1,0:T(8,128)S(1)}, f32[288,256]{1,0:T(8,128)S(1)}, u32[]{:S(2)}, u32[]{:S(2)}) collective-permute-start(f32[288,256]{1,0:T(8,128)S(1)} %add.22.mine_ref), channel_id=1, source_target_pairs={{0,2},{1,3},{2,0},{3,1},{4,6},{5,7},{6,4},{7,5},{8,10},{9,11},{10,... | collective-permute-start | bytes 884744 | tf_op jit(solution)/shard_map/ppermute | solution.py:380
  42.0 9.3 %collective-permute-start.7 = (f32[8,256]{1,0:T(8,128)S(1)}, f32[8,256]{1,0:T(8,128)S(1)}, u32[]{:S(2)}, u32[]{:S(2)}) collective-permute-start(f32[8,256]{1,0:T(8,128)S(1)} %get-tuple-element.16.s0), channel_id=1, source_target_pairs={{0,48},{4,52},{8,56},{12,60},{16,32},{20,36},{24,40},{28,44},{32,1... | collective-permute-start | bytes 24584 | tf_op jit(solution)/shard_map/ppermute | solution.py:377
  43.1 9.0 %collective-permute-start.6 = (f32[8,256]{1,0:T(8,128)S(1)}, f32[8,256]{1,0:T(8,128)S(1)}, u32[]{:S(2)}, u32[]{:S(2)}) collective-permute-start(f32[8,256]{1,0:T(8,128)S(1)} %get-tuple-element.16.s0), channel_id=1, source_target_pairs={{0,32},{4,36},{8,40},{12,44},{16,48},{20,52},{24,56},{28,60},{32,0... | collective-permute-start | bytes 24584 | tf_op jit(solution)/shard_map/ppermute | solution.py:377
  51.1 2.5 %collective-permute-start.5 = (f32[8,256]{1,0:T(8,128)S(1)}, f32[8,256]{1,0:T(8,128)S(1)}, u32[]{:S(2)}, u32[]{:S(2)}) collective-permute-start(f32[8,256]{1,0:T(8,128)S(1)} %get-tuple-element.16.s0), channel_id=1, source_target_pairs={{0,16},{4,20},{8,24},{12,28},{16,0},{20,4},{24,8},{28,12},{32,48},... | collective-permute-start | bytes 24584 | tf_op jit(solution)/shard_map/ppermute | solution.py:377
  53.6 3.2 %collective-permute-start.8 = (bf16[288,256]{1,0:T(8,128)(2,1)S(1)}, bf16[288,256]{1,0:T(8,128)(2,1)S(1)}, u32[]{:S(2)}, u32[]{:S(2)}) collective-permute-start(bf16[288,256]{1,0:T(8,128)(2,1)S(1)} %get-tuple-element.17.probs_ref), channel_id=1, source_target_pairs={{0,1},{1,0},{2,3},{3,2},{4,5},{5,4},{6,7},{7,6},{8,9},{9,8},{10,11... | collective-permute-start | bytes 442376 | tf_op jit(solution)/shard_map/ppermute | solution.py:380
  56.6 6.0 %copy-start.2 = (s32[192]{0:T(256)S(1)}, s32[192]{0:T(256)}, u32[]{:S(2)}) copy-start(s32[192]{0:T(256)} %offset_ref.1) | copy-start | bytes 2308
  56.7 15.0 %copy-start.1 = (f32[10]{0:T(128)S(1)}, f32[10]{0:T(128)}, u32[]{:S(2)}) copy-start(f32[10]{0:T(128)} %param.13) | copy-start | bytes 124
  58.6 13.1 %all-to-all-start.1 = ((bf16[16,96,128]{2,1,0:T(8,128)(2,1)}), bf16[16,96,128]{2,1,0:T(8,128)(2,1)S(1)}, u32[]{:S(2)}, u32[]{:S(2)}) async-start(bf16[16,96,128]{2,1,0:T(8,128)(2,1)} %bitcast.6), calls=%async_computation.1 | async-start | bytes 786432 | tf_op jit(solution)/shard_map/all_to_all | solution.py:385
  62.2 1.3 %collective-permute-start.9 = (f32[8,256]{1,0:T(8,128)S(1)}, f32[8,256]{1,0:T(8,128)S(1)}, u32[]{:S(2)}, u32[]{:S(2)}) collective-permute-start(f32[8,256]{1,0:T(8,128)S(1)} %get-tuple-element.19), channel_id=1, source_target_pairs={{0,1},{1,0},{2,3},{3,2},{4,5},{5,4},{6,7},{7,6},{8,9},{9,8},{10,11... | collective-permute-start | bytes 24584 | tf_op jit(solution)/shard_map/ppermute | solution.py:380
